TPU v7x, 256 devices: a whole 4x4x8 slice. The times are simulated.
256 devices in a mesh: dom: 32 (over x, y, core), head: 8 (over z).
Axes of the slice: x: 4, y: 4, z: 8, core: 2. Of those that a mesh axis runs over, the one named last changes fastest.
Arguments:
- feats: bfloat16 [32768, 256], P('dom'), may hold values from -15 to 15
- w_qkv: bfloat16 [3, 256, 256], P(None, None, 'head'), may hold values from -0.375 to 0.375
- w_out: bfloat16 [256, 256], P('head'), may hold values from -0.375 to 0.375
- virt_embed: bfloat16 [64, 256], replicated, may hold values from -6 to 6
- member: int32 [32768], P('dom'), may hold values from 0 to 63
- expander: int32 [32768, 2], P('dom'), may hold values from 0 to 32767, as said below
- local_mask: int32 [32768, 1024], P('dom'), may hold values from 0 to 1, as said below
- cotangent: bfloat16 [32768, 256], P('dom'), may hold values from -6 to 6
Outputs:
- mixed: bfloat16 [32768, 256], P('dom', 'head')
- grad_feats: bfloat16 [32768, 256], P('dom', 'head')
- grad_qkv: float32 [3, 256, 256], P(None, None, 'head')
- grad_out: float32 [256, 256], P('head')
- grad_virtual: float32 [64, 256], P(None, 'head')
Inputs may be any that keep to these rules, and one draw needn't show every extreme that they name: Each column of expander is a permutation of the nodes; for the node at row r of its slab, expander[., e] lies in slab (r + e) mod 32. `local_mask`: every node's entry at its own column is 1.
All inputs are finite; a program needn't handle non-finite values.
Results may differ from a plain program's by a relative error of at most 0.009.
The roundings to bfloat16 on the way count: a program that leaves them out, or rounds other values in their place, can miss the bound.
Values may be sent and summed in bfloat16 or wider, within the bound.
No kernel may reach another device: no remote copies, remote signals or barrier semaphores. Data moves between devices by JAX's collectives and lax.ppermute only.
A program may use at most 64 MiB of HBM per device.

v0:
```python
import jax
import jax.numpy as jnp
from jax import lax
from jax.sharding import PartitionSpec as P

HD = 32
VIRT = 64
EXP = 2


masked_score = -1e30


def product(form, left, right):
    return jnp.einsum(form, left, right, preferred_element_type=jnp.float32)


def split_heads(table, heads):
    return table.reshape(table.shape[:-1] + (heads, table.shape[-1] // heads))


def outgoing(table, block, slabs):
    shaped = table.reshape((block, slabs) + table.shape[1:])
    parts = [jnp.roll(shaped[:, :, branch], branch, axis=1) for branch in range(EXP)]
    return jnp.moveaxis(jnp.stack(parts, axis=0), 2, 0)


def incoming(arrived, block, slabs):
    parts = []
    for branch in range(EXP):
        piece = jnp.moveaxis(arrived[:, branch], 0, 1)
        parts.append(jnp.roll(piece, -branch, axis=1).reshape((block * slabs,) + piece.shape[2:]))
    return jnp.stack(parts, axis=1)


def attend_forward(
    query, keys, values, mask, side_keys, side_values, virt_keys, virt_values, scale
):
    local_s = product("rhe,jhe->hrj", query, keys) * scale
    local_s = jnp.where(mask[None] > 0, local_s, masked_score)
    side_s = product("rhe,rkhe->hrk", query, side_keys) * scale
    virt_s = product("rhe,vhe->hrv", query, virt_keys) * scale
    highest = jnp.maximum(
        jnp.maximum(jnp.max(local_s, axis=2), jnp.max(side_s, axis=2)), jnp.max(virt_s, axis=2)
    )[:, :, None]
    local_w = jnp.where(mask[None] > 0, jnp.exp(local_s - highest), 0.0)
    side_w = jnp.exp(side_s - highest)
    virt_w = jnp.exp(virt_s - highest)
    total = (
        jnp.sum(local_w, axis=2, keepdims=True)
        + jnp.sum(side_w, axis=2, keepdims=True)
        + jnp.sum(virt_w, axis=2, keepdims=True)
    )
    local_p = local_w / total
    side_p = side_w / total
    virt_p = virt_w / total
    output = product("hrj,jhe->rhe", local_p.astype(jnp.bfloat16), values)
    output = output + product("hrk,rkhe->rhe", side_p.astype(jnp.bfloat16), side_values)
    output = output + product("hrv,vhe->rhe", virt_p.astype(jnp.bfloat16), virt_values)
    return (output.astype(jnp.bfloat16), (local_p, side_p, virt_p))


def attend_backward(
    query, keys, values, side_keys, side_values, virt_keys, virt_values, weights, grad_output, scale
):
    local_p, side_p, virt_p = weights
    local_b = local_p.astype(jnp.bfloat16)
    side_b = side_p.astype(jnp.bfloat16)
    virt_b = virt_p.astype(jnp.bfloat16)
    local_d = product("rhe,jhe->hrj", grad_output, values)
    side_d = product("rhe,rkhe->hrk", grad_output, side_values)
    virt_d = product("rhe,vhe->hrv", grad_output, virt_values)
    centre = (
        jnp.sum(local_p * local_d, axis=2, keepdims=True)
        + jnp.sum(side_p * side_d, axis=2, keepdims=True)
        + jnp.sum(virt_p * virt_d, axis=2, keepdims=True)
    )
    local_g = (local_p * (local_d - centre)).astype(jnp.bfloat16)
    side_g = (side_p * (side_d - centre)).astype(jnp.bfloat16)
    virt_g = (virt_p * (virt_d - centre)).astype(jnp.bfloat16)
    grad_query = product("hrj,jhe->rhe", local_g, keys)
    grad_query = grad_query + product("hrk,rkhe->rhe", side_g, side_keys)
    grad_query = grad_query + product("hrv,vhe->rhe", virt_g, virt_keys)
    grad_query = (scale * grad_query).astype(jnp.bfloat16)
    grad_keys = scale * product("hrj,rhe->jhe", local_g, query)
    grad_values = product("hrj,rhe->jhe", local_b, grad_output)
    grad_side_keys = (scale * product("hrk,rhe->rkhe", side_g, query)).astype(jnp.bfloat16)
    grad_side_values = product("hrk,rhe->rkhe", side_b, grad_output).astype(jnp.bfloat16)
    grad_virt_keys = scale * product("hrv,rhe->vhe", virt_g, query)
    grad_virt_values = product("hrv,rhe->vhe", virt_b, grad_output)
    return (
        grad_query,
        grad_keys,
        grad_values,
        grad_side_keys,
        grad_side_values,
        grad_virt_keys,
        grad_virt_values,
    )


def shards(feats, w_qkv, w_out, virt_embed, member, expander, local_mask, cotangent):
    rows, width = feats.shape
    width_local = w_qkv.shape[2]
    heads_local = width_local // HD
    slabs = lax.axis_size("dom")
    block = rows // slabs
    nodes = rows * slabs
    scale = HD ** (-0.5)
    pool_scale = (VIRT / nodes) ** 0.5
    grad_scale = nodes ** (-0.5)
    col_start = lax.axis_index("head") * width_local
    feats_own = lax.dynamic_slice_in_dim(feats, col_start, width_local, 1)
    grad_own = lax.dynamic_slice_in_dim(cotangent, col_start, width_local, 1)
    projected = product("nd,jdc->jnc", feats, w_qkv).astype(jnp.bfloat16)
    virt_ids = jnp.arange(VIRT, dtype=jnp.int32)
    member_cols = (member[None, :] == virt_ids[:, None]).astype(jnp.bfloat16)
    pooled = lax.psum(jnp.dot(member_cols, feats, preferred_element_type=jnp.float32), "dom")
    virt_state = (virt_embed.astype(jnp.float32) + pool_scale * pooled).astype(jnp.bfloat16)
    virt_pair = product("vd,jdc->jvc", virt_state, w_qkv[1:]).astype(jnp.bfloat16)
    key_value = jnp.concatenate([projected[1], projected[2]], axis=1)
    target = expander % rows
    send_rows = outgoing(
        jnp.broadcast_to(key_value[:, None], (rows, EXP, 2 * width_local)), block, slabs
    )
    send_place = outgoing(target, block, slabs)
    recv_rows, recv_place = (
        lax.all_to_all(send_rows, "dom", split_axis=0, concat_axis=0, tiled=True),
        lax.all_to_all(send_place, "dom", split_axis=0, concat_axis=0, tiled=True),
    )
    reply = lax.all_to_all(key_value[recv_place], "dom", split_axis=0, concat_axis=0, tiled=True)
    branch_ids = jnp.broadcast_to(jnp.arange(EXP, dtype=jnp.int32)[None, :, None], recv_place.shape)
    inverse_rows = (
        jnp.zeros((EXP, rows, 2 * width_local), jnp.bfloat16)
        .at[branch_ids, recv_place]
        .set(recv_rows)
    )
    forward_rows = incoming(reply, block, slabs)
    side_rows = jnp.concatenate([forward_rows, jnp.transpose(inverse_rows, (1, 0, 2))], axis=1)
    query = split_heads(projected[0], heads_local)
    keys = split_heads(projected[1], heads_local)
    values = split_heads(projected[2], heads_local)
    side_keys = split_heads(side_rows[:, :, :width_local], heads_local)
    side_values = split_heads(side_rows[:, :, width_local:], heads_local)
    virt_keys = split_heads(virt_pair[0], heads_local)
    virt_values = split_heads(virt_pair[1], heads_local)
    attended, weights = attend_forward(
        query, keys, values, local_mask, side_keys, side_values, virt_keys, virt_values, scale
    )
    attended_flat = attended.reshape(rows, width_local)
    mixed_cols = lax.psum_scatter(
        jnp.dot(attended_flat, w_out, preferred_element_type=jnp.float32),
        "head",
        scatter_dimension=1,
        tiled=True,
    )
    mixed = (feats_own.astype(jnp.float32) + mixed_cols).astype(jnp.bfloat16)
    grad_attended = product("nd,cd->nc", cotangent, w_out).astype(jnp.bfloat16)
    grad_out_part = grad_scale * product("nc,nd->cd", attended_flat, cotangent)
    grad_out = lax.psum(grad_out_part, "dom")
    results = attend_backward(
        query,
        keys,
        values,
        side_keys,
        side_values,
        virt_keys,
        virt_values,
        weights,
        split_heads(grad_attended, heads_local),
        scale,
    )
    (
        grad_query,
        grad_keys,
        grad_values,
        grad_side_keys,
        grad_side_values,
        grad_virt_keys,
        grad_virt_values,
    ) = results
    virt_grads = lax.psum(
        jnp.stack(
            [grad_virt_keys.reshape(VIRT, width_local), grad_virt_values.reshape(VIRT, width_local)]
        ),
        "dom",
    )
    virt_grads = virt_grads.astype(jnp.bfloat16)
    side_grads = jnp.concatenate(
        [
            grad_side_keys.reshape(rows, 2 * EXP, width_local),
            grad_side_values.reshape(rows, 2 * EXP, width_local),
        ],
        axis=2,
    )
    send_forward = outgoing(side_grads[:, :EXP], block, slabs)
    send_inverse = side_grads[:, EXP:][recv_place, branch_ids]
    recv_forward, recv_inverse = (
        lax.all_to_all(send_forward, "dom", split_axis=0, concat_axis=0, tiled=True),
        lax.all_to_all(send_inverse, "dom", split_axis=0, concat_axis=0, tiled=True),
    )
    from_forward = (
        jnp.zeros((rows, 2 * width_local), jnp.float32)
        .at[recv_place]
        .add(recv_forward.astype(jnp.float32))
    )
    from_inverse = jnp.sum(incoming(recv_inverse, block, slabs).astype(jnp.float32), axis=1)
    local_kv = jnp.concatenate(
        [grad_keys.reshape(rows, width_local), grad_values.reshape(rows, width_local)], axis=1
    )
    kv_grad = (local_kv + from_forward + from_inverse).astype(jnp.bfloat16)
    stacked_grads = jnp.stack(
        [grad_query.reshape(rows, width_local), kv_grad[:, :width_local], kv_grad[:, width_local:]]
    )
    feats_part = product("jnc,jdc->nd", stacked_grads, w_qkv)
    virt_part = product("jvc,jdc->vd", virt_grads, w_qkv[1:])
    feats_cols, virt_cols = (
        lax.psum_scatter(feats_part, "head", scatter_dimension=1, tiled=True),
        lax.psum_scatter(virt_part, "head", scatter_dimension=1, tiled=True),
    )
    member_rows = (member[:, None] == virt_ids[None, :]).astype(jnp.float32)
    lookup = jnp.dot(member_rows, virt_cols, precision=lax.Precision.HIGHEST)
    grad_feats = (grad_own.astype(jnp.float32) + feats_cols + pool_scale * lookup).astype(
        jnp.bfloat16
    )
    virt_weight_part = product("vd,jvc->jdc", virt_state, virt_grads)
    virt_weight_term = grad_scale * jnp.concatenate(
        [jnp.zeros((1, width, width_local), jnp.float32), virt_weight_part], axis=0
    )
    grad_qkv_part = grad_scale * product("nd,jnc->jdc", feats, stacked_grads)
    grad_qkv = lax.psum(grad_qkv_part, "dom")
    grad_qkv = grad_qkv + virt_weight_term
    return (mixed, grad_feats, grad_qkv, grad_out, virt_cols)


def solution(mesh):
    return jax.shard_map(
        shards,
        mesh=mesh,
        in_specs=(
            P("dom", None),
            P(None, None, "head"),
            P("head", None),
            P(),
            P("dom"),
            P("dom", None),
            P("dom", None),
            P("dom", None),
        ),
        out_specs=(
            P("dom", "head"),
            P("dom", "head"),
            P(None, None, "head"),
            P("head", None),
            P(None, "head"),
        ),
        check_vma=False,
    )
```

profile of v0, /device:TPU:2, one launch (start us, length us, event | category | flops | bytes accessed | tf_op | source)
XLA Modules:
  0.0 476.0 jit_solution(1930410079334598169)
XLA Ops:
  8.9 7.6 %all-to-all-start = ((s32[32,2,32]{2,1,0:T(2,128)}), s32[32,2,32]{2,1,0:T(2,128)S(1)}, u32[]{:S(2)}, u32[]{:S(2)}) async-start(s32[32,2,32]{2,1,0:T(2,128)} %add_bitcast_fusion), calls=%async_computation | async-start | bytes 65536 | tf_op jit(solution)/shard_map/all_to_all | solution.py:129
  22.3 5.4 %copy.43 = s32[1024,1024]{0,1:T(8,128)} copy(s32[1024,1024]{1,0:T(8,128)} %param.14) | data formatting | bytes 8388608 | tf_op args[6]
  27.6 5.7 %fusion = (f32[1024]{0:T(1024)S(1)}, pred[1024,1024]{0,1:T(32,128)(4,1)}, f32[1024,1024]{0,1:T(8,128)}) fusion(s32[1024,1024]{0,1:T(8,128)} %copy.43, bf16[3,1024,32]{1,2,0:T(8,128)(2,1)S(1)} %fusion.3), kind=kOutput, calls=%fused_computation.8 | convolution fusion | flops 71302144 | bytes 9572352 | tf_op jit(solution)/shard_map/rhe,jhe->hrj/dot_general | solution.py:15
  38.7 7.4 %all-to-all-start.2 = ((bf16[32,2,2048]{2,1,0:T(2,128)(2,1)}), bf16[32,2,2048]{2,1,0:T(2,128)(2,1)S(1)}, u32[]{:S(2)}, u32[]{:S(2)}) async-start(bf16[32,2,2048]{2,1,0:T(2,128)(2,1)} %reshape.332), calls=%async_computation.2 | async-start | bytes 524288 | tf_op jit(solution)/shard_map/all_to_all | solution.py:128
  46.7 6.2 %gather_fusion = bf16[2048,64]{1,0:T(8,128)(2,1)S(1)} fusion(bf16[1024,64]{1,0:T(8,128)(2,1)S(1)} %copy.46, s32[2048]{0:T(1024)S(1)} %broadcast_clamp_fusion), kind=kCustom, calls=%fused_computation | custom fusion | bytes 532480 | tf_op jit(solution)/shard_map/gather | solution.py:131
  54.1 75.0 %all-reduce.5.cloned.1.call-done = f32[64,256]{1,0:T(8,128)} async-done(((f32[64,256]{1,0:T(8,128)}), f32[64,256]{1,0:T(8,128)}) %all-reduce.5.cloned.1.call-update) | async-done | bytes 65552 | tf_op jit(solution)/shard_map/psum | solution.py:118
  130.0 6.0 %all-to-all-start.1 = ((bf16[32,2,2048]{2,1,0:T(2,128)(2,1)}), bf16[32,2,2048]{2,1,0:T(2,128)(2,1)S(1)}, u32[]{:S(2)}, u32[]{:S(2)}) async-start(bf16[32,2,2048]{2,1,0:T(2,128)(2,1)} %reshape.334), calls=%async_computation.1 | async-start | bytes 524288 | tf_op jit(solution)/shard_map/all_to_all | solution.py:131
  136.6 6.3 %scatter_custom_fusion.1 = bf16[2048,64]{1,0:T(8,128)(2,1)S(1)} fusion(s32[2048]{0:T(1024)S(1)} %reshape.304, bf16[2048,64]{1,0:T(8,128)(2,1)S(1)} %bitcast.264, bf16[]{:T(256)} %constant.22.clone.1), kind=kCustom, calls=%fused_computation.93 | custom fusion | bytes 262146
  149.4 4.8 %multiply_reduce_fusion = (f32[1024]{0:T(1024)S(1)}, f32[1024,1024]{0,1:T(8,128)}, f32[1024,1024]{0,1:T(8,128)}) fusion(f32[1024]{0:T(1024)S(1)} %add_add_fusion.1, pred[1024,1024]{0,1:T(32,128)(4,1)S(1)} %copy-done.8, f32[1024]{0:T(1024)S(1)} %maximum_maximum_fusion, f32[1024,1024]{0,1:T(8,128)S(1)} %copy-done.2, ...), kind=kOutput, calls=%fused_computation.5 | convolution fusion | flops 74447872 | bytes 13774848 | tf_op jit(solution)/shard_map/rhe,jhe->hrj/dot_general | solution.py:15
  156.8 2.0 fusion.26
  160.2 3.7 convolution_bitcast_fusion.1
  166.5 3.9 fusion.19
  170.4 3.9 fusion.18
  174.3 2.6 pad_maximum_fusion.1
  176.9 9.4 %gather_fusion.1 = bf16[2048,64]{1,0:T(8,128)(2,1)S(1)} fusion(bf16[1024,2,64]{2,1,0:T(2,128)(2,1)S(1)} %get-tuple-element.14, s32[2048]{0:T(1024)S(1)} %reshape.290), kind=kCustom, calls=%fused_computation.1 | custom fusion | bytes 540672 | tf_op jit(solution)/shard_map/gather | solution.py:197
  187.5 7.1 %all-to-all-start.3 = ((bf16[32,2,2048]{2,1,0:T(2,128)(2,1)}), bf16[32,2,2048]{2,1,0:T(2,128)(2,1)}, u32[]{:S(2)}, u32[]{:S(2)}) async-start(bf16[32,2,2048]{2,1,0:T(2,128)(2,1)} %reshape.336), calls=%async_computation.4 | async-start | bytes 524288 | tf_op jit(solution)/shard_map/all_to_all | solution.py:200
  194.6 4.6 multiply_convert_fusion
  202.5 2.0 fusion.28
  204.5 1.8 copy.73
  206.3 2.0 fusion.5
  210.6 1.7 fusion.16
  212.3 7.4 %all-to-all-start.4 = ((bf16[32,2,2048]{2,1,0:T(2,128)(2,1)}), bf16[32,2,2048]{2,1,0:T(2,128)(2,1)S(1)}, u32[]{:S(2)}, u32[]{:S(2)}) async-start(bf16[32,2,2048]{2,1,0:T(2,128)(2,1)} %reshape.338), calls=%async_computation.5 | async-start | bytes 524288 | tf_op jit(solution)/shard_map/all_to_all | solution.py:199
  222.1 5.3 %all-to-all-done.4 = bf16[32,2,2048]{2,1,0:T(2,128)(2,1)S(1)} async-done(((bf16[32,2,2048]{2,1,0:T(2,128)(2,1)}), bf16[32,2,2048]{2,1,0:T(2,128)(2,1)S(1)}, u32[]{:S(2)}, u32[]{:S(2)}) %all-to-all-start.4) | async-done | bytes 262176 | tf_op jit(solution)/shard_map/all_to_all | solution.py:199
  227.8 11.9 %scatter_custom_fusion = f32[1024,64]{1,0:T(8,128)S(1)} fusion(f32[1024,64]{1,0:T(8,128)S(1)} %copy.62, s32[2048]{0:T(1024)} %copy-done.26, bf16[2048,64]{1,0:T(8,128)(2,1)S(1)} %bitcast.252), kind=kCustom, calls=%fused_computation.51 | custom fusion | flops 262144 | bytes 786432 | tf_op jit(solution)/shard_map/scatter-add | solution.py:205
  239.8 1.7 fusion.13
  241.6 2.2 fusion.86
  244.4 108.8 %all-reduce.1 = (bf16[2,64,32]{1,2,0:T(8,128)(2,1)S(1)}, f32[32,256]{1,0:T(8,128)}) all-reduce(f32[2,64,32]{1,2,0:T(8,128)S(1)} %pad_maximum_fusion.10, f32[32,256]{1,0:T(8,128)S(1)} %convolution_multiply_fusion.4), channel_id=1, replica_groups=mesh['dom'=32,'head'=8] {'dom'}, use_global_device_ids=true, to_apply=%region_15.16 | all-reduce | flops 12288 | bytes 90112 | tf_op jit(solution)/shard_map/psum | solution.py:182
  356.2 1.6 multiply_add_fusion
  357.8 31.3 %reduce-scatter.4.cloned.1.call-done = f32[1024,32]{0,1:T(8,128)} async-done(((f32[1024,256]{0,1:T(8,128)}), f32[1024,32]{0,1:T(8,128)}) %reduce-scatter.4.cloned.1.call-update) | async-done | bytes 131088 | tf_op jit(solution)/shard_map/reduce_scatter | solution.py:151
  390.6 36.6 %reduce-scatter.8.cloned.1.call-done = f32[64,32]{0,1:T(8,128)} async-done(((f32[64,256]{0,1:T(8,128)}), f32[64,32]{0,1:T(8,128)}) %reduce-scatter.8.cloned.1.call-update) | async-done | bytes 8208 | tf_op jit(solution)/shard_map/reduce_scatter | solution.py:219
  427.2 40.0 %reduce-scatter.6.cloned.1.call-done = f32[1024,32]{0,1:T(8,128)} async-done(((f32[1024,256]{0,1:T(8,128)}), f32[1024,32]{0,1:T(8,128)}) %reduce-scatter.6.cloned.1.call-update) | async-done | bytes 131088 | tf_op jit(solution)/shard_map/reduce_scatter | solution.py:218
  467.1 2.1 fusion.11
  (182 shorter events, 43.3 us)
Async XLA Ops:
  7.2 9.4 %copy-start = (bf16[1024,256]{1,0:T(8,128)(2,1)S(1)}, bf16[1024,256]{1,0:T(8,128)(2,1)}, u32[]{:S(2)}) copy-start(bf16[1024,256]{1,0:T(8,128)(2,1)} %param.8) | copy-start | bytes 1572868
  8.9 29.8 %all-to-all-start = ((s32[32,2,32]{2,1,0:T(2,128)}), s32[32,2,32]{2,1,0:T(2,128)S(1)}, u32[]{:S(2)}, u32[]{:S(2)}) async-start(s32[32,2,32]{2,1,0:T(2,128)} %add_bitcast_fusion), calls=%async_computation | async-start | bytes 65536 | tf_op jit(solution)/shard_map/all_to_all | solution.py:129
  16.5 112.5 %all-reduce.5.cloned.1.call-start = ((), (), s32[]{:S(2)}) async-start(), calls=%async_computation.8 | async-start | bytes 131072 | tf_op jit(solution)/shard_map/psum | solution.py:118
  27.6 5.9 %copy-start.3 = (bf16[1024,256]{1,0:T(8,128)(2,1)S(1)}, bf16[1024,256]{1,0:T(8,128)(2,1)}, u32[]{:S(2)}) copy-start(bf16[1024,256]{1,0:T(8,128)(2,1)} %param.15) | copy-start | bytes 1572868
  27.6 5.9 %copy-start.23 = (bf16[32,256]{1,0:T(8,128)(2,1)S(1)}, bf16[32,256]{1,0:T(8,128)(2,1)}, u32[]{:S(2)}) copy-start(bf16[32,256]{1,0:T(8,128)(2,1)} %param.10) | copy-start | bytes 49156
  33.4 12.7 %copy-start.28 = (s32[2]{0:T(128)S(1)}, s32[2]{0:T(128)}, u32[]{:S(2)}) copy-start(s32[2]{0:T(128)} %constant.28) | copy-start | bytes 28
  33.4 12.9 %copy-start.29 = (s32[2]{0:T(128)S(1)}, s32[2]{0:T(128)}, u32[]{:S(2)}) copy-start(s32[2]{0:T(128)} %constant.12) | copy-start | bytes 28
  36.4 92.6 %slice-start = ((bf16[3,256,32]{1,2,0:T(8,128)(2,1)}), bf16[2,256,32]{1,2,0:T(8,128)(2,1)S(1)}, s32[]{:S(2)}) async-start(bf16[3,256,32]{1,2,0:T(8,128)(2,1)} %param.9), calls=%async_computation.13 | async-start | bytes 65536 | tf_op jit(solution)/shard_map/slice | solution.py:120
  36.4 92.6 %copy-start.21 = (bf16[64,256]{1,0:T(8,128)(2,1)S(1)}, bf16[64,256]{1,0:T(8,128)(2,1)}, u32[]{:S(2)}) copy-start(bf16[64,256]{1,0:T(8,128)(2,1)} %param.11) | copy-start | bytes 98308
  38.7 91.3 %all-to-all-start.2 = ((bf16[32,2,2048]{2,1,0:T(2,128)(2,1)}), bf16[32,2,2048]{2,1,0:T(2,128)(2,1)S(1)}, u32[]{:S(2)}, u32[]{:S(2)}) async-start(bf16[32,2,2048]{2,1,0:T(2,128)(2,1)} %reshape.332), calls=%async_computation.2 | async-start | bytes 524288 | tf_op jit(solution)/shard_map/all_to_all | solution.py:128
  46.5 83.5 %copy-start.26 = (s32[2048]{0:T(1024)}, s32[2048]{0:T(1024)S(1)}, u32[]{:S(2)}) copy-start(s32[2048]{0:T(1024)S(1)} %reshape.284) | copy-start | bytes 24580
  130.0 13.7 %all-to-all-start.1 = ((bf16[32,2,2048]{2,1,0:T(2,128)(2,1)}), bf16[32,2,2048]{2,1,0:T(2,128)(2,1)S(1)}, u32[]{:S(2)}, u32[]{:S(2)}) async-start(bf16[32,2,2048]{2,1,0:T(2,128)(2,1)} %reshape.334), calls=%async_computation.1 | async-start | bytes 524288 | tf_op jit(solution)/shard_map/all_to_all | solution.py:131
  136.0 18.1 %copy-start.24 = (bf16[2,64,32]{1,2,0:T(8,128)(2,1)}, bf16[2,64,32]{1,2,0:T(8,128)(2,1)S(1)}, u32[]{:S(2)}) copy-start(bf16[2,64,32]{1,2,0:T(8,128)(2,1)S(1)} %convert_bitcast_fusion.1) | copy-start | bytes 24580
  136.3 30.2 %copy-start.5 = (f32[1024,64]{0,1:T(8,128)}, f32[1024,64]{0,1:T(8,128)S(1)}, u32[]{:S(2)}) copy-start(f32[1024,64]{0,1:T(8,128)S(1)} %get-tuple-element.39) | copy-start | bytes 786436
  149.3 5.7 %copy-start.12 = (bf16[1024,32,1]{1,2,0:T(2,128)(2,1)S(1)}, bf16[1024,32,1]{1,2,0:T(2,128)(2,1)}, u32[]{:S(2)}) copy-start(bf16[1024,32,1]{1,2,0:T(2,128)(2,1)} %copy.70) | copy-start | bytes 196612
  160.2 4.2 copy-start.25
  187.5 24.8 %all-to-all-start.3 = ((bf16[32,2,2048]{2,1,0:T(2,128)(2,1)}), bf16[32,2,2048]{2,1,0:T(2,128)(2,1)}, u32[]{:S(2)}, u32[]{:S(2)}) async-start(bf16[32,2,2048]{2,1,0:T(2,128)(2,1)} %reshape.336), calls=%async_computation.4 | async-start | bytes 524288 | tf_op jit(solution)/shard_map/all_to_all | solution.py:200
  209.3 12.6 %copy-start.14 = (f32[1024,32]{0,1:T(8,128)S(1)}, f32[1024,32]{0,1:T(8,128)}, u32[]{:S(2)}) copy-start(f32[1024,32]{0,1:T(8,128)} %convolution_bitcast_fusion.1) | copy-start | bytes 393220
  209.3 12.6 %copy-start.15 = (f32[1024,32]{0,1:T(8,128)S(1)}, f32[1024,32]{0,1:T(8,128)}, u32[]{:S(2)}) copy-start(f32[1024,32]{0,1:T(8,128)} %fusion.10) | copy-start | bytes 393220
  212.3 15.1 %all-to-all-start.4 = ((bf16[32,2,2048]{2,1,0:T(2,128)(2,1)}), bf16[32,2,2048]{2,1,0:T(2,128)(2,1)S(1)}, u32[]{:S(2)}, u32[]{:S(2)}) async-start(bf16[32,2,2048]{2,1,0:T(2,128)(2,1)} %reshape.338), calls=%async_computation.5 | async-start | bytes 524288 | tf_op jit(solution)/shard_map/all_to_all | solution.py:199
  219.7 136.5 %all-reduce.7.cloned.1.call-start = ((), (), s32[]{:S(2)}) async-start(), calls=%async_computation.12 | async-start | bytes 196608 | tf_op jit(solution)/shard_map/psum | solution.py:231
  221.6 22.4 %copy-start.6 = (f32[1024,64]{0,1:T(8,128)S(1)}, f32[1024,64]{0,1:T(8,128)}, u32[]{:S(2)}) copy-start(f32[1024,64]{0,1:T(8,128)} %copy-done.5) | copy-start | bytes 786436
  221.9 22.3 %copy-start.4 = (bf16[1024,256]{1,0:T(8,128)(2,1)S(1)}, bf16[1024,256]{1,0:T(8,128)(2,1)}, u32[]{:S(2)}) copy-start(bf16[1024,256]{1,0:T(8,128)(2,1)} %param.15) | copy-start | bytes 1572868
  221.9 22.3 %copy-start.17 = (bf16[1024,32]{0,1:T(8,128)(2,1)S(1)}, bf16[1024,32]{0,1:T(8,128)(2,1)}, u32[]{:S(2)}) copy-start(bf16[1024,32]{0,1:T(8,128)(2,1)} %fusion.15) | copy-start | bytes 196612
  222.1 131.1 %copy-start.11 = (bf16[3,256,32]{1,2,0:T(8,128)(2,1)S(1)}, bf16[3,256,32]{1,2,0:T(8,128)(2,1)}, u32[]{:S(2)}) copy-start(bf16[3,256,32]{1,2,0:T(8,128)(2,1)} %param.9) | copy-start | bytes 147460
  222.1 132.0 %copy-start.18 = (bf16[1,1024,32]{1,2,0:T(8,128)(2,1)S(1)}, bf16[1,1024,32]{1,2,0:T(8,128)(2,1)}, u32[]{:S(2)}) copy-start(bf16[1,1024,32]{1,2,0:T(8,128)(2,1)} %fusion.16) | copy-start | bytes 196612
  241.5 114.5 %copy-start.19 = (f32[64,256]{1,0:T(8,128)S(1)}, f32[64,256]{1,0:T(8,128)}, u32[]{:S(2)}) copy-start(f32[64,256]{1,0:T(8,128)} %all-reduce.5.cloned.1.call-done) | copy-start | bytes 196612
  241.6 114.5 %copy-start.22 = (bf16[64,256]{1,0:T(8,128)(2,1)S(1)}, bf16[64,256]{1,0:T(8,128)(2,1)}, u32[]{:S(2)}) copy-start(bf16[64,256]{1,0:T(8,128)(2,1)} %param.11) | copy-start | bytes 98308
  241.6 147.5 %reduce-scatter.4.cloned.1.call-start = ((), (), s32[]{:S(2)}) async-start(), calls=%async_computation.9 | async-start | bytes 1179648 | tf_op jit(solution)/shard_map/reduce_scatter | solution.py:151
  243.8 223.4 %copy-start.27 = (s32[1024]{0:T(1024)S(1)}, s32[1024]{0:T(1024)}, u32[]{:S(2)}) copy-start(s32[1024]{0:T(1024)} %param.12) | copy-start | bytes 12292
  243.8 183.4 %reduce-scatter.8.cloned.1.call-start = ((), (), s32[]{:S(2)}) async-start(), calls=%async_computation.11 | async-start | bytes 147456 | tf_op jit(solution)/shard_map/reduce_scatter | solution.py:219
  354.1 113.0 %reduce-scatter.6.cloned.1.call-start = ((), (), s32[]{:S(2)}) async-start(), calls=%async_computation.10 | async-start | bytes 1179648 | tf_op jit(solution)/shard_map/reduce_scatter | solution.py:218
  (9 other events, 25.3 us)
Sparse Core Ops, SparseCore 0:
  21.2 107.8 all-reduce.4
  241.7 106.6 all-reduce.6
  350.9 38.0 reduce-scatter.3
  392.0 35.1 reduce-scatter.7
  429.7 37.3 reduce-scatter.5
where the time goes:
time: 485 us; the launch traced here: 476 us
  waiting for transfers between devices  189 us (39%)
  blocking collectives  109 us (22%)
  local copies, waits for them, and re-layouts  49.4 us (10%)
  matrix products  40.9 us (8%)
  other arithmetic  37.3 us (8%)
  starting transfers between devices  35.7 us (7%)
  between operations  15 us (3%)
    psum x1, blocking collectives, shards(): lax.psum(jnp.stack([grad_virt_keys.reshape(VIRT, width_local), grad_virt_...  109 us
    psum x1, waiting for transfers between devices, shards(): lax.psum(jnp.dot(member_cols, feats, preferred_element_type=jnp.float32),...  75 us
    reduce_scatter x1, waiting for transfers between devices, shards(): lax.psum_scatter(feats_part, 'head', scatter_dimension=1, tiled=True)  40 us
    reduce_scatter x1, waiting for transfers between devices, shards(): lax.psum_scatter(virt_part, 'head', scatter_dimension=1, tiled=True)  36.6 us
    dot_general x23, matrix products, product(): return jnp.einsum(form, left, right, preferred_element_type=jnp.float32)  34.2 us
    reduce_scatter x1, waiting for transfers between devices, shards(): lax.psum_scatter(jnp.dot(attended_flat, w_out, preferred_element_type=jnp...  31.3 us
    unnamed x77, local copies, waits for them, and re-layouts  20.3 us
    scatter-add x1, other arithmetic, shards(): from_forward = jnp.zeros((rows, 2 * width_local), jnp.float32).at[recv_pl...  11.9 us
  transfers between devices with their start and end apart: 10, of which 6 were waited for; matrix products, arithmetic and copies ran while one was open for 14% of the time, Pallas kernels for 0%

commit v1 on v0

v1 whole, which is shorter than its diff:
```python
import functools

import jax
import jax.numpy as jnp
from jax import lax
from jax.experimental import pallas as pl
from jax.experimental.pallas import tpu as pltpu
from jax.sharding import PartitionSpec as P

HD = 32
VIRT = 64
SLABS = 32
HEADS = 8
ROWS = 1024
WIDTH = 256
NODES = SLABS * ROWS
BLOCK = ROWS // SLABS
SCALE = HD ** (-0.5)
POOL_SCALE = (VIRT / NODES) ** 0.5
GRAD_SCALE = NODES ** (-0.5)
TI = 256
TA = 512
MASKED = -1e30
LOG2E = 1.4426950408889634
SCALE2 = SCALE * LOG2E

f32 = jnp.float32
bf16 = jnp.bfloat16
i32 = jnp.int32


def dot(a, b):
    return jnp.dot(a, b, preferred_element_type=f32)


def dot_nt(a, b):
    return lax.dot_general(a, b, (((1,), (1,)), ((), ())), preferred_element_type=f32)


def iota(shape, dim):
    return lax.broadcasted_iota(i32, shape, dim)


def hot(cond):
    return jnp.where(cond, 1.0, 0.0).astype(bf16)


def split3(x):
    hi = x.astype(bf16)
    rest = x - hi.astype(f32)
    mid = rest.astype(bf16)
    low = (rest - mid.astype(f32)).astype(bf16)
    return hi, mid, low


def dot3(x, one_hot):
    hi, mid, low = split3(x)
    return dot(hi, one_hot) + dot(mid, one_hot) + dot(low, one_hot)


def lane(shape):
    return iota(shape, len(shape) - 1)


def first_virt(slab):
    return 16 * (slab & 3) + 2 * (slab >> 2)


def branch0(shape):
    return (lane(shape) & 32) == 0


def place_rows(table):
    whole = table.astype(i32)
    hi = (whole >> 5).astype(f32).astype(bf16)
    low = (whole & 31).astype(f32).astype(bf16)
    shape = (SLABS, ROWS)
    own = (iota(shape, 1) >> 5) == iota(shape, 0)
    rows = []
    for e in range(2):
        pick = hot(iota((128, ROWS), 0) == 32 * e + (iota((128, ROWS), 1) & 31))
        full = 32.0 * dot(hi, pick) + dot(low, pick)
        rows.append(jnp.sum(jnp.where(own, full, 0.0), axis=0, keepdims=True))
    return rows


def pool_kernel(feats_at, member_at, expander_at, out, feats, member, expander, sems):
    copies = [
        pltpu.make_async_copy(source, target, sems.at[k])
        for k, (source, target) in enumerate(
            ((feats_at, feats), (member_at, member), (expander_at, expander))
        )
    ]
    for copy in copies:
        copy.start()
    copies[2].wait()
    out[...] = jnp.zeros(out.shape, f32)
    shape = (SLABS, ROWS)
    total = jnp.zeros((SLABS, 128), f32)
    for e in range(2):
        target = expander[e : e + 1, :]
        own = (iota(shape, 1) & 31) == ((iota(shape, 0) - e) & 31)
        hi = jnp.where(own, ((target >> 5) & 31).astype(f32), 0.0).astype(bf16)
        low = jnp.where(own, (target & 31).astype(f32), 0.0).astype(bf16)
        slot = hot((iota((ROWS, 128), 0) >> 5) + 32 * e == iota((ROWS, 128), 1))
        total = total + 32.0 * dot(hi, slot) + dot(low, slot)
    out[:, 4, :] = total
    copies[1].wait()
    shape = (VIRT, ROWS)
    order = iota(shape, 0)
    own = hot(member[...] == first_virt(order & 31) + (order >> 5))
    copies[0].wait()
    pooled = dot(own, feats[...])
    out[:, 0, :] = pooled[:32, :128]
    out[:, 1, :] = pooled[:32, 128:]
    out[:, 2, :] = pooled[32:, :128]
    out[:, 3, :] = pooled[32:, 128:]


def project_kernel(
    feats, cotangent, w_qkv, w_out, embed_in,
    table, kv_weights, share, embed, query_t, grad_t, table_t,
):
    embed[...] = embed_in[...]
    w_q, w_k, w_v = w_qkv[0], w_qkv[1], w_qkv[2]
    w_kv4 = jnp.concatenate([w_k, w_k, w_v, w_v], axis=0)
    kv_weights[...] = w_kv4
    share[...] = jnp.concatenate([w_q, w_k, w_v, w_out[...]], axis=0)
    table[...] = dot_nt(feats[...], w_kv4).astype(bf16)
    query_t[...] = dot_nt(w_q, feats[...]).astype(bf16)
    grad_t[...] = dot_nt(w_out[...], cotangent[...]).astype(bf16)
    table_t[...] = dot_nt(jnp.concatenate([w_k, w_v], axis=0), feats[...]).astype(bf16)


def turn_parts(x):
    turned = x.astype(f32).T
    return (
        jnp.concatenate([turned[0:32], turned[64:96]], axis=0),
        jnp.concatenate([turned[32:64], turned[96:128]], axis=0),
    )


def join_parts(parts):
    first, second = parts
    return jnp.concatenate([first[0:32], second[0:32], first[32:64], second[32:64]], axis=0)


def split_places(places):
    at = iota((256, 128), 0)
    found = []
    for place in places:
        whole = place.astype(i32)
        low = whole & 255
        cols = [hot(at == low[:, 128 * c : 128 * c + 128]) for c in range(8)]
        found.append((whole >> 8, jnp.concatenate(cols, axis=1)))
    return found


def gather_rows(found, pair):
    parts = []
    for (high, low_hot), part in zip(found, pair):
        part = part.astype(bf16)
        left = jnp.concatenate([part[:, 256 * k : 256 * k + 256] for k in range(4)], axis=0)
        got = dot(left, low_hot)
        chosen = got[192:256]
        for k in range(3):
            chosen = jnp.where(high == k, got[64 * k : 64 * k + 64], chosen)
        parts.append(chosen)
    return join_parts(parts)


def scatter_rows(found, pair):
    parts = []
    for (high, low_hot), part in zip(found, pair):
        left = jnp.concatenate([jnp.where(high == k, part, 0.0) for k in range(4)], axis=0)
        got = dot_nt(left.astype(bf16), low_hot)
        parts.append(jnp.concatenate([got[64 * k : 64 * k + 64] for k in range(4)], axis=1))
    return join_parts(parts)


def to_slabs(turned):
    return turned.T.astype(bf16).reshape(SLABS, BLOCK, 128)


def rows_kernel(slab, arrived, table, table_t, virt_embed, kv_weights, out, places, state, wide):
    row0, row1 = place_rows(arrived[:, 4, :])
    at = iota((8, ROWS), 0)
    places[...] = jnp.where(at == 0, row0, jnp.where(at == 1, row1, 0.0))
    shape = (8, VIRT)
    pick = hot((iota(shape, 1) == first_virt(slab[0]) + iota(shape, 0)) & (iota(shape, 0) < 2))
    embed = dot(pick, virt_embed[...])
    pooled = jnp.sum(arrived[...], axis=0)
    first = jnp.concatenate([pooled[0:1], pooled[1:2]], axis=1)
    second = jnp.concatenate([pooled[2:3], pooled[3:4]], axis=1)
    at = iota((8, WIDTH), 0)
    pooled = jnp.where(at == 0, first, jnp.where(at == 1, second, 0.0))
    virt_state = embed + POOL_SCALE * pooled
    at = iota((128, WIDTH), 0) - 2 * (slab[0] >> 2)
    whole = jnp.where(at == 0, virt_state[0:1], jnp.where(at == 1, virt_state[1:2], 0.0))
    state[...] = whole.astype(bf16)
    virt_state = jnp.concatenate([virt_state, jnp.zeros((8, WIDTH), f32)], axis=0).astype(bf16)
    virt_rows = dot_nt(virt_state, kv_weights[...]).astype(bf16)
    out[:, 64:80, :] = jnp.broadcast_to(virt_rows[None], (SLABS, 16, 128))
    wide[...] = table[...].astype(f32)
    leave_rows(wide, out)
    out[:, 32:64, :] = to_slabs(gather_rows(split_places((row0, row1)), (table_t[...],) * 2))


def spread_rows(arrived, at, held):
    blocks = [arrived[s, at : at + 32, :].astype(f32) for s in range(SLABS)]
    low_branch = branch0((BLOCK, 128))
    for s in range(SLABS):
        block = jnp.where(low_branch, blocks[s], blocks[(s + 1) % SLABS])
        held[pl.ds(s, BLOCK, stride=SLABS), :] = block
    return held[...]


def leave_rows(held, out):
    low_branch = branch0((BLOCK, 128))
    blocks = [held[pl.ds(s, BLOCK, stride=SLABS), :] for s in range(SLABS)]
    for s in range(SLABS):
        block = jnp.where(low_branch, blocks[s], blocks[(s - 1) % SLABS])
        out[s, 0:32, :] = block.astype(bf16)


def right_tables(table_t):
    key, value = table_t[0:32, :], table_t[32:64, :]
    at = iota((16, ROWS), 0)
    none = jnp.zeros((16, ROWS), bf16)
    less_base = jnp.where(at < 3, -1.0, 0.0).astype(bf16)
    less_centre = jnp.where((at >= 3) & (at < 6), -1.0, 0.0).astype(bf16)
    keys = jnp.concatenate([key, key, key, less_base, none], axis=0)
    values = jnp.concatenate([none, none, none, none, value, less_centre, none], axis=0)
    return keys, values


def left_query(query, parts):
    wide = [part.astype(f32) for part in split3(query.astype(f32) * SCALE2)]
    rest = jnp.zeros((24, query.shape[1]), f32)
    return jnp.concatenate(wide + [parts, rest], axis=0).T.astype(bf16)


def left_grad(grad, parts):
    rest = jnp.zeros((24, grad.shape[1]), f32)
    front = jnp.zeros((64, grad.shape[1]), f32)
    return jnp.concatenate([front, grad.astype(f32), parts, rest], axis=0).T.astype(bf16)


def stack_rows(rows, fill):
    at = iota((8, ROWS), 0)
    block = jnp.full((8, ROWS), fill, f32)
    for k, row in enumerate(rows):
        block = jnp.where(at == k, row, block)
    return block


def local_kernel(query_t, grad_t, mask, table_t, stats):
    none = jnp.zeros((8, TI), f32)
    q_own = left_query(query_t[...], none)
    g_own = left_grad(grad_t[...], none)
    keys, values = right_tables(table_t)
    scores = jnp.where(mask[...] > 0, dot(q_own, keys), MASKED)
    highest = jnp.max(scores, axis=1, keepdims=True)
    weight = jnp.exp2(scores - highest)
    value_dots = dot(g_own, values)
    total = jnp.sum(weight, axis=1, keepdims=True)
    centre = jnp.sum(weight * value_dots, axis=1, keepdims=True)
    at = lane((TI, 128))
    stat = jnp.where(at == 0, highest, jnp.where(at == 1, total, centre))
    stats[...] = stat.T[0:8]


def side_kernel(
    query_t, grad_t, stats, arrived, places,
    out, parts_out, attended_out, grad_query_out,
    near,
):
    virt_rows = arrived[:, 64:80, :].astype(f32)
    pieces = [virt_rows[4 * ((v & 15) >> 1) + (v >> 4), 0:2, :] for v in range(0, VIRT, 2)]
    virt_rows = jnp.concatenate(pieces, axis=0)
    at = lane((VIRT, 128))
    virt_left = jnp.where(at < 64, virt_rows, 0.0), jnp.where(at >= 64, virt_rows, 0.0)
    virt_left = jnp.concatenate(virt_left, axis=0).astype(bf16)
    virt_t = jnp.concatenate([virt_rows, jnp.zeros((64, 128), f32)], axis=0).T.astype(bf16)
    found = split_places((places[0:1, :], places[1:2, :]))
    forward = spread_rows(arrived, 32, near).T
    inverse = scatter_rows(found, turn_parts(arrived[:, 0:32, :].reshape(ROWS, 128)))
    side_k = (forward[0:32], forward[32:64], inverse[0:32], inverse[32:64])
    side_v = (forward[64:96], forward[96:128], inverse[64:96], inverse[96:128])
    q_t, g_t = query_t[...], grad_t[...]
    q_wide, g_wide = q_t.astype(f32), g_t.astype(f32)
    none = jnp.zeros((32, ROWS), bf16)
    virt = dot(virt_left, jnp.concatenate([q_t, none, g_t, none], axis=0))
    virt_s, virt_d = SCALE2 * virt[0:VIRT], virt[VIRT:]
    side_s = [SCALE2 * jnp.sum(q_wide * part, axis=0, keepdims=True) for part in side_k]
    side_d = [jnp.sum(g_wide * part, axis=0, keepdims=True) for part in side_v]
    side_s, side_d = stack_rows(side_s, MASKED), stack_rows(side_d, 0.0)
    local_m, local_t, local_c = stats[0:1, :], stats[1:2, :], stats[2:3, :]
    highest = jnp.maximum(jnp.max(virt_s, axis=0, keepdims=True), jnp.max(side_s, axis=0, keepdims=True))
    highest = jnp.maximum(local_m, highest)
    virt_p = jnp.exp2(virt_s - highest)
    side_p = jnp.exp2(side_s - highest)
    factor = jnp.exp2(local_m - highest)
    total = factor * local_t
    total = total + jnp.sum(virt_p, axis=0, keepdims=True) + jnp.sum(side_p, axis=0, keepdims=True)
    share = 1.0 / total
    virt_p = virt_p * share
    side_p = side_p * share
    centre = factor * share * local_c + jnp.sum(virt_p * virt_d, axis=0, keepdims=True)
    centre = centre + jnp.sum(side_p * side_d, axis=0, keepdims=True)
    base = highest + LOG2E * jnp.log(total)
    parts = [part.astype(f32) for column in (base, centre) for part in split3(column)]
    parts_out[...] = stack_rows(parts, 0.0)
    virt_g = (virt_p * (virt_d - centre)).astype(bf16)
    virt_p = virt_p.astype(bf16)
    side_g = (side_p * (side_d - centre)).astype(bf16).astype(f32)
    side_p = side_p.astype(bf16).astype(f32)
    attended = dot(virt_t[64:96, 0:VIRT], virt_p)
    grad_query = dot(virt_t[0:32, 0:VIRT], virt_g)
    key_terms, value_terms = [], []
    for k in range(4):
        one_p, one_g = side_p[k : k + 1], side_g[k : k + 1]
        attended = attended + one_p * side_v[k]
        grad_query = grad_query + one_g * side_k[k]
        key_terms.append((SCALE * (one_g * q_wide)).astype(bf16).astype(f32))
        value_terms.append((one_p * g_wide).astype(bf16).astype(f32))
    near[...] = jnp.concatenate(key_terms[:2] + value_terms[:2], axis=0).T
    leave_rows(near, out)
    pair = [jnp.concatenate([key_terms[k], value_terms[k]], axis=0) for k in (2, 3)]
    out[:, 32:64, :] = to_slabs(gather_rows(found, pair))
    sums = jnp.concatenate([SCALE * dot_nt(q_t, virt_g), dot_nt(g_t, virt_p)], axis=0)
    hi = sums.astype(bf16).astype(f32)
    both_parts = jnp.concatenate([hi, sums - hi], axis=0)
    both_parts = jnp.concatenate([both_parts, jnp.zeros((128, 64), f32)], axis=1).T[0:VIRT]
    both_parts = both_parts.astype(bf16)
    for slab in range(SLABS):
        first = 16 * (slab & 3)
        out[slab, 64:80, :] = both_parts[first : first + 16]
    attended_out[...] = attended
    grad_query_out[...] = grad_query


def attend_kernel(
    parts, attended, grad_query, query_t, grad_t, table_t, cotangent_at, mask_at,
    local, result, out_term,
    cotangent, mask, sems,
):
    tiles = ROWS // TA
    copies = []
    for tile in range(tiles):
        span = pl.ds(tile * TA, TA)
        copies.append(pltpu.make_async_copy(mask_at.at[span], mask.at[span], sems.at[tile]))
    copies.append(pltpu.make_async_copy(cotangent_at, cotangent, sems.at[tiles]))
    for copy in copies:
        copy.start()
    all_keys, all_values = right_tables(table_t)
    q_t, g_t = query_t[...], grad_t[...]
    q_own = left_query(q_t, parts[...])
    g_own = left_grad(g_t, parts[...])
    key_t, value_t = table_t[0:32, :], table_t[32:64, :]
    grad_k = jnp.zeros((32, ROWS), f32)
    grad_v = jnp.zeros((32, ROWS), f32)
    for tile in range(tiles):
        span = slice(tile * TA, tile * TA + TA)
        copies[tile].wait()
        scores = jnp.where(mask[span, :] > 0, dot(q_own[span], all_keys), MASKED)
        weight = jnp.exp2(scores)
        local_p = weight.astype(bf16)
        local_g = (weight * dot(g_own[span], all_values)).astype(bf16)
        result[0:32, span] = (SCALE * (grad_query[:, span] + dot_nt(key_t, local_g))).astype(bf16)
        result[32:64, span] = (attended[:, span] + dot_nt(value_t, local_p)).astype(bf16)
        grad_k = grad_k + dot(q_t[:, span], local_g)
        grad_v = grad_v + dot(g_t[:, span], local_p)
    local[0:32, :] = SCALE * grad_k
    local[32:64, :] = grad_v
    copies[tiles].wait()
    out_term[...] = GRAD_SCALE * dot(result[32:64, :], cotangent[...])


def gather_kernel(arrived, places, local, result, rows_out, stacked_out, virt_out, near):
    found = split_places((places[0:1, :], places[1:2, :]))
    forward = scatter_rows(found, turn_parts(arrived[:, 0:32, :].reshape(ROWS, 128)))
    side = forward + spread_rows(arrived, 32, near).T
    keys_grad = (local[0:32, :] + side[0:32] + side[32:64]).astype(bf16)
    values_grad = (local[32:64, :] + side[64:96] + side[96:128]).astype(bf16)
    stacked = jnp.concatenate([result[0:32, :], keys_grad, values_grad, result[32:64, :]], axis=0)
    stacked_out[...] = stacked
    rows_out[:, 0:128, :] = stacked.astype(f32).T.astype(bf16).reshape(HEADS, 128, 128)
    parts = jnp.sum(arrived[:, 64:80, :].astype(f32), axis=0)
    virt = (parts + pltpu.roll(parts, 64, 1)).astype(bf16).astype(f32)
    inner = (lane((16, 128)) >= 32) & (lane((16, 128)) < 96)
    virt = jnp.where(inner, pltpu.roll(virt, 32, 1), 0.0)
    virt_out[...] = virt
    rows_out[:, 128:144, :] = jnp.broadcast_to(virt.astype(bf16)[None], (HEADS, 16, 128))


def partial_kernel(core, stacked, virt, feats, state, out_term, keep, give, held):
    virt = jnp.concatenate([virt[...], jnp.zeros((112, 128), f32)], axis=0)
    grads = dot(stacked[...], feats[...]) + dot(virt.T.astype(bf16), state[...])
    held[0] = GRAD_SCALE * grads[0:64]
    held[1, 0:32, :] = GRAD_SCALE * grads[64:96]
    held[1, 32:64, :] = out_term[...]
    keep[...] = held[core[0]]
    give[...] = held[1 - core[0]]


def mix_kernel(
    head, group, rows, weights0, weights1, weights2, weights3, feats_at, cotangent_at,
    columns, virt_out, feats, cotangent, turned, sems,
):
    which = head[0]
    span = pl.ds(pl.multiple_of(which * 128, 128), 128)
    copies = [
        pltpu.make_async_copy(feats_at.at[span], feats, sems.at[0]),
        pltpu.make_async_copy(cotangent_at.at[span], cotangent, sems.at[1]),
    ]
    for copy in copies:
        copy.start()
    grads = jnp.zeros((144, WIDTH), f32)
    mixed = jnp.zeros((128, WIDTH), f32)
    inner = lane((144, 128)) < 96
    for turn in (0, 4, 1, 5, 2, 6, 7, 3):
        row = rows[(which + turn) & 7]
        zero = jnp.zeros_like(row)
        source = (weights0, weights1, weights2, weights3)[turn & 3]
        at = 128 if turn in (3, 4, 5, 6) else 0
        weight = source[at : at + 128, :]
        grads = grads + dot(jnp.where(inner, row, zero), weight)
        mixed = mixed + dot(jnp.where(inner, zero, row)[0:128], weight)
    turned[...] = jnp.concatenate([grads[128:144], jnp.zeros((112, WIDTH), f32)], axis=0).T
    own = turned[pl.ds(pl.multiple_of(which * 32, 32), 32), :]
    virt_out[...] = pltpu.roll(own, 16 * group[0], 1)
    for copy in copies:
        copy.wait()
    grads = (cotangent[...].astype(f32) + grads[0:128]).T
    mixed = (feats[...].astype(f32) + mixed).T.astype(bf16)
    hi = grads.astype(bf16)
    low = (grads - hi.astype(f32)).astype(bf16)
    columns[:, 0:32, :] = mixed.reshape(HEADS, 32, 128)
    columns[:, 32:64, :] = hi.reshape(HEADS, 32, 128)
    columns[:, 64:96, :] = low.reshape(HEADS, 32, 128)


def finish_kernel(
    core, columns, near, far, virt0, virt1, virt2, virt3, member,
    mixed, grad_feats, grad_qkv, grad_out, grad_virtual, held,
):
    held[core[0]] = near[...]
    held[1 - core[0]] = far[...]
    grad_qkv[0:64, :] = held[0]
    grad_qkv[64:96, :] = held[1, 0:32, :]
    grad_out[...] = held[1, 32:64, :]
    virt = (virt0[...] + virt1[...]) + (virt2[...] + virt3[...])
    grad_virtual[...] = virt[:, :VIRT]
    lookup = POOL_SCALE * dot3(virt, hot(member[...] == iota((128, ROWS), 0)))
    for h in range(HEADS):
        at = slice(128 * h, 128 * h + 128)
        mixed[:, at] = columns[h, 0:32, :]
        whole = columns[h, 32:64, :].astype(f32) + columns[h, 64:96, :].astype(f32)
        grad_feats[:, at] = (whole + lookup[:, at]).astype(bf16)


def array(shape, kind):
    return jax.ShapeDtypeStruct(shape, kind)


VMEM = pl.BlockSpec(memory_space=pltpu.VMEM)
SMEM = pl.BlockSpec(memory_space=pltpu.SMEM)
HBM = pl.BlockSpec(memory_space=pltpu.HBM)


def call(kernel, specs, outs, scratch=(), mib=48, **named):
    return pl.pallas_call(
        kernel,
        out_shape=outs,
        in_specs=specs,
        out_specs=jax.tree.map(lambda _: VMEM, outs),
        scratch_shapes=list(scratch),
        compiler_params=pltpu.CompilerParams(vmem_limit_bytes=mib * 1024 * 1024),
        **named,
    )


def exchange(x, axis):
    return lax.all_to_all(x, axis, split_axis=0, concat_axis=0, tiled=True)


def swap(x, axis, k):
    return lax.ppermute(x, axis, [(i, i ^ k) for i in range(lax.axis_size(axis))])


def shift(x, k):
    return lax.ppermute(x, "head", [((h + k) % HEADS, h) for h in range(HEADS)])


def shards(feats, w_qkv, w_out, virt_embed, member, expander, local_mask, cotangent):
    slab = lax.axis_index("dom").astype(i32).reshape(1)
    head = lax.axis_index("head").astype(i32).reshape(1)
    members = member.reshape(1, ROWS)
    first = call(
        pool_kernel,
        [HBM] * 3,
        array((SLABS, 8, 128), f32),
        scratch=[
            pltpu.VMEM((ROWS, WIDTH), bf16),
            pltpu.VMEM((1, ROWS), i32),
            pltpu.VMEM((2, ROWS), i32),
            pltpu.SemaphoreType.DMA((3,)),
        ],
        mib=60,
    )(feats, members, expander.T)
    feats_late, first = lax.optimization_barrier([feats, first])
    first = exchange(first, "dom")
    table, kv_weights, share, embed, query_t, grad_t, table_t = call(
        project_kernel,
        [VMEM] * 5,
        (
            array((ROWS, 128), bf16),
            array((128, WIDTH), bf16),
            array((128, WIDTH), bf16),
            array((VIRT, WIDTH), bf16),
            array((32, ROWS), bf16),
            array((32, ROWS), bf16),
            array((64, ROWS), bf16),
        ),
    )(feats_late, cotangent, jnp.transpose(w_qkv, (0, 2, 1)), w_out, virt_embed)
    second, places, state = call(
        rows_kernel,
        [SMEM] + [VMEM] * 5,
        (array((SLABS, 80, 128), bf16), array((8, ROWS), f32), array((128, WIDTH), bf16)),
        scratch=[pltpu.VMEM((ROWS, 128), f32)],
    )(slab, first, table, table_t, embed, kv_weights)
    second, share, query_t = lax.optimization_barrier([second, share, query_t])
    two = jnp.concatenate([share, swap(share, "head", 4)], axis=0)
    across = lambda rows: pl.BlockSpec((rows, TI), lambda i: (0, i))
    stats = pl.pallas_call(
        local_kernel,
        grid=(ROWS // TI,),
        out_shape=array((8, ROWS), f32),
        in_specs=[across(32), across(32), pl.BlockSpec((TI, ROWS), lambda i: (i, 0)), VMEM],
        out_specs=across(8),
        compiler_params=pltpu.CompilerParams(vmem_limit_bytes=48 * 1024 * 1024),
    )(query_t, grad_t, local_mask, table_t)
    second, two, stats = lax.optimization_barrier([exchange(second, "dom"), two, stats])
    third, parts, attended, grad_query = call(
        side_kernel,
        [VMEM] * 5,
        (
            array((SLABS, 80, 128), bf16),
            array((8, ROWS), f32),
            array((32, ROWS), f32),
            array((32, ROWS), f32),
        ),
        scratch=[pltpu.VMEM((ROWS, 128), f32)],
    )(query_t, grad_t, stats, second, places)
    local, result, out_term = call(
        attend_kernel,
        [VMEM] * 6 + [HBM] * 2,
        (array((64, ROWS), f32), array((64, ROWS), bf16), array((32, WIDTH), f32)),
        scratch=[
            pltpu.VMEM((ROWS, WIDTH), bf16),
            pltpu.VMEM((ROWS, ROWS), i32),
            pltpu.SemaphoreType.DMA((ROWS // TA + 1,)),
        ],
    )(parts, attended, grad_query, query_t, grad_t, table_t, cotangent, local_mask)
    third, two = lax.optimization_barrier([third, two])
    others = [shift(two, k) for k in (1, 2, 7)]
    third, *others = lax.optimization_barrier([exchange(third, "dom")] + others)
    rows, stacked, virt = call(
        gather_kernel,
        [VMEM] * 4,
        (array((HEADS, 144, 128), bf16), array((128, ROWS), bf16), array((16, 128), f32)),
        scratch=[
            pltpu.VMEM((ROWS, 128), f32),
        ],
    )(third, places, local, result)
    rows, stacked = lax.optimization_barrier([rows, stacked])
    rows = exchange(rows, "head")
    keep, give = call(
        partial_kernel,
        [SMEM] + [VMEM] * 5,
        (array((64, WIDTH), f32), array((64, WIDTH), f32)),
        scratch=[pltpu.VMEM((2, 64, WIDTH), f32)],
    )(slab & 1, stacked, virt, feats, state, out_term)
    keep = keep + swap(give, "dom", 1)
    keep = (keep + swap(keep, "dom", 2)) + (swap(keep, "dom", 4) + swap(keep, "dom", 6))
    rows, keep = lax.optimization_barrier([rows, keep])
    columns, virt = call(
        mix_kernel,
        [SMEM] * 2 + [VMEM] * 5 + [HBM] * 2,
        (array((HEADS, 96, 128), bf16), array((32, 128), f32)),
        scratch=[
            pltpu.VMEM((128, WIDTH), bf16),
            pltpu.VMEM((128, WIDTH), bf16),
            pltpu.VMEM((WIDTH, 128), f32),
            pltpu.SemaphoreType.DMA((2,)),
        ],
    )(head, slab & 3, rows, two, *others, feats, cotangent)
    columns = exchange(columns, "head")
    keep = (keep + swap(keep, "dom", 8)) + (swap(keep, "dom", 16) + swap(keep, "dom", 24))
    virts = [virt] + [swap(virt, "dom", k) for k in (1, 2, 3)]
    mixed, grad_feats, grad_qkv, grad_out, grad_virtual = call(
        finish_kernel,
        [SMEM] + [VMEM] * 8,
        (
            array((32, ROWS), bf16),
            array((32, ROWS), bf16),
            array((96, WIDTH), f32),
            array((32, WIDTH), f32),
            array((32, VIRT), f32),
        ),
        scratch=[pltpu.VMEM((2, 64, WIDTH), f32)],
    )(slab & 1, columns, keep, swap(keep, "dom", 1), *virts, members)
    grad_qkv = jnp.transpose(grad_qkv.reshape(3, 32, WIDTH), (0, 2, 1))
    return (mixed.T, grad_feats.T, grad_qkv, grad_out, grad_virtual.T)


def solution(mesh):
    return jax.shard_map(
        shards,
        mesh=mesh,
        in_specs=(
            P("dom", None),
            P(None, None, "head"),
            P("head", None),
            P(),
            P("dom"),
            P("dom", None),
            P("dom", None),
            P("dom", None),
        ),
        out_specs=(
            P("dom", "head"),
            P("dom", "head"),
            P(None, None, "head"),
            P("head", None),
            P(None, "head"),
        ),
        check_vma=False,
    )
```

time: 485 us -> 103 us (0.21); the launches traced: 476 us -> 102 us
  waiting for transfers between devices: 189 us -> 17.5 us
  blocking collectives: 109 us -> 0 us
  matrix products: 40.9 us -> 0 us
  local copies, waits for them, and re-layouts: 49.4 us -> 8.74 us
  other arithmetic: 37.3 us -> 0.06 us
  starting transfers between devices: 35.7 us -> 56 us
  Pallas kernels: 0 us -> 19.3 us
  between operations: 15 us -> 0.82 us
    psum x1 -> x0, blocking collectives: 109 us -> none  [shards(): lax.psum(jnp.stack([grad_virt_keys.reshape(VIRT, width_local), grad_virt_...]
    reduce_scatter x3 -> x0, waiting for transfers between devices: 108 us -> none  [the longest x1 40 us: shards(): lax.psum_scatter(feats_part, 'head', scatter_dimension=1, tiled=True)]
    psum x2 -> x0, waiting for transfers between devices: 75 us -> none  [the longest x1 75 us: shards(): lax.psum(jnp.dot(member_cols, feats, preferred_element_type=jnp.float32),...]
    dot_general x26 -> x0, matrix products: 39.9 us -> none  [the longest x23 34.2 us: product(): return jnp.einsum(form, left, right, preferred_element_type=jnp.float32)]
    ppermute x0 -> x15, starting transfers between devices: none -> 23.3 us  [the longest x12 17.9 us: swap(): lax.ppermute(x, axis, [(i, i ^ k) for i in range(lax.axis_size(axis))])]
    pallas_call x0 -> x10, Pallas kernels: none -> 19.3 us  [the longest x1 4.14 us: shards(): call(attend_kernel, [VMEM] * 6 + [HBM] * 2, (array((64, ROWS), f32), arra...]
    gather x2 -> x0, local copies, waits for them, and re-layouts: 15.6 us -> none  [the longest x1 9.43 us: shards(): send_inverse = side_grads[:, EXP:][recv_place, branch_ids]]
    scatter-add x1 -> x0, other arithmetic: 11.9 us -> none  [shards(): from_forward = jnp.zeros((rows, 2 * width_local), jnp.float32).at[recv_pl...]
  transfers between devices with their start and end apart: 10 -> 20, of which waited for: 6 -> 9; matrix products, arithmetic and copies ran while one was open for 14% -> 0% of each run, Pallas kernels for 0% -> 9%
where the time goes in v1:
time: 103 us; the launch traced here: 102 us
  starting transfers between devices  56 us (54%)
  Pallas kernels  19.3 us (19%)
  waiting for transfers between devices  17.5 us (17%)
  local copies, waits for them, and re-layouts  8.74 us (8%)
    all_to_all x5, starting transfers between devices, exchange(): return lax.all_to_all(x, axis, split_axis=0, concat_axis=0, tiled=True)  32.7 us
    ppermute x12, starting transfers between devices, swap(): lax.ppermute(x, axis, [(i, i ^ k) for i in range(lax.axis_size(axis))])  17.9 us
    unnamed x20, local copies, waits for them, and re-layouts  8.74 us
    all_to_all x5, waiting for transfers between devices, exchange(): return lax.all_to_all(x, axis, split_axis=0, concat_axis=0, tiled=True)  8.21 us
    ppermute x12, waiting for transfers between devices, swap(): lax.ppermute(x, axis, [(i, i ^ k) for i in range(lax.axis_size(axis))])  8.07 us
    ppermute x3, starting transfers between devices, shift(): return lax.ppermute(x, 'head', [((h + k) % HEADS, h) for h in range(HEADS)])  5.38 us
    pallas_call x1, Pallas kernels, shards(): call(attend_kernel, [VMEM] * 6 + [HBM] * 2, (array((64, ROWS), f32), arra...  4.14 us
    pallas_call x1, Pallas kernels, shards(): pl.pallas_call(local_kernel, grid=(ROWS // TI,), out_shape=array((8, ROWS...  3.01 us
  transfers between devices with their start and end apart: 20, of which 9 were waited for; matrix products, arithmetic and copies ran while one was open for 0% of the time, Pallas kernels for 9%

profile of v1, /device:TPU:2, one launch (start us, length us, event | category | flops | bytes accessed | tf_op | source)
XLA Modules:
  0.0 102.4 jit_solution(11593312682653208200)
XLA Ops:
  0.6 2.2 %shard_map.119 = f32[32,8,128]{2,1,0:T(8,128)} custom-call(bf16[1024,256]{1,0:T(8,128)(2,1)} %feats_at.3, s32[1,1024]{1,0:T(1,128)} %bitcast.12, s32[2,1024]{1,0:T(2,128)} %bitcast.14), custom_call_target="tpu_custom_call" | custom-call | tf_op jit(solution)/shard_map/pallas_call | solution.py:500
  2.8 7.6 %all-to-all-start = ((f32[32,8,128]{2,1,0:T(8,128)}), f32[32,8,128]{2,1,0:T(8,128)S(1)}, u32[]{:S(2)}, u32[]{:S(2)}) async-start(f32[32,8,128]{2,1,0:T(8,128)} %shard_map.119), calls=%async_computation | async-start | bytes 262144 | tf_op jit(solution)/shard_map/all_to_all | solution.py:485
  11.5 1.0 %copy-done.4 = bf16[1024,256]{1,0:T(8,128)(2,1)S(1)} copy-done((bf16[1024,256]{1,0:T(8,128)(2,1)S(1)}, bf16[1024,256]{1,0:T(8,128)(2,1)}, u32[]{:S(2)}) %copy-start.4) | copy-done | bytes 524312
  15.5 1.6 %all-to-all-done.arrived = f32[32,8,128]{2,1,0:T(8,128)S(1)} async-done(((f32[32,8,128]{2,1,0:T(8,128)}), f32[32,8,128]{2,1,0:T(8,128)S(1)}, u32[]{:S(2)}, u32[]{:S(2)}) %all-to-all-start) | async-done | bytes 131104 | tf_op jit(solution)/shard_map/all_to_all | solution.py:485
  17.1 1.9 %shard_map.121 = (bf16[32,80,128]{2,1,0:T(8,128)(2,1)}, f32[8,1024]{1,0:T(8,128)S(1)}, bf16[128,256]{1,0:T(8,128)(2,1)S(1)}) custom-call(s32[1]{0:T(128)} %bitcast.slab, f32[32,8,128]{2,1,0:T(8,128)S(1)} %all-to-all-done.arrived, bf16[1024,128]{1,0:T(8,128)(2,1)S(1)} %get-tuple-element.54.table, bf16[64,1024]{1,0:T(8,128)(2,1)S(1)} %get-tuple-element.55.table_t, ...), custom_call_target="tpu_custom_call" | custom-call | tf_op jit(solution)/shard_map/pallas_call | solution.py:527
  19.1 5.9 %all-to-all-start.1 = ((bf16[32,80,128]{2,1,0:T(8,128)(2,1)}), bf16[32,80,128]{2,1,0:T(8,128)(2,1)S(1)}, u32[]{:S(2)}, u32[]{:S(2)}) async-start(bf16[32,80,128]{2,1,0:T(8,128)(2,1)} %get-tuple-element.63), calls=%async_computation.1 | async-start | bytes 1310720 | tf_op jit(solution)/shard_map/all_to_all | solution.py:485
  25.0 7.3 %collective-permute-start = (bf16[128,256]{1,0:T(8,128)(2,1)S(1)}, bf16[128,256]{1,0:T(8,128)(2,1)S(1)}, u32[]{:S(2)}, u32[]{:S(2)}) collective-permute-start(bf16[128,256]{1,0:T(8,128)(2,1)S(1)} %get-tuple-element.64), channel_id=1, source_target_pairs={{0,4},{1,5},{2,6},{3,7},{4,0},{5,1},{6,2},{7,3},{8,12},{9,13},{10,... | collective-permute-start | bytes 196616 | tf_op jit(solution)/shard_map/ppermute | solution.py:489
  32.3 2.2 %copy-done = s32[1024,1024]{1,0:T(8,128)S(1)} copy-done((s32[1024,1024]{1,0:T(8,128)S(1)}, s32[1024,1024]{1,0:T(8,128)}, u32[]{:S(2)}) %copy-start) | copy-done | bytes 4194328
  34.5 3.0 %shard_map.122.stats = f32[8,1024]{1,0:T(8,128)S(1)} custom-call(bf16[32,1024]{1,0:T(8,128)(2,1)S(1)} %get-tuple-element.61.query_t, bf16[32,1024]{1,0:T(8,128)(2,1)S(1)} %get-tuple-element.62.grad_t, s32[1024,1024]{1,0:T(8,128)S(1)} %copy-done, bf16[64,1024]{1,0:T(8,128)(2,1)S(1)} %get-tuple-element.55.table_t), custom_call_target="tpu_custom_call" | custom-call | tf_op jit(solution)/shard_map/pallas_call | solution.py:536
  37.5 3.0 %shard_map.123 = (bf16[32,80,128]{2,1,0:T(8,128)(2,1)}, f32[8,1024]{1,0:T(8,128)S(1)}, f32[32,1024]{1,0:T(8,128)S(1)}, f32[32,1024]{1,0:T(8,128)S(1)}) custom-call(bf16[32,1024]{1,0:T(8,128)(2,1)S(1)} %get-tuple-element.61.query_t, bf16[32,1024]{1,0:T(8,128)(2,1)S(1)} %get-tuple-element.62.grad_t, f32[8,1024]{1,0:T(8,128)S(1)} %shard_map.122.stats, ...), custom_call_target="tpu_custom_call" | custom-call | tf_op jit(solution)/shard_map/pallas_call | solution.py:545
  40.5 7.5 %all-to-all-start.2 = ((bf16[32,80,128]{2,1,0:T(8,128)(2,1)}), bf16[32,80,128]{2,1,0:T(8,128)(2,1)S(1)}, u32[]{:S(2)}, u32[]{:S(2)}) async-start(bf16[32,80,128]{2,1,0:T(8,128)(2,1)} %get-tuple-element.70), calls=%async_computation.2 | async-start | bytes 1310720 | tf_op jit(solution)/shard_map/all_to_all | solution.py:485
  48.0 1.1 %collective-permute-start.3 = (bf16[256,256]{1,0:T(8,128)(2,1)S(1)}, bf16[256,256]{1,0:T(8,128)(2,1)S(1)}, u32[]{:S(2)}, u32[]{:S(2)}) collective-permute-start(bf16[256,256]{1,0:T(8,128)(2,1)S(1)} %pad_maximum_fusion.weights0), channel_id=1, source_target_pairs={{7,0},{0,1},{1,2},{2,3},{3,4},{4,5},{5,6},{6,7},{15,8},{8,9},{9,10... | collective-permute-start | bytes 393224 | tf_op jit(solution)/shard_map/ppermute | solution.py:493
  49.1 3.0 %collective-permute-start.2 = (bf16[256,256]{1,0:T(8,128)(2,1)S(1)}, bf16[256,256]{1,0:T(8,128)(2,1)S(1)}, u32[]{:S(2)}, u32[]{:S(2)}) collective-permute-start(bf16[256,256]{1,0:T(8,128)(2,1)S(1)} %pad_maximum_fusion.weights0), channel_id=1, source_target_pairs={{2,0},{3,1},{4,2},{5,3},{6,4},{7,5},{0,6},{1,7},{10,8},{11,9},{12,... | collective-permute-start | bytes 393224 | tf_op jit(solution)/shard_map/ppermute | solution.py:493
  52.2 1.2 %collective-permute-start.1 = (bf16[256,256]{1,0:T(8,128)(2,1)S(1)}, bf16[256,256]{1,0:T(8,128)(2,1)S(1)}, u32[]{:S(2)}, u32[]{:S(2)}) collective-permute-start(bf16[256,256]{1,0:T(8,128)(2,1)S(1)} %pad_maximum_fusion.weights0), channel_id=1, source_target_pairs={{1,0},{2,1},{3,2},{4,3},{5,4},{6,5},{7,6},{0,7},{9,8},{10,9},{11,1... | collective-permute-start | bytes 393224 | tf_op jit(solution)/shard_map/ppermute | solution.py:493
  53.4 2.2 %copy-done.1 = s32[1024,1024]{1,0:T(8,128)S(1)} copy-done((s32[1024,1024]{1,0:T(8,128)S(1)}, s32[1024,1024]{1,0:T(8,128)}, u32[]{:S(2)}) %copy-start.1) | copy-done | bytes 4194328
  55.6 4.1 %shard_map.124 = (f32[64,1024]{1,0:T(8,128)S(1)}, bf16[64,1024]{1,0:T(8,128)(2,1)S(1)}, f32[32,256]{1,0:T(8,128)S(1)}) custom-call(f32[8,1024]{1,0:T(8,128)S(1)} %get-tuple-element.73.parts, f32[32,1024]{1,0:T(8,128)S(1)} %get-tuple-element.74.attended, f32[32,1024]{1,0:T(8,128)S(1)} %get-tuple-element.75.grad_query, ...), custom_call_target="tpu_custom_call" | custom-call | tf_op jit(solution)/shard_map/pallas_call | solution.py:556
  59.7 1.2 %collective-permute-done.1.weights1 = bf16[256,256]{1,0:T(8,128)(2,1)S(1)} collective-permute-done((bf16[256,256]{1,0:T(8,128)(2,1)S(1)}, bf16[256,256]{1,0:T(8,128)(2,1)S(1)}, u32[]{:S(2)}, u32[]{:S(2)}) %collective-permute-start.1) | collective-permute-done | bytes 131104 | tf_op jit(solution)/shard_map/ppermute | solution.py:493
  60.9 1.6 %shard_map.125 = (bf16[8,144,128]{2,1,0:T(8,128)(2,1)}, bf16[128,1024]{1,0:T(8,128)(2,1)S(1)}, f32[16,128]{1,0:T(8,128)S(1)}) custom-call(bf16[32,80,128]{2,1,0:T(8,128)(2,1)S(1)} %all-to-all-done.2.arrived, f32[8,1024]{1,0:T(8,128)S(1)} %get-tuple-element.67.places, f32[64,1024]{1,0:T(8,128)S(1)} %get-tuple-element.76.local, ...), custom_call_target="tpu_custom_call" | custom-call | tf_op jit(solution)/shard_map/pallas_call | solution.py:569
  62.5 5.6 %all-to-all-start.3 = ((bf16[8,144,128]{2,1,0:T(8,128)(2,1)}), bf16[8,144,128]{2,1,0:T(8,128)(2,1)S(1)}, u32[]{:S(2)}, u32[]{:S(2)}) async-start(bf16[8,144,128]{2,1,0:T(8,128)(2,1)} %get-tuple-element.80), calls=%async_computation.3 | async-start | bytes 589824 | tf_op jit(solution)/shard_map/all_to_all | solution.py:485
  68.6 1.2 %collective-permute-done.4 = f32[64,256]{1,0:T(8,128)S(1)} collective-permute-done((f32[64,256]{1,0:T(8,128)S(1)}, f32[64,256]{1,0:T(8,128)S(1)}, u32[]{:S(2)}, u32[]{:S(2)}) %collective-permute-start.4) | collective-permute-done | bytes 65568 | tf_op jit(solution)/shard_map/ppermute | solution.py:489
  69.8 2.8 %collective-permute-start.7 = (f32[64,256]{1,0:T(8,128)S(1)}, f32[64,256]{1,0:T(8,128)S(1)}, u32[]{:S(2)}, u32[]{:S(2)}) collective-permute-start(f32[64,256]{1,0:T(8,128)S(1)} %add.21), channel_id=1, source_target_pairs={{0,48},{8,56},{16,32},{24,40},{32,16},{40,24},{48,0},{56,8},{64,11... | collective-permute-start | bytes 196616 | tf_op jit(solution)/shard_map/ppermute | solution.py:489
  74.0 1.4 %collective-permute-done.7 = f32[64,256]{1,0:T(8,128)S(1)} collective-permute-done((f32[64,256]{1,0:T(8,128)S(1)}, f32[64,256]{1,0:T(8,128)S(1)}, u32[]{:S(2)}, u32[]{:S(2)}) %collective-permute-start.7) | collective-permute-done | bytes 65568 | tf_op jit(solution)/shard_map/ppermute | solution.py:489
  75.4 3.3 %collective-permute-done.6 = f32[64,256]{1,0:T(8,128)S(1)} collective-permute-done((f32[64,256]{1,0:T(8,128)S(1)}, f32[64,256]{1,0:T(8,128)S(1)}, u32[]{:S(2)}, u32[]{:S(2)}) %collective-permute-start.6) | collective-permute-done | bytes 65568 | tf_op jit(solution)/shard_map/ppermute | solution.py:489
  78.7 1.3 %all-to-all-done.3.rows = bf16[8,144,128]{2,1,0:T(8,128)(2,1)S(1)} async-done(((bf16[8,144,128]{2,1,0:T(8,128)(2,1)}), bf16[8,144,128]{2,1,0:T(8,128)(2,1)S(1)}, u32[]{:S(2)}, u32[]{:S(2)}) %all-to-all-start.3) | async-done | bytes 294944 | tf_op jit(solution)/shard_map/all_to_all | solution.py:485
  80.0 1.5 %collective-permute-start.10 = (f32[64,256]{1,0:T(8,128)S(1)}, f32[64,256]{1,0:T(8,128)S(1)}, u32[]{:S(2)}, u32[]{:S(2)}) collective-permute-start(f32[64,256]{1,0:T(8,128)S(1)} %add_add_fusion.1), channel_id=1, source_target_pairs={{0,192},{8,200},{16,208},{24,216},{32,224},{40,232},{48,240},{56,2... | collective-permute-start | bytes 196616 | tf_op jit(solution)/shard_map/ppermute | solution.py:489
  81.5 1.6 %collective-permute-start.9 = (f32[64,256]{1,0:T(8,128)S(1)}, f32[64,256]{1,0:T(8,128)S(1)}, u32[]{:S(2)}, u32[]{:S(2)}) collective-permute-start(f32[64,256]{1,0:T(8,128)S(1)} %add_add_fusion.1), channel_id=1, source_target_pairs={{0,128},{8,136},{16,144},{24,152},{32,160},{40,168},{48,176},{56,1... | collective-permute-start | bytes 196616 | tf_op jit(solution)/shard_map/ppermute | solution.py:489
  84.1 1.6 %shard_map.127 = (bf16[8,96,128]{2,1,0:T(8,128)(2,1)}, f32[32,128]{1,0:T(8,128)S(1)}) custom-call(s32[1]{0:T(128)} %bitcast.1.head, s32[1]{0:T(128)S(6)} %and.10.group, bf16[8,144,128]{2,1,0:T(8,128)(2,1)S(1)} %all-to-all-done.3.rows, bf16[256,256]{1,0:T(8,128)(2,1)S(1)} %pad_maximum_fusion.weights0, bf16[256,256]{1,0:T(8,128)(2,1)S(1)} %collective-permute-done.1.weights1, ...), custom_call_target="tpu_custom_call" | custom-call | tf_op jit(solution)/shard_map/pallas_call | solution.py:588
  85.7 6.0 %all-to-all-start.4 = ((bf16[8,96,128]{2,1,0:T(8,128)(2,1)}), bf16[8,96,128]{2,1,0:T(8,128)(2,1)S(1)}, u32[]{:S(2)}, u32[]{:S(2)}) async-start(bf16[8,96,128]{2,1,0:T(8,128)(2,1)} %get-tuple-element.91), calls=%async_computation.4 | async-start | bytes 393216 | tf_op jit(solution)/shard_map/all_to_all | solution.py:485
  92.4 1.6 %collective-permute-start.13 = (f32[32,128]{1,0:T(8,128)S(1)}, f32[32,128]{1,0:T(8,128)S(1)}, u32[]{:S(2)}, u32[]{:S(2)}) collective-permute-start(f32[32,128]{1,0:T(8,128)S(1)} %get-tuple-element.93.virt0), channel_id=1, source_target_pairs={{0,16},{8,24},{16,0},{24,8},{32,48},{40,56},{48,32},{56,40},{64,80... | collective-permute-start | bytes 49160 | tf_op jit(solution)/shard_map/ppermute | solution.py:489
  94.0 1.1 %collective-permute-done.14.virt3 = f32[32,128]{1,0:T(8,128)S(1)} collective-permute-done((f32[32,128]{1,0:T(8,128)S(1)}, f32[32,128]{1,0:T(8,128)S(1)}, u32[]{:S(2)}, u32[]{:S(2)}) %collective-permute-start.14) | collective-permute-done | bytes 16416 | tf_op jit(solution)/shard_map/ppermute | solution.py:489
  95.1 1.0 %collective-permute-done.13.virt2 = f32[32,128]{1,0:T(8,128)S(1)} collective-permute-done((f32[32,128]{1,0:T(8,128)S(1)}, f32[32,128]{1,0:T(8,128)S(1)}, u32[]{:S(2)}, u32[]{:S(2)}) %collective-permute-start.13) | collective-permute-done | bytes 16416 | tf_op jit(solution)/shard_map/ppermute | solution.py:489
  96.2 5.3 %all-to-all-done.4.columns = bf16[8,96,128]{2,1,0:T(8,128)(2,1)S(1)} async-done(((bf16[8,96,128]{2,1,0:T(8,128)(2,1)}), bf16[8,96,128]{2,1,0:T(8,128)(2,1)S(1)}, u32[]{:S(2)}, u32[]{:S(2)}) %all-to-all-start.4) | async-done | bytes 196640 | tf_op jit(solution)/shard_map/all_to_all | solution.py:485
  (42 shorter events, 8.5 us)
Async XLA Ops:
  2.8 14.3 %all-to-all-start = ((f32[32,8,128]{2,1,0:T(8,128)}), f32[32,8,128]{2,1,0:T(8,128)S(1)}, u32[]{:S(2)}, u32[]{:S(2)}) async-start(f32[32,8,128]{2,1,0:T(8,128)} %shard_map.119), calls=%async_computation | async-start | bytes 262144 | tf_op jit(solution)/shard_map/all_to_all | solution.py:485
  10.5 1.0 %copy-start.2 = (bf16[1024,256]{1,0:T(8,128)(2,1)S(1)}, bf16[1024,256]{1,0:T(8,128)(2,1)}, u32[]{:S(2)}) copy-start(bf16[1024,256]{1,0:T(8,128)(2,1)} %feats_at.3) | copy-start | bytes 1572868
  11.5 1.0 %copy-start.4 = (bf16[1024,256]{1,0:T(8,128)(2,1)S(1)}, bf16[1024,256]{1,0:T(8,128)(2,1)}, u32[]{:S(2)}) copy-start(bf16[1024,256]{1,0:T(8,128)(2,1)} %cotangent_at.3) | copy-start | bytes 1572868
  12.6 0.8 copy-start.6
  13.4 0.8 copy-start.7
  14.1 0.7 copy-start.8
  19.1 34.3 %copy-start.5 = (bf16[1024,256]{1,0:T(8,128)(2,1)S(1)}, bf16[1024,256]{1,0:T(8,128)(2,1)}, u32[]{:S(2)}) copy-start(bf16[1024,256]{1,0:T(8,128)(2,1)} %cotangent_at.3) | copy-start | bytes 1572868
  19.1 18.4 %all-to-all-start.1 = ((bf16[32,80,128]{2,1,0:T(8,128)(2,1)}), bf16[32,80,128]{2,1,0:T(8,128)(2,1)S(1)}, u32[]{:S(2)}, u32[]{:S(2)}) async-start(bf16[32,80,128]{2,1,0:T(8,128)(2,1)} %get-tuple-element.63), calls=%async_computation.1 | async-start | bytes 1310720 | tf_op jit(solution)/shard_map/all_to_all | solution.py:485
  25.0 12.5 %collective-permute-start = (bf16[128,256]{1,0:T(8,128)(2,1)S(1)}, bf16[128,256]{1,0:T(8,128)(2,1)S(1)}, u32[]{:S(2)}, u32[]{:S(2)}) collective-permute-start(bf16[128,256]{1,0:T(8,128)(2,1)S(1)} %get-tuple-element.64), channel_id=1, source_target_pairs={{0,4},{1,5},{2,6},{3,7},{4,0},{5,1},{6,2},{7,3},{8,12},{9,13},{10,... | collective-permute-start | bytes 196616 | tf_op jit(solution)/shard_map/ppermute | solution.py:489
  32.3 2.2 %copy-start = (s32[1024,1024]{1,0:T(8,128)S(1)}, s32[1024,1024]{1,0:T(8,128)}, u32[]{:S(2)}) copy-start(s32[1024,1024]{1,0:T(8,128)} %mask_at.1) | copy-start | bytes 12582916
  40.5 27.7 %copy-start.3 = (bf16[1024,256]{1,0:T(8,128)(2,1)S(1)}, bf16[1024,256]{1,0:T(8,128)(2,1)}, u32[]{:S(2)}) copy-start(bf16[1024,256]{1,0:T(8,128)(2,1)} %feats_at.3) | copy-start | bytes 1572868
  40.5 20.5 %all-to-all-start.2 = ((bf16[32,80,128]{2,1,0:T(8,128)(2,1)}), bf16[32,80,128]{2,1,0:T(8,128)(2,1)S(1)}, u32[]{:S(2)}, u32[]{:S(2)}) async-start(bf16[32,80,128]{2,1,0:T(8,128)(2,1)} %get-tuple-element.70), calls=%async_computation.2 | async-start | bytes 1310720 | tf_op jit(solution)/shard_map/all_to_all | solution.py:485
  48.0 11.7 %collective-permute-start.3 = (bf16[256,256]{1,0:T(8,128)(2,1)S(1)}, bf16[256,256]{1,0:T(8,128)(2,1)S(1)}, u32[]{:S(2)}, u32[]{:S(2)}) collective-permute-start(bf16[256,256]{1,0:T(8,128)(2,1)S(1)} %pad_maximum_fusion.weights0), channel_id=1, source_target_pairs={{7,0},{0,1},{1,2},{2,3},{3,4},{4,5},{5,6},{6,7},{15,8},{8,9},{9,10... | collective-permute-start | bytes 393224 | tf_op jit(solution)/shard_map/ppermute | solution.py:493
  49.1 10.6 %collective-permute-start.2 = (bf16[256,256]{1,0:T(8,128)(2,1)S(1)}, bf16[256,256]{1,0:T(8,128)(2,1)S(1)}, u32[]{:S(2)}, u32[]{:S(2)}) collective-permute-start(bf16[256,256]{1,0:T(8,128)(2,1)S(1)} %pad_maximum_fusion.weights0), channel_id=1, source_target_pairs={{2,0},{3,1},{4,2},{5,3},{6,4},{7,5},{0,6},{1,7},{10,8},{11,9},{12,... | collective-permute-start | bytes 393224 | tf_op jit(solution)/shard_map/ppermute | solution.py:493
  52.2 8.8 %collective-permute-start.1 = (bf16[256,256]{1,0:T(8,128)(2,1)S(1)}, bf16[256,256]{1,0:T(8,128)(2,1)S(1)}, u32[]{:S(2)}, u32[]{:S(2)}) collective-permute-start(bf16[256,256]{1,0:T(8,128)(2,1)S(1)} %pad_maximum_fusion.weights0), channel_id=1, source_target_pairs={{1,0},{2,1},{3,2},{4,3},{5,4},{6,5},{7,6},{0,7},{9,8},{10,9},{11,1... | collective-permute-start | bytes 393224 | tf_op jit(solution)/shard_map/ppermute | solution.py:493
  53.4 2.2 %copy-start.1 = (s32[1024,1024]{1,0:T(8,128)S(1)}, s32[1024,1024]{1,0:T(8,128)}, u32[]{:S(2)}) copy-start(s32[1024,1024]{1,0:T(8,128)} %mask_at.1) | copy-start | bytes 12582916
  55.6 45.9 %copy-start.9 = (s32[1024]{0:T(1024)S(1)}, s32[1024]{0:T(1024)}, u32[]{:S(2)}) copy-start(s32[1024]{0:T(1024)} %param.12) | copy-start | bytes 12292
  62.5 17.5 %all-to-all-start.3 = ((bf16[8,144,128]{2,1,0:T(8,128)(2,1)}), bf16[8,144,128]{2,1,0:T(8,128)(2,1)S(1)}, u32[]{:S(2)}, u32[]{:S(2)}) async-start(bf16[8,144,128]{2,1,0:T(8,128)(2,1)} %get-tuple-element.80), calls=%async_computation.3 | async-start | bytes 589824 | tf_op jit(solution)/shard_map/all_to_all | solution.py:485
  68.5 1.3 %collective-permute-start.4 = (f32[64,256]{1,0:T(8,128)S(1)}, f32[64,256]{1,0:T(8,128)S(1)}, u32[]{:S(2)}, u32[]{:S(2)}) collective-permute-start(f32[64,256]{1,0:T(8,128)S(1)} %get-tuple-element.86), channel_id=1, source_target_pairs={{0,8},{8,0},{16,24},{24,16},{32,40},{40,32},{48,56},{56,48},{64,72... | collective-permute-start | bytes 196616 | tf_op jit(solution)/shard_map/ppermute | solution.py:489
  69.8 5.6 %collective-permute-start.7 = (f32[64,256]{1,0:T(8,128)S(1)}, f32[64,256]{1,0:T(8,128)S(1)}, u32[]{:S(2)}, u32[]{:S(2)}) collective-permute-start(f32[64,256]{1,0:T(8,128)S(1)} %add.21), channel_id=1, source_target_pairs={{0,48},{8,56},{16,32},{24,40},{32,16},{40,24},{48,0},{56,8},{64,11... | collective-permute-start | bytes 196616 | tf_op jit(solution)/shard_map/ppermute | solution.py:489
  72.6 6.1 %collective-permute-start.6 = (f32[64,256]{1,0:T(8,128)S(1)}, f32[64,256]{1,0:T(8,128)S(1)}, u32[]{:S(2)}, u32[]{:S(2)}) collective-permute-start(f32[64,256]{1,0:T(8,128)S(1)} %add.21), channel_id=1, source_target_pairs={{0,32},{8,40},{16,48},{24,56},{32,0},{40,8},{48,16},{56,24},{64,96... | collective-permute-start | bytes 196616 | tf_op jit(solution)/shard_map/ppermute | solution.py:489
  73.5 5.2 %collective-permute-start.5 = (f32[64,256]{1,0:T(8,128)S(1)}, f32[64,256]{1,0:T(8,128)S(1)}, u32[]{:S(2)}, u32[]{:S(2)}) collective-permute-start(f32[64,256]{1,0:T(8,128)S(1)} %add.21), channel_id=1, source_target_pairs={{0,16},{8,24},{16,0},{24,8},{32,48},{40,56},{48,32},{56,40},{64,80... | collective-permute-start | bytes 196616 | tf_op jit(solution)/shard_map/ppermute | solution.py:489
  80.0 11.7 %collective-permute-start.10 = (f32[64,256]{1,0:T(8,128)S(1)}, f32[64,256]{1,0:T(8,128)S(1)}, u32[]{:S(2)}, u32[]{:S(2)}) collective-permute-start(f32[64,256]{1,0:T(8,128)S(1)} %add_add_fusion.1), channel_id=1, source_target_pairs={{0,192},{8,200},{16,208},{24,216},{32,224},{40,232},{48,240},{56,2... | collective-permute-start | bytes 196616 | tf_op jit(solution)/shard_map/ppermute | solution.py:489
  81.5 10.3 %collective-permute-start.9 = (f32[64,256]{1,0:T(8,128)S(1)}, f32[64,256]{1,0:T(8,128)S(1)}, u32[]{:S(2)}, u32[]{:S(2)}) collective-permute-start(f32[64,256]{1,0:T(8,128)S(1)} %add_add_fusion.1), channel_id=1, source_target_pairs={{0,128},{8,136},{16,144},{24,152},{32,160},{40,168},{48,176},{56,1... | collective-permute-start | bytes 196616 | tf_op jit(solution)/shard_map/ppermute | solution.py:489
  83.1 8.7 %collective-permute-start.8 = (f32[64,256]{1,0:T(8,128)S(1)}, f32[64,256]{1,0:T(8,128)S(1)}, u32[]{:S(2)}, u32[]{:S(2)}) collective-permute-start(f32[64,256]{1,0:T(8,128)S(1)} %add_add_fusion.1), channel_id=1, source_target_pairs={{0,64},{8,72},{16,80},{24,88},{32,96},{40,104},{48,112},{56,120},{... | collective-permute-start | bytes 196616 | tf_op jit(solution)/shard_map/ppermute | solution.py:489
  85.7 15.8 %all-to-all-start.4 = ((bf16[8,96,128]{2,1,0:T(8,128)(2,1)}), bf16[8,96,128]{2,1,0:T(8,128)(2,1)S(1)}, u32[]{:S(2)}, u32[]{:S(2)}) async-start(bf16[8,96,128]{2,1,0:T(8,128)(2,1)} %get-tuple-element.91), calls=%async_computation.4 | async-start | bytes 393216 | tf_op jit(solution)/shard_map/all_to_all | solution.py:485
  91.8 4.4 %collective-permute-start.11 = (f32[64,256]{1,0:T(8,128)S(1)}, f32[64,256]{1,0:T(8,128)S(1)}, u32[]{:S(2)}, u32[]{:S(2)}) collective-permute-start(f32[64,256]{1,0:T(8,128)S(1)} %add_add_fusion.near), channel_id=1, source_target_pairs={{0,8},{8,0},{16,24},{24,16},{32,40},{40,32},{48,56},{56,48},{64,72... | collective-permute-start | bytes 196616 | tf_op jit(solution)/shard_map/ppermute | solution.py:489
  91.9 3.3 %collective-permute-start.14 = (f32[32,128]{1,0:T(8,128)S(1)}, f32[32,128]{1,0:T(8,128)S(1)}, u32[]{:S(2)}, u32[]{:S(2)}) collective-permute-start(f32[32,128]{1,0:T(8,128)S(1)} %get-tuple-element.93.virt0), channel_id=1, source_target_pairs={{0,24},{8,16},{16,8},{24,0},{32,56},{40,48},{48,40},{56,32},{64,88... | collective-permute-start | bytes 49160 | tf_op jit(solution)/shard_map/ppermute | solution.py:489
  92.4 3.7 %collective-permute-start.13 = (f32[32,128]{1,0:T(8,128)S(1)}, f32[32,128]{1,0:T(8,128)S(1)}, u32[]{:S(2)}, u32[]{:S(2)}) collective-permute-start(f32[32,128]{1,0:T(8,128)S(1)} %get-tuple-element.93.virt0), channel_id=1, source_target_pairs={{0,16},{8,24},{16,0},{24,8},{32,48},{40,56},{48,32},{56,40},{64,80... | collective-permute-start | bytes 49160 | tf_op jit(solution)/shard_map/ppermute | solution.py:489
  94.0 2.2 %collective-permute-start.12 = (f32[32,128]{1,0:T(8,128)S(1)}, f32[32,128]{1,0:T(8,128)S(1)}, u32[]{:S(2)}, u32[]{:S(2)}) collective-permute-start(f32[32,128]{1,0:T(8,128)S(1)} %get-tuple-element.93.virt0), channel_id=1, source_target_pairs={{0,8},{8,0},{16,24},{24,16},{32,40},{40,32},{48,56},{56,48},{64,72... | collective-permute-start | bytes 49160 | tf_op jit(solution)/shard_map/ppermute | solution.py:489

commit v2 on v1

--- a/solution.py
+++ b/solution.py
@@ -405,7 +405,7 @@
 
 
 def mix_kernel(
-    head, group, rows, weights0, weights1, weights2, weights3, feats_at, cotangent_at,
+    head, group, rows, weights0, weights2, weights6, weights1, weights7, feats_at, cotangent_at,
     columns, virt_out, feats, cotangent, turned, sems,
 ):
     which = head[0]
@@ -419,11 +419,12 @@
     grads = jnp.zeros((144, WIDTH), f32)
     mixed = jnp.zeros((128, WIDTH), f32)
     inner = lane((144, 128)) < 96
-    for turn in (0, 4, 1, 5, 2, 6, 7, 3):
+    sources = {0: weights0, 4: weights0, 1: weights1, 5: weights1, 7: weights7, 3: weights7}
+    sources.update({2: weights2, 6: weights6})
+    for turn, source in sources.items():
         row = rows[(which + turn) & 7]
         zero = jnp.zeros_like(row)
-        source = (weights0, weights1, weights2, weights3)[turn & 3]
-        at = 128 if turn in (3, 4, 5, 6) else 0
+        at = 128 if turn in (3, 4, 5) else 0
         weight = source[at : at + 128, :]
         grads = grads + dot(jnp.where(inner, row, zero), weight)
         mixed = mixed + dot(jnp.where(inner, zero, row)[0:128], weight)
@@ -539,7 +540,7 @@
         out_shape=array((8, ROWS), f32),
         in_specs=[across(32), across(32), pl.BlockSpec((TI, ROWS), lambda i: (i, 0)), VMEM],
         out_specs=across(8),
-        compiler_params=pltpu.CompilerParams(vmem_limit_bytes=48 * 1024 * 1024),
+        compiler_params=pltpu.CompilerParams(vmem_limit_bytes=52 * 1024 * 1024),
     )(query_t, grad_t, local_mask, table_t)
     second, two, stats = lax.optimization_barrier([exchange(second, "dom"), two, stats])
     third, parts, attended, grad_query = call(
@@ -562,10 +563,11 @@
             pltpu.VMEM((ROWS, ROWS), i32),
             pltpu.SemaphoreType.DMA((ROWS // TA + 1,)),
         ],
+        mib=52,
     )(parts, attended, grad_query, query_t, grad_t, table_t, cotangent, local_mask)
-    third, two = lax.optimization_barrier([third, two])
-    others = [shift(two, k) for k in (1, 2, 7)]
-    third, *others = lax.optimization_barrier([exchange(third, "dom")] + others)
+    third, two, share = lax.optimization_barrier([third, two, share])
+    others = [shift(share, 2), shift(share, 6), shift(two, 1), shift(two, 7)]
+    third = exchange(third, "dom")
     rows, stacked, virt = call(
         gather_kernel,
         [VMEM] * 4,
@@ -574,7 +576,7 @@
             pltpu.VMEM((ROWS, 128), f32),
         ],
     )(third, places, local, result)
-    rows, stacked = lax.optimization_barrier([rows, stacked])
+    rows, stacked, *others = lax.optimization_barrier([rows, stacked] + others)
     rows = exchange(rows, "head")
     keep, give = call(
         partial_kernel,
@@ -587,7 +589,7 @@
     rows, keep = lax.optimization_barrier([rows, keep])
     columns, virt = call(
         mix_kernel,
-        [SMEM] * 2 + [VMEM] * 5 + [HBM] * 2,
+        [SMEM] * 2 + [VMEM] * 6 + [HBM] * 2,
         (array((HEADS, 96, 128), bf16), array((32, 128), f32)),
         scratch=[
             pltpu.VMEM((128, WIDTH), bf16),

time: 103 us -> 103 us (level)
  local copies, waits for them, and re-layouts: 8.74 us -> 4.36 us
  Pallas kernels: 19.3 us -> 22.1 us
  starting transfers between devices: 56 us -> 57.2 us
    unnamed x20 -> x16, local copies, waits for them, and re-layouts: 8.74 us -> 4.36 us
    pallas_call x1, Pallas kernels: 3.01 us -> 4.77 us  [shards(): pl.pallas_call(local_kernel, grid=(ROWS // TI,), out_shape=array((8, ROWS...]
    pallas_call x1, Pallas kernels: 4.14 us -> 5.21 us  [shards(): call(attend_kernel, [VMEM] * 6 + [HBM] * 2, (array((64, ROWS), f32), arra...]
    ppermute x3 -> x4, starting transfers between devices: 5.38 us -> 6.04 us  [shift(): return lax.ppermute(x, 'head', [((h + k) % HEADS, h) for h in range(HEADS)])]
  transfers between devices with their start and end apart: 20 -> 21, of which waited for: 9 -> 8; matrix products, arithmetic and copies ran while one was open for 0% -> 0% of each run, Pallas kernels for 9% -> 14%
where the time goes in v2:
time: 103 us; the launch traced here: 102 us
  starting transfers between devices  57.2 us (56%)
  Pallas kernels  22.1 us (21%)
  waiting for transfers between devices  17.3 us (17%)
  local copies, waits for them, and re-layouts  4.36 us (4%)
    all_to_all x5, starting transfers between devices, exchange(): return lax.all_to_all(x, axis, split_axis=0, concat_axis=0, tiled=True)  32.3 us
    ppermute x12, starting transfers between devices, swap(): lax.ppermute(x, axis, [(i, i ^ k) for i in range(lax.axis_size(axis))])  18.9 us
    all_to_all x5, waiting for transfers between devices, exchange(): return lax.all_to_all(x, axis, split_axis=0, concat_axis=0, tiled=True)  8.61 us
    ppermute x12, waiting for transfers between devices, swap(): lax.ppermute(x, axis, [(i, i ^ k) for i in range(lax.axis_size(axis))])  8.45 us
    ppermute x4, starting transfers between devices, shift(): return lax.ppermute(x, 'head', [((h + k) % HEADS, h) for h in range(HEADS)])  6.04 us
    pallas_call x1, Pallas kernels, shards(): call(attend_kernel, [VMEM] * 6 + [HBM] * 2, (array((64, ROWS), f32), arra...  5.21 us
    pallas_call x1, Pallas kernels, shards(): pl.pallas_call(local_kernel, grid=(ROWS // TI,), out_shape=array((8, ROWS...  4.77 us
    unnamed x16, local copies, waits for them, and re-layouts  4.36 us
  transfers between devices with their start and end apart: 21, of which 8 were waited for; matrix products, arithmetic and copies ran while one was open for 0% of the time, Pallas kernels for 14%

profile of v2, /device:TPU:2, one launch (start us, length us, event | category | flops | bytes accessed | tf_op | source)
XLA Modules:
  0.0 101.9 jit_solution(13360159942642936407)
XLA Ops:
  0.6 2.2 %shard_map.119 = f32[32,8,128]{2,1,0:T(8,128)} custom-call(bf16[1024,256]{1,0:T(8,128)(2,1)} %feats_at.3, s32[1,1024]{1,0:T(1,128)} %bitcast.12, s32[2,1024]{1,0:T(2,128)} %bitcast.14), custom_call_target="tpu_custom_call" | custom-call | tf_op jit(solution)/shard_map/pallas_call | solution.py:501
  2.8 7.6 %all-to-all-start = ((f32[32,8,128]{2,1,0:T(8,128)}), f32[32,8,128]{2,1,0:T(8,128)S(1)}, u32[]{:S(2)}, u32[]{:S(2)}) async-start(f32[32,8,128]{2,1,0:T(8,128)} %shard_map.119), calls=%async_computation | async-start | bytes 262144 | tf_op jit(solution)/shard_map/all_to_all | solution.py:486
  10.5 1.0 %copy-done = bf16[1024,256]{1,0:T(8,128)(2,1)S(1)} copy-done((bf16[1024,256]{1,0:T(8,128)(2,1)S(1)}, bf16[1024,256]{1,0:T(8,128)(2,1)}, u32[]{:S(2)}) %copy-start) | copy-done | bytes 524312
  11.5 1.0 %copy-done.2 = bf16[1024,256]{1,0:T(8,128)(2,1)S(1)} copy-done((bf16[1024,256]{1,0:T(8,128)(2,1)S(1)}, bf16[1024,256]{1,0:T(8,128)(2,1)}, u32[]{:S(2)}) %copy-start.2) | copy-done | bytes 524312
  12.6 0.8 copy-done.4
  15.5 1.6 %all-to-all-done.arrived = f32[32,8,128]{2,1,0:T(8,128)S(1)} async-done(((f32[32,8,128]{2,1,0:T(8,128)}), f32[32,8,128]{2,1,0:T(8,128)S(1)}, u32[]{:S(2)}, u32[]{:S(2)}) %all-to-all-start) | async-done | bytes 131104 | tf_op jit(solution)/shard_map/all_to_all | solution.py:486
  17.1 1.9 %shard_map.121 = (bf16[32,80,128]{2,1,0:T(8,128)(2,1)}, f32[8,1024]{1,0:T(8,128)S(1)}, bf16[128,256]{1,0:T(8,128)(2,1)S(1)}) custom-call(s32[1]{0:T(128)} %bitcast.slab, f32[32,8,128]{2,1,0:T(8,128)S(1)} %all-to-all-done.arrived, bf16[1024,128]{1,0:T(8,128)(2,1)S(1)} %get-tuple-element.55.table, bf16[64,1024]{1,0:T(8,128)(2,1)S(1)} %get-tuple-element.56.table_t, ...), custom_call_target="tpu_custom_call" | custom-call | tf_op jit(solution)/shard_map/pallas_call | solution.py:528
  19.1 5.9 %all-to-all-start.1 = ((bf16[32,80,128]{2,1,0:T(8,128)(2,1)}), bf16[32,80,128]{2,1,0:T(8,128)(2,1)S(1)}, u32[]{:S(2)}, u32[]{:S(2)}) async-start(bf16[32,80,128]{2,1,0:T(8,128)(2,1)} %get-tuple-element.64), calls=%async_computation.1 | async-start | bytes 1310720 | tf_op jit(solution)/shard_map/all_to_all | solution.py:486
  25.0 7.3 %collective-permute-start = (bf16[128,256]{1,0:T(8,128)(2,1)S(1)}, bf16[128,256]{1,0:T(8,128)(2,1)S(1)}, u32[]{:S(2)}, u32[]{:S(2)}) collective-permute-start(bf16[128,256]{1,0:T(8,128)(2,1)S(1)} %get-tuple-element.79), channel_id=1, source_target_pairs={{0,4},{1,5},{2,6},{3,7},{4,0},{5,1},{6,2},{7,3},{8,12},{9,13},{10,... | collective-permute-start | bytes 196616 | tf_op jit(solution)/shard_map/ppermute | solution.py:490
  32.3 4.8 %shard_map.122.stats = f32[8,1024]{1,0:T(8,128)S(1)} custom-call(bf16[32,1024]{1,0:T(8,128)(2,1)S(1)} %get-tuple-element.62.query_t, bf16[32,1024]{1,0:T(8,128)(2,1)S(1)} %get-tuple-element.63.grad_t, s32[1024,1024]{1,0:T(8,128)} %mask_at.1, bf16[64,1024]{1,0:T(8,128)(2,1)S(1)} %get-tuple-element.56.table_t), custom_call_target="tpu_custom_call" | custom-call | tf_op jit(solution)/shard_map/pallas_call | solution.py:537
  37.1 3.0 %shard_map.123 = (bf16[32,80,128]{2,1,0:T(8,128)(2,1)}, f32[8,1024]{1,0:T(8,128)S(1)}, f32[32,1024]{1,0:T(8,128)S(1)}, f32[32,1024]{1,0:T(8,128)S(1)}) custom-call(bf16[32,1024]{1,0:T(8,128)(2,1)S(1)} %get-tuple-element.62.query_t, bf16[32,1024]{1,0:T(8,128)(2,1)S(1)} %get-tuple-element.63.grad_t, f32[8,1024]{1,0:T(8,128)S(1)} %shard_map.122.stats, ...), custom_call_target="tpu_custom_call" | custom-call | tf_op jit(solution)/shard_map/pallas_call | solution.py:546
  40.1 7.5 %all-to-all-start.2 = ((bf16[32,80,128]{2,1,0:T(8,128)(2,1)}), bf16[32,80,128]{2,1,0:T(8,128)(2,1)S(1)}, u32[]{:S(2)}, u32[]{:S(2)}) async-start(bf16[32,80,128]{2,1,0:T(8,128)(2,1)} %get-tuple-element.71), calls=%async_computation.2 | async-start | bytes 1310720 | tf_op jit(solution)/shard_map/all_to_all | solution.py:486
  47.6 3.1 %collective-permute-start.3 = (bf16[256,256]{1,0:T(8,128)(2,1)S(1)}, bf16[256,256]{1,0:T(8,128)(2,1)S(1)}, u32[]{:S(2)}, u32[]{:S(2)}) collective-permute-start(bf16[256,256]{1,0:T(8,128)(2,1)S(1)} %pad_maximum_fusion.weights0), channel_id=1, source_target_pairs={{1,0},{2,1},{3,2},{4,3},{5,4},{6,5},{7,6},{0,7},{9,8},{10,9},{11,1... | collective-permute-start | bytes 393224 | tf_op jit(solution)/shard_map/ppermute | solution.py:494
  50.7 2.7 %collective-permute-start.1 = (bf16[128,256]{1,0:T(8,128)(2,1)S(1)}, bf16[128,256]{1,0:T(8,128)(2,1)S(1)}, u32[]{:S(2)}, u32[]{:S(2)}) collective-permute-start(bf16[128,256]{1,0:T(8,128)(2,1)S(1)} %get-tuple-element.79), channel_id=1, source_target_pairs={{2,0},{3,1},{4,2},{5,3},{6,4},{7,5},{0,6},{1,7},{10,8},{11,9},{12,... | collective-permute-start | bytes 196616 | tf_op jit(solution)/shard_map/ppermute | solution.py:494
  53.6 5.2 %shard_map.124 = (f32[64,1024]{1,0:T(8,128)S(1)}, bf16[64,1024]{1,0:T(8,128)(2,1)S(1)}, f32[32,256]{1,0:T(8,128)S(1)}) custom-call(f32[8,1024]{1,0:T(8,128)S(1)} %get-tuple-element.72.parts, f32[32,1024]{1,0:T(8,128)S(1)} %get-tuple-element.73.attended, f32[32,1024]{1,0:T(8,128)S(1)} %get-tuple-element.74.grad_query, ...), custom_call_target="tpu_custom_call" | custom-call | tf_op jit(solution)/shard_map/pallas_call | solution.py:557
  58.9 1.6 %shard_map.125 = (bf16[8,144,128]{2,1,0:T(8,128)(2,1)}, bf16[128,1024]{1,0:T(8,128)(2,1)S(1)}, f32[16,128]{1,0:T(8,128)S(1)}) custom-call(bf16[32,80,128]{2,1,0:T(8,128)(2,1)S(1)} %all-to-all-done.2.arrived, f32[8,1024]{1,0:T(8,128)S(1)} %get-tuple-element.68.places, f32[64,1024]{1,0:T(8,128)S(1)} %get-tuple-element.75.local, ...), custom_call_target="tpu_custom_call" | custom-call | tf_op jit(solution)/shard_map/pallas_call | solution.py:571
  60.6 5.6 %all-to-all-start.3 = ((bf16[8,144,128]{2,1,0:T(8,128)(2,1)}), bf16[8,144,128]{2,1,0:T(8,128)(2,1)S(1)}, u32[]{:S(2)}, u32[]{:S(2)}) async-start(bf16[8,144,128]{2,1,0:T(8,128)(2,1)} %get-tuple-element.81), calls=%async_computation.3 | async-start | bytes 589824 | tf_op jit(solution)/shard_map/all_to_all | solution.py:486
  66.6 1.2 %collective-permute-done.5 = f32[64,256]{1,0:T(8,128)S(1)} collective-permute-done((f32[64,256]{1,0:T(8,128)S(1)}, f32[64,256]{1,0:T(8,128)S(1)}, u32[]{:S(2)}, u32[]{:S(2)}) %collective-permute-start.5) | collective-permute-done | bytes 65568 | tf_op jit(solution)/shard_map/ppermute | solution.py:490
  67.9 1.5 %collective-permute-start.6 = (f32[64,256]{1,0:T(8,128)S(1)}, f32[64,256]{1,0:T(8,128)S(1)}, u32[]{:S(2)}, u32[]{:S(2)}) collective-permute-start(f32[64,256]{1,0:T(8,128)S(1)} %add.21), channel_id=1, source_target_pairs={{0,16},{8,24},{16,0},{24,8},{32,48},{40,56},{48,32},{56,40},{64,80... | collective-permute-start | bytes 196616 | tf_op jit(solution)/shard_map/ppermute | solution.py:490
  69.4 2.7 %collective-permute-start.7 = (f32[64,256]{1,0:T(8,128)S(1)}, f32[64,256]{1,0:T(8,128)S(1)}, u32[]{:S(2)}, u32[]{:S(2)}) collective-permute-start(f32[64,256]{1,0:T(8,128)S(1)} %add.21), channel_id=1, source_target_pairs={{0,32},{8,40},{16,48},{24,56},{32,0},{40,8},{48,16},{56,24},{64,96... | collective-permute-start | bytes 196616 | tf_op jit(solution)/shard_map/ppermute | solution.py:490
  72.6 3.0 %collective-permute-done.7 = f32[64,256]{1,0:T(8,128)S(1)} collective-permute-done((f32[64,256]{1,0:T(8,128)S(1)}, f32[64,256]{1,0:T(8,128)S(1)}, u32[]{:S(2)}, u32[]{:S(2)}) %collective-permute-start.7) | collective-permute-done | bytes 65568 | tf_op jit(solution)/shard_map/ppermute | solution.py:490
  75.6 1.9 %collective-permute-done.8 = f32[64,256]{1,0:T(8,128)S(1)} collective-permute-done((f32[64,256]{1,0:T(8,128)S(1)}, f32[64,256]{1,0:T(8,128)S(1)}, u32[]{:S(2)}, u32[]{:S(2)}) %collective-permute-start.8) | collective-permute-done | bytes 65568 | tf_op jit(solution)/shard_map/ppermute | solution.py:490
  77.6 1.6 %all-to-all-done.3.rows = bf16[8,144,128]{2,1,0:T(8,128)(2,1)S(1)} async-done(((bf16[8,144,128]{2,1,0:T(8,128)(2,1)}), bf16[8,144,128]{2,1,0:T(8,128)(2,1)S(1)}, u32[]{:S(2)}, u32[]{:S(2)}) %all-to-all-start.3) | async-done | bytes 294944 | tf_op jit(solution)/shard_map/all_to_all | solution.py:486
  79.2 1.4 %collective-permute-start.10 = (f32[64,256]{1,0:T(8,128)S(1)}, f32[64,256]{1,0:T(8,128)S(1)}, u32[]{:S(2)}, u32[]{:S(2)}) collective-permute-start(f32[64,256]{1,0:T(8,128)S(1)} %add_add_fusion.1), channel_id=1, source_target_pairs={{0,128},{8,136},{16,144},{24,152},{32,160},{40,168},{48,176},{56,1... | collective-permute-start | bytes 196616 | tf_op jit(solution)/shard_map/ppermute | solution.py:490
  80.6 1.9 %collective-permute-start.11 = (f32[64,256]{1,0:T(8,128)S(1)}, f32[64,256]{1,0:T(8,128)S(1)}, u32[]{:S(2)}, u32[]{:S(2)}) collective-permute-start(f32[64,256]{1,0:T(8,128)S(1)} %add_add_fusion.1), channel_id=1, source_target_pairs={{0,192},{8,200},{16,208},{24,216},{32,224},{40,232},{48,240},{56,2... | collective-permute-start | bytes 196616 | tf_op jit(solution)/shard_map/ppermute | solution.py:490
  82.5 1.4 %collective-permute-start.9 = (f32[64,256]{1,0:T(8,128)S(1)}, f32[64,256]{1,0:T(8,128)S(1)}, u32[]{:S(2)}, u32[]{:S(2)}) collective-permute-start(f32[64,256]{1,0:T(8,128)S(1)} %add_add_fusion.1), channel_id=1, source_target_pairs={{0,64},{8,72},{16,80},{24,88},{32,96},{40,104},{48,112},{56,120},{... | collective-permute-start | bytes 196616 | tf_op jit(solution)/shard_map/ppermute | solution.py:490
  83.9 1.6 %shard_map.127 = (bf16[8,96,128]{2,1,0:T(8,128)(2,1)}, f32[32,128]{1,0:T(8,128)S(1)}) custom-call(s32[1]{0:T(128)} %bitcast.1.head, s32[1]{0:T(128)S(6)} %and.10.group, bf16[8,144,128]{2,1,0:T(8,128)(2,1)S(1)} %all-to-all-done.3.rows, bf16[256,256]{1,0:T(8,128)(2,1)S(1)} %pad_maximum_fusion.weights0, bf16[128,256]{1,0:T(8,128)(2,1)S(1)} %collective-permute-done.1.weights2, ...), custom_call_target="tpu_custom_call" | custom-call | tf_op jit(solution)/shard_map/pallas_call | solution.py:590
  85.5 5.7 %all-to-all-start.4 = ((bf16[8,96,128]{2,1,0:T(8,128)(2,1)}), bf16[8,96,128]{2,1,0:T(8,128)(2,1)S(1)}, u32[]{:S(2)}, u32[]{:S(2)}) async-start(bf16[8,96,128]{2,1,0:T(8,128)(2,1)} %get-tuple-element.93), calls=%async_computation.4 | async-start | bytes 393216 | tf_op jit(solution)/shard_map/all_to_all | solution.py:486
  91.8 1.4 %collective-permute-start.15 = (f32[32,128]{1,0:T(8,128)S(1)}, f32[32,128]{1,0:T(8,128)S(1)}, u32[]{:S(2)}, u32[]{:S(2)}) collective-permute-start(f32[32,128]{1,0:T(8,128)S(1)} %get-tuple-element.95.virt0), channel_id=1, source_target_pairs={{0,24},{8,16},{16,8},{24,0},{32,56},{40,48},{48,40},{56,32},{64,88... | collective-permute-start | bytes 49160 | tf_op jit(solution)/shard_map/ppermute | solution.py:490
  93.3 2.3 %collective-permute-done.14.virt2 = f32[32,128]{1,0:T(8,128)S(1)} collective-permute-done((f32[32,128]{1,0:T(8,128)S(1)}, f32[32,128]{1,0:T(8,128)S(1)}, u32[]{:S(2)}, u32[]{:S(2)}) %collective-permute-start.14) | collective-permute-done | bytes 16416 | tf_op jit(solution)/shard_map/ppermute | solution.py:490
  95.6 5.4 %all-to-all-done.4.columns = bf16[8,96,128]{2,1,0:T(8,128)(2,1)S(1)} async-done(((bf16[8,96,128]{2,1,0:T(8,128)(2,1)}), bf16[8,96,128]{2,1,0:T(8,128)(2,1)S(1)}, u32[]{:S(2)}, u32[]{:S(2)}) %all-to-all-start.4) | async-done | bytes 196640 | tf_op jit(solution)/shard_map/all_to_all | solution.py:486
  101.0 0.9 shard_map.128
  (40 shorter events, 4.2 us)
Async XLA Ops:
  2.8 14.3 %all-to-all-start = ((f32[32,8,128]{2,1,0:T(8,128)}), f32[32,8,128]{2,1,0:T(8,128)S(1)}, u32[]{:S(2)}, u32[]{:S(2)}) async-start(f32[32,8,128]{2,1,0:T(8,128)} %shard_map.119), calls=%async_computation | async-start | bytes 262144 | tf_op jit(solution)/shard_map/all_to_all | solution.py:486
  10.5 1.0 %copy-start = (bf16[1024,256]{1,0:T(8,128)(2,1)S(1)}, bf16[1024,256]{1,0:T(8,128)(2,1)}, u32[]{:S(2)}) copy-start(bf16[1024,256]{1,0:T(8,128)(2,1)} %feats_at.3) | copy-start | bytes 1572868
  11.5 1.0 %copy-start.2 = (bf16[1024,256]{1,0:T(8,128)(2,1)S(1)}, bf16[1024,256]{1,0:T(8,128)(2,1)}, u32[]{:S(2)}) copy-start(bf16[1024,256]{1,0:T(8,128)(2,1)} %cotangent_at.3) | copy-start | bytes 1572868
  12.6 0.8 copy-start.4
  13.4 0.8 copy-start.5
  14.1 0.7 copy-start.6
  19.1 34.6 %copy-start.3 = (bf16[1024,256]{1,0:T(8,128)(2,1)S(1)}, bf16[1024,256]{1,0:T(8,128)(2,1)}, u32[]{:S(2)}) copy-start(bf16[1024,256]{1,0:T(8,128)(2,1)} %cotangent_at.3) | copy-start | bytes 1572868
  19.1 18.0 %all-to-all-start.1 = ((bf16[32,80,128]{2,1,0:T(8,128)(2,1)}), bf16[32,80,128]{2,1,0:T(8,128)(2,1)S(1)}, u32[]{:S(2)}, u32[]{:S(2)}) async-start(bf16[32,80,128]{2,1,0:T(8,128)(2,1)} %get-tuple-element.64), calls=%async_computation.1 | async-start | bytes 1310720 | tf_op jit(solution)/shard_map/all_to_all | solution.py:486
  25.0 12.0 %collective-permute-start = (bf16[128,256]{1,0:T(8,128)(2,1)S(1)}, bf16[128,256]{1,0:T(8,128)(2,1)S(1)}, u32[]{:S(2)}, u32[]{:S(2)}) collective-permute-start(bf16[128,256]{1,0:T(8,128)(2,1)S(1)} %get-tuple-element.79), channel_id=1, source_target_pairs={{0,4},{1,5},{2,6},{3,7},{4,0},{5,1},{6,2},{7,3},{8,12},{9,13},{10,... | collective-permute-start | bytes 196616 | tf_op jit(solution)/shard_map/ppermute | solution.py:490
  40.1 26.1 %copy-start.1 = (bf16[1024,256]{1,0:T(8,128)(2,1)S(1)}, bf16[1024,256]{1,0:T(8,128)(2,1)}, u32[]{:S(2)}) copy-start(bf16[1024,256]{1,0:T(8,128)(2,1)} %feats_at.3) | copy-start | bytes 1572868
  40.1 18.8 %all-to-all-start.2 = ((bf16[32,80,128]{2,1,0:T(8,128)(2,1)}), bf16[32,80,128]{2,1,0:T(8,128)(2,1)S(1)}, u32[]{:S(2)}, u32[]{:S(2)}) async-start(bf16[32,80,128]{2,1,0:T(8,128)(2,1)} %get-tuple-element.71), calls=%async_computation.2 | async-start | bytes 1310720 | tf_op jit(solution)/shard_map/all_to_all | solution.py:486
  47.6 13.1 %collective-permute-start.3 = (bf16[256,256]{1,0:T(8,128)(2,1)S(1)}, bf16[256,256]{1,0:T(8,128)(2,1)S(1)}, u32[]{:S(2)}, u32[]{:S(2)}) collective-permute-start(bf16[256,256]{1,0:T(8,128)(2,1)S(1)} %pad_maximum_fusion.weights0), channel_id=1, source_target_pairs={{1,0},{2,1},{3,2},{4,3},{5,4},{6,5},{7,6},{0,7},{9,8},{10,9},{11,1... | collective-permute-start | bytes 393224 | tf_op jit(solution)/shard_map/ppermute | solution.py:494
  50.7 9.9 %collective-permute-start.4 = (bf16[256,256]{1,0:T(8,128)(2,1)S(1)}, bf16[256,256]{1,0:T(8,128)(2,1)S(1)}, u32[]{:S(2)}, u32[]{:S(2)}) collective-permute-start(bf16[256,256]{1,0:T(8,128)(2,1)S(1)} %pad_maximum_fusion.weights0), channel_id=1, source_target_pairs={{7,0},{0,1},{1,2},{2,3},{3,4},{4,5},{5,6},{6,7},{15,8},{8,9},{9,10... | collective-permute-start | bytes 393224 | tf_op jit(solution)/shard_map/ppermute | solution.py:494
  50.7 9.7 %collective-permute-start.1 = (bf16[128,256]{1,0:T(8,128)(2,1)S(1)}, bf16[128,256]{1,0:T(8,128)(2,1)S(1)}, u32[]{:S(2)}, u32[]{:S(2)}) collective-permute-start(bf16[128,256]{1,0:T(8,128)(2,1)S(1)} %get-tuple-element.79), channel_id=1, source_target_pairs={{2,0},{3,1},{4,2},{5,3},{6,4},{7,5},{0,6},{1,7},{10,8},{11,9},{12,... | collective-permute-start | bytes 196616 | tf_op jit(solution)/shard_map/ppermute | solution.py:494
  53.4 7.2 %collective-permute-start.2 = (bf16[128,256]{1,0:T(8,128)(2,1)S(1)}, bf16[128,256]{1,0:T(8,128)(2,1)S(1)}, u32[]{:S(2)}, u32[]{:S(2)}) collective-permute-start(bf16[128,256]{1,0:T(8,128)(2,1)S(1)} %get-tuple-element.79), channel_id=1, source_target_pairs={{6,0},{7,1},{0,2},{1,3},{2,4},{3,5},{4,6},{5,7},{14,8},{15,9},{8,1... | collective-permute-start | bytes 196616 | tf_op jit(solution)/shard_map/ppermute | solution.py:494
  53.6 47.3 %copy-start.7 = (s32[1024]{0:T(1024)S(1)}, s32[1024]{0:T(1024)}, u32[]{:S(2)}) copy-start(s32[1024]{0:T(1024)} %param.12) | copy-start | bytes 12292
  60.6 18.6 %all-to-all-start.3 = ((bf16[8,144,128]{2,1,0:T(8,128)(2,1)}), bf16[8,144,128]{2,1,0:T(8,128)(2,1)S(1)}, u32[]{:S(2)}, u32[]{:S(2)}) async-start(bf16[8,144,128]{2,1,0:T(8,128)(2,1)} %get-tuple-element.81), calls=%async_computation.3 | async-start | bytes 589824 | tf_op jit(solution)/shard_map/all_to_all | solution.py:486
  66.5 1.3 %collective-permute-start.5 = (f32[64,256]{1,0:T(8,128)S(1)}, f32[64,256]{1,0:T(8,128)S(1)}, u32[]{:S(2)}, u32[]{:S(2)}) collective-permute-start(f32[64,256]{1,0:T(8,128)S(1)} %get-tuple-element.87), channel_id=1, source_target_pairs={{0,8},{8,0},{16,24},{24,16},{32,40},{40,32},{48,56},{56,48},{64,72... | collective-permute-start | bytes 196616 | tf_op jit(solution)/shard_map/ppermute | solution.py:490
  67.9 4.8 %collective-permute-start.6 = (f32[64,256]{1,0:T(8,128)S(1)}, f32[64,256]{1,0:T(8,128)S(1)}, u32[]{:S(2)}, u32[]{:S(2)}) collective-permute-start(f32[64,256]{1,0:T(8,128)S(1)} %add.21), channel_id=1, source_target_pairs={{0,16},{8,24},{16,0},{24,8},{32,48},{40,56},{48,32},{56,40},{64,80... | collective-permute-start | bytes 196616 | tf_op jit(solution)/shard_map/ppermute | solution.py:490
  69.4 6.2 %collective-permute-start.7 = (f32[64,256]{1,0:T(8,128)S(1)}, f32[64,256]{1,0:T(8,128)S(1)}, u32[]{:S(2)}, u32[]{:S(2)}) collective-permute-start(f32[64,256]{1,0:T(8,128)S(1)} %add.21), channel_id=1, source_target_pairs={{0,32},{8,40},{16,48},{24,56},{32,0},{40,8},{48,16},{56,24},{64,96... | collective-permute-start | bytes 196616 | tf_op jit(solution)/shard_map/ppermute | solution.py:490
  72.1 5.5 %collective-permute-start.8 = (f32[64,256]{1,0:T(8,128)S(1)}, f32[64,256]{1,0:T(8,128)S(1)}, u32[]{:S(2)}, u32[]{:S(2)}) collective-permute-start(f32[64,256]{1,0:T(8,128)S(1)} %add.21), channel_id=1, source_target_pairs={{0,48},{8,56},{16,32},{24,40},{32,16},{40,24},{48,0},{56,8},{64,11... | collective-permute-start | bytes 196616 | tf_op jit(solution)/shard_map/ppermute | solution.py:490
  79.2 12.0 %collective-permute-start.10 = (f32[64,256]{1,0:T(8,128)S(1)}, f32[64,256]{1,0:T(8,128)S(1)}, u32[]{:S(2)}, u32[]{:S(2)}) collective-permute-start(f32[64,256]{1,0:T(8,128)S(1)} %add_add_fusion.1), channel_id=1, source_target_pairs={{0,128},{8,136},{16,144},{24,152},{32,160},{40,168},{48,176},{56,1... | collective-permute-start | bytes 196616 | tf_op jit(solution)/shard_map/ppermute | solution.py:490
  80.6 10.6 %collective-permute-start.11 = (f32[64,256]{1,0:T(8,128)S(1)}, f32[64,256]{1,0:T(8,128)S(1)}, u32[]{:S(2)}, u32[]{:S(2)}) collective-permute-start(f32[64,256]{1,0:T(8,128)S(1)} %add_add_fusion.1), channel_id=1, source_target_pairs={{0,192},{8,200},{16,208},{24,216},{32,224},{40,232},{48,240},{56,2... | collective-permute-start | bytes 196616 | tf_op jit(solution)/shard_map/ppermute | solution.py:490
  82.5 8.7 %collective-permute-start.9 = (f32[64,256]{1,0:T(8,128)S(1)}, f32[64,256]{1,0:T(8,128)S(1)}, u32[]{:S(2)}, u32[]{:S(2)}) collective-permute-start(f32[64,256]{1,0:T(8,128)S(1)} %add_add_fusion.1), channel_id=1, source_target_pairs={{0,64},{8,72},{16,80},{24,88},{32,96},{40,104},{48,112},{56,120},{... | collective-permute-start | bytes 196616 | tf_op jit(solution)/shard_map/ppermute | solution.py:490
  85.5 15.5 %all-to-all-start.4 = ((bf16[8,96,128]{2,1,0:T(8,128)(2,1)}), bf16[8,96,128]{2,1,0:T(8,128)(2,1)S(1)}, u32[]{:S(2)}, u32[]{:S(2)}) async-start(bf16[8,96,128]{2,1,0:T(8,128)(2,1)} %get-tuple-element.93), calls=%async_computation.4 | async-start | bytes 393216 | tf_op jit(solution)/shard_map/all_to_all | solution.py:486
  91.2 4.3 %collective-permute-start.12 = (f32[64,256]{1,0:T(8,128)S(1)}, f32[64,256]{1,0:T(8,128)S(1)}, u32[]{:S(2)}, u32[]{:S(2)}) collective-permute-start(f32[64,256]{1,0:T(8,128)S(1)} %add_add_fusion.near), channel_id=1, source_target_pairs={{0,8},{8,0},{16,24},{24,16},{32,40},{40,32},{48,56},{56,48},{64,72... | collective-permute-start | bytes 196616 | tf_op jit(solution)/shard_map/ppermute | solution.py:490
  91.3 2.0 %collective-permute-start.13 = (f32[32,128]{1,0:T(8,128)S(1)}, f32[32,128]{1,0:T(8,128)S(1)}, u32[]{:S(2)}, u32[]{:S(2)}) collective-permute-start(f32[32,128]{1,0:T(8,128)S(1)} %get-tuple-element.95.virt0), channel_id=1, source_target_pairs={{0,8},{8,0},{16,24},{24,16},{32,40},{40,32},{48,56},{56,48},{64,72... | collective-permute-start | bytes 49160 | tf_op jit(solution)/shard_map/ppermute | solution.py:490
  91.8 3.7 %collective-permute-start.14 = (f32[32,128]{1,0:T(8,128)S(1)}, f32[32,128]{1,0:T(8,128)S(1)}, u32[]{:S(2)}, u32[]{:S(2)}) collective-permute-start(f32[32,128]{1,0:T(8,128)S(1)} %get-tuple-element.95.virt0), channel_id=1, source_target_pairs={{0,16},{8,24},{16,0},{24,8},{32,48},{40,56},{48,32},{56,40},{64,80... | collective-permute-start | bytes 49160 | tf_op jit(solution)/shard_map/ppermute | solution.py:490
  91.8 3.7 %collective-permute-start.15 = (f32[32,128]{1,0:T(8,128)S(1)}, f32[32,128]{1,0:T(8,128)S(1)}, u32[]{:S(2)}, u32[]{:S(2)}) collective-permute-start(f32[32,128]{1,0:T(8,128)S(1)} %get-tuple-element.95.virt0), channel_id=1, source_target_pairs={{0,24},{8,16},{16,8},{24,0},{32,56},{40,48},{48,40},{56,32},{64,88... | collective-permute-start | bytes 49160 | tf_op jit(solution)/shard_map/ppermute | solution.py:490

commit v3 on v2

--- a/solution.py
+++ b/solution.py
@@ -19,7 +19,7 @@
 POOL_SCALE = (VIRT / NODES) ** 0.5
 GRAD_SCALE = NODES ** (-0.5)
 TI = 256
-TA = 512
+TA = 256
 MASKED = -1e30
 LOG2E = 1.4426950408889634
 SCALE2 = SCALE * LOG2E
@@ -54,8 +54,9 @@
 
 
 def dot3(x, one_hot):
-    hi, mid, low = split3(x)
-    return dot(hi, one_hot) + dot(mid, one_hot) + dot(low, one_hot)
+    rows = x.shape[0]
+    got = dot(jnp.concatenate(split3(x), axis=0), one_hot)
+    return got[:rows] + got[rows : 2 * rows] + got[2 * rows :]
 
 
 def lane(shape):
@@ -79,7 +80,8 @@
     rows = []
     for e in range(2):
         pick = hot(iota((128, ROWS), 0) == 32 * e + (iota((128, ROWS), 1) & 31))
-        full = 32.0 * dot(hi, pick) + dot(low, pick)
+        full = dot(jnp.concatenate([hi, low], axis=0), pick)
+        full = 32.0 * full[:SLABS] + full[SLABS:]
         rows.append(jnp.sum(jnp.where(own, full, 0.0), axis=0, keepdims=True))
     return rows
 
@@ -421,13 +423,16 @@
     inner = lane((144, 128)) < 96
     sources = {0: weights0, 4: weights0, 1: weights1, 5: weights1, 7: weights7, 3: weights7}
     sources.update({2: weights2, 6: weights6})
-    for turn, source in sources.items():
-        row = rows[(which + turn) & 7]
-        zero = jnp.zeros_like(row)
-        at = 128 if turn in (3, 4, 5) else 0
-        weight = source[at : at + 128, :]
-        grads = grads + dot(jnp.where(inner, row, zero), weight)
-        mixed = mixed + dot(jnp.where(inner, zero, row)[0:128], weight)
+    turns = list(sources)
+    for two in (turns[0:2], turns[2:4], turns[4:6], turns[6:8]):
+        found = [rows[(which + turn) & 7] for turn in two]
+        zero = jnp.zeros_like(found[0])
+        weight = [sources[turn][pl.ds(128 if turn in (3, 4, 5) else 0, 128), :] for turn in two]
+        weight = jnp.concatenate(weight, axis=0)
+        left = jnp.concatenate([jnp.where(inner, row, zero) for row in found], axis=1)
+        grads = grads + dot(left, weight)
+        left = jnp.concatenate([jnp.where(inner, zero, row)[0:128] for row in found], axis=1)
+        mixed = mixed + dot(left, weight)
     turned[...] = jnp.concatenate([grads[128:144], jnp.zeros((112, WIDTH), f32)], axis=0).T
     own = turned[pl.ds(pl.multiple_of(which * 32, 32), 32), :]
     virt_out[...] = pltpu.roll(own, 16 * group[0], 1)
@@ -598,6 +603,7 @@
             pltpu.SemaphoreType.DMA((2,)),
         ],
     )(head, slab & 3, rows, two, *others, feats, cotangent)
+    columns, keep = lax.optimization_barrier([columns, keep])
     columns = exchange(columns, "head")
     keep = (keep + swap(keep, "dom", 8)) + (swap(keep, "dom", 16) + swap(keep, "dom", 24))
     virts = [virt] + [swap(virt, "dom", k) for k in (1, 2, 3)]

time: 103 us -> 102 us (level)
    all_to_all x5, starting transfers between devices: 32.3 us -> 31.1 us  [exchange(): return lax.all_to_all(x, axis, split_axis=0, concat_axis=0, tiled=True)]
  transfers between devices with their start and end apart: 21 -> 21, of which waited for: 8 -> 9; matrix products, arithmetic and copies ran while one was open for 0% -> 0% of each run, Pallas kernels for 14% -> 12%
where the time goes in v3:
time: 102 us; the launch traced here: 101 us
  starting transfers between devices  56.7 us (56%)
  Pallas kernels  21.4 us (21%)
  waiting for transfers between devices  17.9 us (18%)
  local copies, waits for them, and re-layouts  4.36 us (4%)
    all_to_all x5, starting transfers between devices, exchange(): return lax.all_to_all(x, axis, split_axis=0, concat_axis=0, tiled=True)  31.1 us
    ppermute x12, starting transfers between devices, swap(): lax.ppermute(x, axis, [(i, i ^ k) for i in range(lax.axis_size(axis))])  19.5 us
    all_to_all x5, waiting for transfers between devices, exchange(): return lax.all_to_all(x, axis, split_axis=0, concat_axis=0, tiled=True)  9.36 us
    ppermute x12, waiting for transfers between devices, swap(): lax.ppermute(x, axis, [(i, i ^ k) for i in range(lax.axis_size(axis))])  7.88 us
    ppermute x4, starting transfers between devices, shift(): return lax.ppermute(x, 'head', [((h + k) % HEADS, h) for h in range(HEADS)])  6.04 us
    pallas_call x1, Pallas kernels, shards(): pl.pallas_call(local_kernel, grid=(ROWS // TI,), out_shape=array((8, ROWS...  4.77 us
    pallas_call x1, Pallas kernels, shards(): call(attend_kernel, [VMEM] * 6 + [HBM] * 2, (array((64, ROWS), f32), arra...  4.62 us
    unnamed x16, local copies, waits for them, and re-layouts  4.36 us
  transfers between devices with their start and end apart: 21, of which 9 were waited for; matrix products, arithmetic and copies ran while one was open for 0% of the time, Pallas kernels for 12%

profile of v3, /device:TPU:2, one launch (start us, length us, event | category | flops | bytes accessed | tf_op | source)
XLA Modules:
  0.0 101.2 jit_solution(15204426554989674290)
XLA Ops:
  0.6 2.2 %shard_map.119 = f32[32,8,128]{2,1,0:T(8,128)} custom-call(bf16[1024,256]{1,0:T(8,128)(2,1)} %feats_at.3, s32[1,1024]{1,0:T(1,128)} %bitcast.12, s32[2,1024]{1,0:T(2,128)} %bitcast.14), custom_call_target="tpu_custom_call" | custom-call | tf_op jit(solution)/shard_map/pallas_call | solution.py:506
  2.8 7.6 %all-to-all-start = ((f32[32,8,128]{2,1,0:T(8,128)}), f32[32,8,128]{2,1,0:T(8,128)S(1)}, u32[]{:S(2)}, u32[]{:S(2)}) async-start(f32[32,8,128]{2,1,0:T(8,128)} %shard_map.119), calls=%async_computation | async-start | bytes 262144 | tf_op jit(solution)/shard_map/all_to_all | solution.py:491
  10.5 1.0 %copy-done = bf16[1024,256]{1,0:T(8,128)(2,1)S(1)} copy-done((bf16[1024,256]{1,0:T(8,128)(2,1)S(1)}, bf16[1024,256]{1,0:T(8,128)(2,1)}, u32[]{:S(2)}) %copy-start) | copy-done | bytes 524312
  11.5 1.0 %copy-done.2 = bf16[1024,256]{1,0:T(8,128)(2,1)S(1)} copy-done((bf16[1024,256]{1,0:T(8,128)(2,1)S(1)}, bf16[1024,256]{1,0:T(8,128)(2,1)}, u32[]{:S(2)}) %copy-start.2) | copy-done | bytes 524312
  15.5 1.6 %all-to-all-done.arrived = f32[32,8,128]{2,1,0:T(8,128)S(1)} async-done(((f32[32,8,128]{2,1,0:T(8,128)}), f32[32,8,128]{2,1,0:T(8,128)S(1)}, u32[]{:S(2)}, u32[]{:S(2)}) %all-to-all-start) | async-done | bytes 131104 | tf_op jit(solution)/shard_map/all_to_all | solution.py:491
  17.1 2.0 %shard_map.121 = (bf16[32,80,128]{2,1,0:T(8,128)(2,1)}, f32[8,1024]{1,0:T(8,128)S(1)}, bf16[128,256]{1,0:T(8,128)(2,1)S(1)}) custom-call(s32[1]{0:T(128)} %bitcast.slab, f32[32,8,128]{2,1,0:T(8,128)S(1)} %all-to-all-done.arrived, bf16[1024,128]{1,0:T(8,128)(2,1)S(1)} %get-tuple-element.57.table, bf16[64,1024]{1,0:T(8,128)(2,1)S(1)} %get-tuple-element.58.table_t, ...), custom_call_target="tpu_custom_call" | custom-call | tf_op jit(solution)/shard_map/pallas_call | solution.py:533
  19.1 5.9 %all-to-all-start.1 = ((bf16[32,80,128]{2,1,0:T(8,128)(2,1)}), bf16[32,80,128]{2,1,0:T(8,128)(2,1)S(1)}, u32[]{:S(2)}, u32[]{:S(2)}) async-start(bf16[32,80,128]{2,1,0:T(8,128)(2,1)} %get-tuple-element.66), calls=%async_computation.1 | async-start | bytes 1310720 | tf_op jit(solution)/shard_map/all_to_all | solution.py:491
  25.0 7.3 %collective-permute-start = (bf16[128,256]{1,0:T(8,128)(2,1)S(1)}, bf16[128,256]{1,0:T(8,128)(2,1)S(1)}, u32[]{:S(2)}, u32[]{:S(2)}) collective-permute-start(bf16[128,256]{1,0:T(8,128)(2,1)S(1)} %get-tuple-element.81), channel_id=1, source_target_pairs={{0,4},{1,5},{2,6},{3,7},{4,0},{5,1},{6,2},{7,3},{8,12},{9,13},{10,... | collective-permute-start | bytes 196616 | tf_op jit(solution)/shard_map/ppermute | solution.py:495
  32.3 4.8 %shard_map.122.stats = f32[8,1024]{1,0:T(8,128)S(1)} custom-call(bf16[32,1024]{1,0:T(8,128)(2,1)S(1)} %get-tuple-element.64.query_t, bf16[32,1024]{1,0:T(8,128)(2,1)S(1)} %get-tuple-element.65.grad_t, s32[1024,1024]{1,0:T(8,128)} %mask_at.1, bf16[64,1024]{1,0:T(8,128)(2,1)S(1)} %get-tuple-element.58.table_t), custom_call_target="tpu_custom_call" | custom-call | tf_op jit(solution)/shard_map/pallas_call | solution.py:542
  37.1 3.0 %shard_map.123 = (bf16[32,80,128]{2,1,0:T(8,128)(2,1)}, f32[8,1024]{1,0:T(8,128)S(1)}, f32[32,1024]{1,0:T(8,128)S(1)}, f32[32,1024]{1,0:T(8,128)S(1)}) custom-call(bf16[32,1024]{1,0:T(8,128)(2,1)S(1)} %get-tuple-element.64.query_t, bf16[32,1024]{1,0:T(8,128)(2,1)S(1)} %get-tuple-element.65.grad_t, f32[8,1024]{1,0:T(8,128)S(1)} %shard_map.122.stats, ...), custom_call_target="tpu_custom_call" | custom-call | tf_op jit(solution)/shard_map/pallas_call | solution.py:551
  40.1 7.5 %all-to-all-start.2 = ((bf16[32,80,128]{2,1,0:T(8,128)(2,1)}), bf16[32,80,128]{2,1,0:T(8,128)(2,1)S(1)}, u32[]{:S(2)}, u32[]{:S(2)}) async-start(bf16[32,80,128]{2,1,0:T(8,128)(2,1)} %get-tuple-element.73), calls=%async_computation.2 | async-start | bytes 1310720 | tf_op jit(solution)/shard_map/all_to_all | solution.py:491
  47.6 3.1 %collective-permute-start.3 = (bf16[256,256]{1,0:T(8,128)(2,1)S(1)}, bf16[256,256]{1,0:T(8,128)(2,1)S(1)}, u32[]{:S(2)}, u32[]{:S(2)}) collective-permute-start(bf16[256,256]{1,0:T(8,128)(2,1)S(1)} %pad_maximum_fusion.weights0), channel_id=1, source_target_pairs={{1,0},{2,1},{3,2},{4,3},{5,4},{6,5},{7,6},{0,7},{9,8},{10,9},{11,1... | collective-permute-start | bytes 393224 | tf_op jit(solution)/shard_map/ppermute | solution.py:499
  50.7 2.7 %collective-permute-start.1 = (bf16[128,256]{1,0:T(8,128)(2,1)S(1)}, bf16[128,256]{1,0:T(8,128)(2,1)S(1)}, u32[]{:S(2)}, u32[]{:S(2)}) collective-permute-start(bf16[128,256]{1,0:T(8,128)(2,1)S(1)} %get-tuple-element.81), channel_id=1, source_target_pairs={{2,0},{3,1},{4,2},{5,3},{6,4},{7,5},{0,6},{1,7},{10,8},{11,9},{12,... | collective-permute-start | bytes 196616 | tf_op jit(solution)/shard_map/ppermute | solution.py:499
  53.6 4.6 %shard_map.124 = (f32[64,1024]{1,0:T(8,128)S(1)}, bf16[64,1024]{1,0:T(8,128)(2,1)S(1)}, f32[32,256]{1,0:T(8,128)S(1)}) custom-call(f32[8,1024]{1,0:T(8,128)S(1)} %get-tuple-element.74.parts, f32[32,1024]{1,0:T(8,128)S(1)} %get-tuple-element.75.attended, f32[32,1024]{1,0:T(8,128)S(1)} %get-tuple-element.76.grad_query, ...), custom_call_target="tpu_custom_call" | custom-call | tf_op jit(solution)/shard_map/pallas_call | solution.py:562
  58.4 1.6 %shard_map.125 = (bf16[8,144,128]{2,1,0:T(8,128)(2,1)}, bf16[128,1024]{1,0:T(8,128)(2,1)S(1)}, f32[16,128]{1,0:T(8,128)S(1)}) custom-call(bf16[32,80,128]{2,1,0:T(8,128)(2,1)S(1)} %all-to-all-done.2.arrived, f32[8,1024]{1,0:T(8,128)S(1)} %get-tuple-element.70.places, f32[64,1024]{1,0:T(8,128)S(1)} %get-tuple-element.77.local, ...), custom_call_target="tpu_custom_call" | custom-call | tf_op jit(solution)/shard_map/pallas_call | solution.py:576
  60.7 5.0 %all-to-all-start.3 = ((bf16[8,144,128]{2,1,0:T(8,128)(2,1)}), bf16[8,144,128]{2,1,0:T(8,128)(2,1)S(1)}, u32[]{:S(2)}, u32[]{:S(2)}) async-start(bf16[8,144,128]{2,1,0:T(8,128)(2,1)} %get-tuple-element.83), calls=%async_computation.3 | async-start | bytes 589824 | tf_op jit(solution)/shard_map/all_to_all | solution.py:491
  66.6 0.9 collective-permute-done.5
  67.5 1.3 %collective-permute-start.6 = (f32[64,256]{1,0:T(8,128)S(1)}, f32[64,256]{1,0:T(8,128)S(1)}, u32[]{:S(2)}, u32[]{:S(2)}) collective-permute-start(f32[64,256]{1,0:T(8,128)S(1)} %add.21), channel_id=1, source_target_pairs={{0,16},{8,24},{16,0},{24,8},{32,48},{40,56},{48,32},{56,40},{64,80... | collective-permute-start | bytes 196616 | tf_op jit(solution)/shard_map/ppermute | solution.py:495
  68.8 2.7 %collective-permute-start.7 = (f32[64,256]{1,0:T(8,128)S(1)}, f32[64,256]{1,0:T(8,128)S(1)}, u32[]{:S(2)}, u32[]{:S(2)}) collective-permute-start(f32[64,256]{1,0:T(8,128)S(1)} %add.21), channel_id=1, source_target_pairs={{0,32},{8,40},{16,48},{24,56},{32,0},{40,8},{48,16},{56,24},{64,96... | collective-permute-start | bytes 196616 | tf_op jit(solution)/shard_map/ppermute | solution.py:495
  71.5 0.8 collective-permute-start.8
  72.3 2.7 %collective-permute-done.7 = f32[64,256]{1,0:T(8,128)S(1)} collective-permute-done((f32[64,256]{1,0:T(8,128)S(1)}, f32[64,256]{1,0:T(8,128)S(1)}, u32[]{:S(2)}, u32[]{:S(2)}) %collective-permute-start.7) | collective-permute-done | bytes 65568 | tf_op jit(solution)/shard_map/ppermute | solution.py:495
  75.1 1.9 %collective-permute-done.8 = f32[64,256]{1,0:T(8,128)S(1)} collective-permute-done((f32[64,256]{1,0:T(8,128)S(1)}, f32[64,256]{1,0:T(8,128)S(1)}, u32[]{:S(2)}, u32[]{:S(2)}) %collective-permute-start.8) | collective-permute-done | bytes 65568 | tf_op jit(solution)/shard_map/ppermute | solution.py:495
  77.0 2.2 %all-to-all-done.3.rows = bf16[8,144,128]{2,1,0:T(8,128)(2,1)S(1)} async-done(((bf16[8,144,128]{2,1,0:T(8,128)(2,1)}), bf16[8,144,128]{2,1,0:T(8,128)(2,1)S(1)}, u32[]{:S(2)}, u32[]{:S(2)}) %all-to-all-start.3) | async-done | bytes 294944 | tf_op jit(solution)/shard_map/all_to_all | solution.py:491
  79.2 1.4 %shard_map.127 = (bf16[8,96,128]{2,1,0:T(8,128)(2,1)}, f32[32,128]{1,0:T(8,128)S(1)}) custom-call(s32[1]{0:T(128)} %bitcast.1.head, s32[1]{0:T(128)S(6)} %and.10.group, bf16[8,144,128]{2,1,0:T(8,128)(2,1)S(1)} %all-to-all-done.3.rows, bf16[256,256]{1,0:T(8,128)(2,1)S(1)} %pad_maximum_fusion.weights0, bf16[128,256]{1,0:T(8,128)(2,1)S(1)} %collective-permute-done.1.weights2, ...), custom_call_target="tpu_custom_call" | custom-call | tf_op jit(solution)/shard_map/pallas_call | solution.py:595
  80.7 1.5 %collective-permute-start.10 = (f32[64,256]{1,0:T(8,128)S(1)}, f32[64,256]{1,0:T(8,128)S(1)}, u32[]{:S(2)}, u32[]{:S(2)}) collective-permute-start(f32[64,256]{1,0:T(8,128)S(1)} %add_add_fusion.1), channel_id=1, source_target_pairs={{0,128},{8,136},{16,144},{24,152},{32,160},{40,168},{48,176},{56,1... | collective-permute-start | bytes 196616 | tf_op jit(solution)/shard_map/ppermute | solution.py:495
  82.2 1.9 %collective-permute-start.11 = (f32[64,256]{1,0:T(8,128)S(1)}, f32[64,256]{1,0:T(8,128)S(1)}, u32[]{:S(2)}, u32[]{:S(2)}) collective-permute-start(f32[64,256]{1,0:T(8,128)S(1)} %add_add_fusion.1), channel_id=1, source_target_pairs={{0,192},{8,200},{16,208},{24,216},{32,224},{40,232},{48,240},{56,2... | collective-permute-start | bytes 196616 | tf_op jit(solution)/shard_map/ppermute | solution.py:495
  84.1 1.4 %collective-permute-start.9 = (f32[64,256]{1,0:T(8,128)S(1)}, f32[64,256]{1,0:T(8,128)S(1)}, u32[]{:S(2)}, u32[]{:S(2)}) collective-permute-start(f32[64,256]{1,0:T(8,128)S(1)} %add_add_fusion.1), channel_id=1, source_target_pairs={{0,64},{8,72},{16,80},{24,88},{32,96},{40,104},{48,112},{56,120},{... | collective-permute-start | bytes 196616 | tf_op jit(solution)/shard_map/ppermute | solution.py:495
  85.5 5.0 %all-to-all-start.4 = ((bf16[8,96,128]{2,1,0:T(8,128)(2,1)}), bf16[8,96,128]{2,1,0:T(8,128)(2,1)S(1)}, u32[]{:S(2)}, u32[]{:S(2)}) async-start(bf16[8,96,128]{2,1,0:T(8,128)(2,1)} %get-tuple-element.97), calls=%async_computation.4 | async-start | bytes 393216 | tf_op jit(solution)/shard_map/all_to_all | solution.py:491
  91.2 1.4 %collective-permute-start.15 = (f32[32,128]{1,0:T(8,128)S(1)}, f32[32,128]{1,0:T(8,128)S(1)}, u32[]{:S(2)}, u32[]{:S(2)}) collective-permute-start(f32[32,128]{1,0:T(8,128)S(1)} %get-tuple-element.99.virt0), channel_id=1, source_target_pairs={{0,24},{8,16},{16,8},{24,0},{32,56},{40,48},{48,40},{56,32},{64,88... | collective-permute-start | bytes 49160 | tf_op jit(solution)/shard_map/ppermute | solution.py:495
  92.6 2.3 %collective-permute-done.14.virt2 = f32[32,128]{1,0:T(8,128)S(1)} collective-permute-done((f32[32,128]{1,0:T(8,128)S(1)}, f32[32,128]{1,0:T(8,128)S(1)}, u32[]{:S(2)}, u32[]{:S(2)}) %collective-permute-start.14) | collective-permute-done | bytes 16416 | tf_op jit(solution)/shard_map/ppermute | solution.py:495
  94.9 5.4 %all-to-all-done.4.columns = bf16[8,96,128]{2,1,0:T(8,128)(2,1)S(1)} async-done(((bf16[8,96,128]{2,1,0:T(8,128)(2,1)}), bf16[8,96,128]{2,1,0:T(8,128)(2,1)S(1)}, u32[]{:S(2)}, u32[]{:S(2)}) %all-to-all-start.4) | async-done | bytes 196640 | tf_op jit(solution)/shard_map/all_to_all | solution.py:491
  100.3 0.9 shard_map.128
  (40 shorter events, 5.6 us)
Async XLA Ops:
  2.8 14.3 %all-to-all-start = ((f32[32,8,128]{2,1,0:T(8,128)}), f32[32,8,128]{2,1,0:T(8,128)S(1)}, u32[]{:S(2)}, u32[]{:S(2)}) async-start(f32[32,8,128]{2,1,0:T(8,128)} %shard_map.119), calls=%async_computation | async-start | bytes 262144 | tf_op jit(solution)/shard_map/all_to_all | solution.py:491
  10.5 1.0 %copy-start = (bf16[1024,256]{1,0:T(8,128)(2,1)S(1)}, bf16[1024,256]{1,0:T(8,128)(2,1)}, u32[]{:S(2)}) copy-start(bf16[1024,256]{1,0:T(8,128)(2,1)} %feats_at.3) | copy-start | bytes 1572868
  11.5 1.0 %copy-start.2 = (bf16[1024,256]{1,0:T(8,128)(2,1)S(1)}, bf16[1024,256]{1,0:T(8,128)(2,1)}, u32[]{:S(2)}) copy-start(bf16[1024,256]{1,0:T(8,128)(2,1)} %cotangent_at.3) | copy-start | bytes 1572868
  12.6 0.8 copy-start.4
  13.4 0.8 copy-start.5
  14.1 0.7 copy-start.6
  19.1 34.6 %copy-start.3 = (bf16[1024,256]{1,0:T(8,128)(2,1)S(1)}, bf16[1024,256]{1,0:T(8,128)(2,1)}, u32[]{:S(2)}) copy-start(bf16[1024,256]{1,0:T(8,128)(2,1)} %cotangent_at.3) | copy-start | bytes 1572868
  19.1 18.0 %all-to-all-start.1 = ((bf16[32,80,128]{2,1,0:T(8,128)(2,1)}), bf16[32,80,128]{2,1,0:T(8,128)(2,1)S(1)}, u32[]{:S(2)}, u32[]{:S(2)}) async-start(bf16[32,80,128]{2,1,0:T(8,128)(2,1)} %get-tuple-element.66), calls=%async_computation.1 | async-start | bytes 1310720 | tf_op jit(solution)/shard_map/all_to_all | solution.py:491
  25.0 12.0 %collective-permute-start = (bf16[128,256]{1,0:T(8,128)(2,1)S(1)}, bf16[128,256]{1,0:T(8,128)(2,1)S(1)}, u32[]{:S(2)}, u32[]{:S(2)}) collective-permute-start(bf16[128,256]{1,0:T(8,128)(2,1)S(1)} %get-tuple-element.81), channel_id=1, source_target_pairs={{0,4},{1,5},{2,6},{3,7},{4,0},{5,1},{6,2},{7,3},{8,12},{9,13},{10,... | collective-permute-start | bytes 196616 | tf_op jit(solution)/shard_map/ppermute | solution.py:495
  40.1 25.6 %copy-start.1 = (bf16[1024,256]{1,0:T(8,128)(2,1)S(1)}, bf16[1024,256]{1,0:T(8,128)(2,1)}, u32[]{:S(2)}) copy-start(bf16[1024,256]{1,0:T(8,128)(2,1)} %feats_at.3) | copy-start | bytes 1572868
  40.1 18.4 %all-to-all-start.2 = ((bf16[32,80,128]{2,1,0:T(8,128)(2,1)}), bf16[32,80,128]{2,1,0:T(8,128)(2,1)S(1)}, u32[]{:S(2)}, u32[]{:S(2)}) async-start(bf16[32,80,128]{2,1,0:T(8,128)(2,1)} %get-tuple-element.73), calls=%async_computation.2 | async-start | bytes 1310720 | tf_op jit(solution)/shard_map/all_to_all | solution.py:491
  47.6 13.1 %collective-permute-start.3 = (bf16[256,256]{1,0:T(8,128)(2,1)S(1)}, bf16[256,256]{1,0:T(8,128)(2,1)S(1)}, u32[]{:S(2)}, u32[]{:S(2)}) collective-permute-start(bf16[256,256]{1,0:T(8,128)(2,1)S(1)} %pad_maximum_fusion.weights0), channel_id=1, source_target_pairs={{1,0},{2,1},{3,2},{4,3},{5,4},{6,5},{7,6},{0,7},{9,8},{10,9},{11,1... | collective-permute-start | bytes 393224 | tf_op jit(solution)/shard_map/ppermute | solution.py:499
  50.7 9.9 %collective-permute-start.4 = (bf16[256,256]{1,0:T(8,128)(2,1)S(1)}, bf16[256,256]{1,0:T(8,128)(2,1)S(1)}, u32[]{:S(2)}, u32[]{:S(2)}) collective-permute-start(bf16[256,256]{1,0:T(8,128)(2,1)S(1)} %pad_maximum_fusion.weights0), channel_id=1, source_target_pairs={{7,0},{0,1},{1,2},{2,3},{3,4},{4,5},{5,6},{6,7},{15,8},{8,9},{9,10... | collective-permute-start | bytes 393224 | tf_op jit(solution)/shard_map/ppermute | solution.py:499
  50.7 9.3 %collective-permute-start.1 = (bf16[128,256]{1,0:T(8,128)(2,1)S(1)}, bf16[128,256]{1,0:T(8,128)(2,1)S(1)}, u32[]{:S(2)}, u32[]{:S(2)}) collective-permute-start(bf16[128,256]{1,0:T(8,128)(2,1)S(1)} %get-tuple-element.81), channel_id=1, source_target_pairs={{2,0},{3,1},{4,2},{5,3},{6,4},{7,5},{0,6},{1,7},{10,8},{11,9},{12,... | collective-permute-start | bytes 196616 | tf_op jit(solution)/shard_map/ppermute | solution.py:499
  53.4 7.2 %collective-permute-start.2 = (bf16[128,256]{1,0:T(8,128)(2,1)S(1)}, bf16[128,256]{1,0:T(8,128)(2,1)S(1)}, u32[]{:S(2)}, u32[]{:S(2)}) collective-permute-start(bf16[128,256]{1,0:T(8,128)(2,1)S(1)} %get-tuple-element.81), channel_id=1, source_target_pairs={{6,0},{7,1},{0,2},{1,3},{2,4},{3,5},{4,6},{5,7},{14,8},{15,9},{8,1... | collective-permute-start | bytes 196616 | tf_op jit(solution)/shard_map/ppermute | solution.py:499
  53.6 46.6 %copy-start.7 = (s32[1024]{0:T(1024)S(1)}, s32[1024]{0:T(1024)}, u32[]{:S(2)}) copy-start(s32[1024]{0:T(1024)} %param.12) | copy-start | bytes 12292
  60.7 18.6 %all-to-all-start.3 = ((bf16[8,144,128]{2,1,0:T(8,128)(2,1)}), bf16[8,144,128]{2,1,0:T(8,128)(2,1)S(1)}, u32[]{:S(2)}, u32[]{:S(2)}) async-start(bf16[8,144,128]{2,1,0:T(8,128)(2,1)} %get-tuple-element.83), calls=%async_computation.3 | async-start | bytes 589824 | tf_op jit(solution)/shard_map/all_to_all | solution.py:491
  66.0 1.5 %collective-permute-start.5 = (f32[64,256]{1,0:T(8,128)S(1)}, f32[64,256]{1,0:T(8,128)S(1)}, u32[]{:S(2)}, u32[]{:S(2)}) collective-permute-start(f32[64,256]{1,0:T(8,128)S(1)} %get-tuple-element.89), channel_id=1, source_target_pairs={{0,8},{8,0},{16,24},{24,16},{32,40},{40,32},{48,56},{56,48},{64,72... | collective-permute-start | bytes 196616 | tf_op jit(solution)/shard_map/ppermute | solution.py:495
  67.5 4.8 %collective-permute-start.6 = (f32[64,256]{1,0:T(8,128)S(1)}, f32[64,256]{1,0:T(8,128)S(1)}, u32[]{:S(2)}, u32[]{:S(2)}) collective-permute-start(f32[64,256]{1,0:T(8,128)S(1)} %add.21), channel_id=1, source_target_pairs={{0,16},{8,24},{16,0},{24,8},{32,48},{40,56},{48,32},{56,40},{64,80... | collective-permute-start | bytes 196616 | tf_op jit(solution)/shard_map/ppermute | solution.py:495
  68.8 6.2 %collective-permute-start.7 = (f32[64,256]{1,0:T(8,128)S(1)}, f32[64,256]{1,0:T(8,128)S(1)}, u32[]{:S(2)}, u32[]{:S(2)}) collective-permute-start(f32[64,256]{1,0:T(8,128)S(1)} %add.21), channel_id=1, source_target_pairs={{0,32},{8,40},{16,48},{24,56},{32,0},{40,8},{48,16},{56,24},{64,96... | collective-permute-start | bytes 196616 | tf_op jit(solution)/shard_map/ppermute | solution.py:495
  71.5 5.5 %collective-permute-start.8 = (f32[64,256]{1,0:T(8,128)S(1)}, f32[64,256]{1,0:T(8,128)S(1)}, u32[]{:S(2)}, u32[]{:S(2)}) collective-permute-start(f32[64,256]{1,0:T(8,128)S(1)} %add.21), channel_id=1, source_target_pairs={{0,48},{8,56},{16,32},{24,40},{32,16},{40,24},{48,0},{56,8},{64,11... | collective-permute-start | bytes 196616 | tf_op jit(solution)/shard_map/ppermute | solution.py:495
  80.7 9.8 %collective-permute-start.10 = (f32[64,256]{1,0:T(8,128)S(1)}, f32[64,256]{1,0:T(8,128)S(1)}, u32[]{:S(2)}, u32[]{:S(2)}) collective-permute-start(f32[64,256]{1,0:T(8,128)S(1)} %add_add_fusion.1), channel_id=1, source_target_pairs={{0,128},{8,136},{16,144},{24,152},{32,160},{40,168},{48,176},{56,1... | collective-permute-start | bytes 196616 | tf_op jit(solution)/shard_map/ppermute | solution.py:495
  82.2 8.3 %collective-permute-start.11 = (f32[64,256]{1,0:T(8,128)S(1)}, f32[64,256]{1,0:T(8,128)S(1)}, u32[]{:S(2)}, u32[]{:S(2)}) collective-permute-start(f32[64,256]{1,0:T(8,128)S(1)} %add_add_fusion.1), channel_id=1, source_target_pairs={{0,192},{8,200},{16,208},{24,216},{32,224},{40,232},{48,240},{56,2... | collective-permute-start | bytes 196616 | tf_op jit(solution)/shard_map/ppermute | solution.py:495
  84.1 6.4 %collective-permute-start.9 = (f32[64,256]{1,0:T(8,128)S(1)}, f32[64,256]{1,0:T(8,128)S(1)}, u32[]{:S(2)}, u32[]{:S(2)}) collective-permute-start(f32[64,256]{1,0:T(8,128)S(1)} %add_add_fusion.1), channel_id=1, source_target_pairs={{0,64},{8,72},{16,80},{24,88},{32,96},{40,104},{48,112},{56,120},{... | collective-permute-start | bytes 196616 | tf_op jit(solution)/shard_map/ppermute | solution.py:495
  85.5 14.8 %all-to-all-start.4 = ((bf16[8,96,128]{2,1,0:T(8,128)(2,1)}), bf16[8,96,128]{2,1,0:T(8,128)(2,1)S(1)}, u32[]{:S(2)}, u32[]{:S(2)}) async-start(bf16[8,96,128]{2,1,0:T(8,128)(2,1)} %get-tuple-element.97), calls=%async_computation.4 | async-start | bytes 393216 | tf_op jit(solution)/shard_map/all_to_all | solution.py:491
  90.6 4.3 %collective-permute-start.12 = (f32[64,256]{1,0:T(8,128)S(1)}, f32[64,256]{1,0:T(8,128)S(1)}, u32[]{:S(2)}, u32[]{:S(2)}) collective-permute-start(f32[64,256]{1,0:T(8,128)S(1)} %add_add_fusion.near), channel_id=1, source_target_pairs={{0,8},{8,0},{16,24},{24,16},{32,40},{40,32},{48,56},{56,48},{64,72... | collective-permute-start | bytes 196616 | tf_op jit(solution)/shard_map/ppermute | solution.py:495
  90.7 2.0 %collective-permute-start.13 = (f32[32,128]{1,0:T(8,128)S(1)}, f32[32,128]{1,0:T(8,128)S(1)}, u32[]{:S(2)}, u32[]{:S(2)}) collective-permute-start(f32[32,128]{1,0:T(8,128)S(1)} %get-tuple-element.99.virt0), channel_id=1, source_target_pairs={{0,8},{8,0},{16,24},{24,16},{32,40},{40,32},{48,56},{56,48},{64,72... | collective-permute-start | bytes 49160 | tf_op jit(solution)/shard_map/ppermute | solution.py:495
  91.2 3.7 %collective-permute-start.14 = (f32[32,128]{1,0:T(8,128)S(1)}, f32[32,128]{1,0:T(8,128)S(1)}, u32[]{:S(2)}, u32[]{:S(2)}) collective-permute-start(f32[32,128]{1,0:T(8,128)S(1)} %get-tuple-element.99.virt0), channel_id=1, source_target_pairs={{0,16},{8,24},{16,0},{24,8},{32,48},{40,56},{48,32},{56,40},{64,80... | collective-permute-start | bytes 49160 | tf_op jit(solution)/shard_map/ppermute | solution.py:495
  91.2 3.7 %collective-permute-start.15 = (f32[32,128]{1,0:T(8,128)S(1)}, f32[32,128]{1,0:T(8,128)S(1)}, u32[]{:S(2)}, u32[]{:S(2)}) collective-permute-start(f32[32,128]{1,0:T(8,128)S(1)} %get-tuple-element.99.virt0), channel_id=1, source_target_pairs={{0,24},{8,16},{16,8},{24,0},{32,56},{40,48},{48,40},{56,32},{64,88... | collective-permute-start | bytes 49160 | tf_op jit(solution)/shard_map/ppermute | solution.py:495

commit v4 on v3

--- a/solution.py
+++ b/solution.py
@@ -547,7 +547,8 @@
         out_specs=across(8),
         compiler_params=pltpu.CompilerParams(vmem_limit_bytes=52 * 1024 * 1024),
     )(query_t, grad_t, local_mask, table_t)
-    second, two, stats = lax.optimization_barrier([exchange(second, "dom"), two, stats])
+    after = shift(share, 2)
+    second, two, after, stats = lax.optimization_barrier([exchange(second, "dom"), two, after, stats])
     third, parts, attended, grad_query = call(
         side_kernel,
         [VMEM] * 5,
@@ -571,7 +572,7 @@
         mib=52,
     )(parts, attended, grad_query, query_t, grad_t, table_t, cotangent, local_mask)
     third, two, share = lax.optimization_barrier([third, two, share])
-    others = [shift(share, 2), shift(share, 6), shift(two, 1), shift(two, 7)]
+    others = [shift(share, 6), shift(two, 1), shift(two, 7)]
     third = exchange(third, "dom")
     rows, stacked, virt = call(
         gather_kernel,
@@ -602,7 +603,7 @@
             pltpu.VMEM((WIDTH, 128), f32),
             pltpu.SemaphoreType.DMA((2,)),
         ],
-    )(head, slab & 3, rows, two, *others, feats, cotangent)
+    )(head, slab & 3, rows, two, after, *others, feats, cotangent)
     columns, keep = lax.optimization_barrier([columns, keep])
     columns = exchange(columns, "head")
     keep = (keep + swap(keep, "dom", 8)) + (swap(keep, "dom", 16) + swap(keep, "dom", 24))

time: 102 us -> 103 us (level)
  waiting for transfers between devices: 17.9 us -> 21.5 us
  starting transfers between devices: 56.7 us -> 53.5 us
    all_to_all x5, waiting for transfers between devices: 9.36 us -> 11.9 us  [exchange(): return lax.all_to_all(x, axis, split_axis=0, concat_axis=0, tiled=True)]
    ppermute x4, starting transfers between devices: 6.04 us -> 4.04 us  [shift(): return lax.ppermute(x, 'head', [((h + k) % HEADS, h) for h in range(HEADS)])]
    ppermute x4, waiting for transfers between devices: 0.64 us -> 2.29 us  [shift(): return lax.ppermute(x, 'head', [((h + k) % HEADS, h) for h in range(HEADS)])]
    all_to_all x5, starting transfers between devices: 31.1 us -> 30 us  [exchange(): return lax.all_to_all(x, axis, split_axis=0, concat_axis=0, tiled=True)]
where the time goes in v4:
time: 103 us; the launch traced here: 102 us
  starting transfers between devices  53.5 us (52%)
  waiting for transfers between devices  21.5 us (21%)
  Pallas kernels  21.4 us (21%)
  local copies, waits for them, and re-layouts  4.36 us (4%)
    all_to_all x5, starting transfers between devices, exchange(): return lax.all_to_all(x, axis, split_axis=0, concat_axis=0, tiled=True)  30 us
    ppermute x12, starting transfers between devices, swap(): lax.ppermute(x, axis, [(i, i ^ k) for i in range(lax.axis_size(axis))])  19.5 us
    all_to_all x5, waiting for transfers between devices, exchange(): return lax.all_to_all(x, axis, split_axis=0, concat_axis=0, tiled=True)  11.9 us
    ppermute x12, waiting for transfers between devices, swap(): lax.ppermute(x, axis, [(i, i ^ k) for i in range(lax.axis_size(axis))])  7.38 us
    pallas_call x1, Pallas kernels, shards(): pl.pallas_call(local_kernel, grid=(ROWS // TI,), out_shape=array((8, ROWS...  4.77 us
    pallas_call x1, Pallas kernels, shards(): call(attend_kernel, [VMEM] * 6 + [HBM] * 2, (array((64, ROWS), f32), arra...  4.62 us
    unnamed x16, local copies, waits for them, and re-layouts  4.36 us
    ppermute x4, starting transfers between devices, shift(): return lax.ppermute(x, 'head', [((h + k) % HEADS, h) for h in range(HEADS)])  4.04 us
  transfers between devices with their start and end apart: 21, of which 9 were waited for; matrix products, arithmetic and copies ran while one was open for 0% of the time, Pallas kernels for 12%

profile of v4, /device:TPU:2, one launch (start us, length us, event | category | flops | bytes accessed | tf_op | source)
XLA Modules:
  0.0 101.6 jit_solution(16004056320467390216)
XLA Ops:
  0.6 2.2 %shard_map.119 = f32[32,8,128]{2,1,0:T(8,128)} custom-call(bf16[1024,256]{1,0:T(8,128)(2,1)} %feats_at.3, s32[1,1024]{1,0:T(1,128)} %bitcast.12, s32[2,1024]{1,0:T(2,128)} %bitcast.14), custom_call_target="tpu_custom_call" | custom-call | tf_op jit(solution)/shard_map/pallas_call | solution.py:506
  2.8 7.6 %all-to-all-start = ((f32[32,8,128]{2,1,0:T(8,128)}), f32[32,8,128]{2,1,0:T(8,128)S(1)}, u32[]{:S(2)}, u32[]{:S(2)}) async-start(f32[32,8,128]{2,1,0:T(8,128)} %shard_map.119), calls=%async_computation | async-start | bytes 262144 | tf_op jit(solution)/shard_map/all_to_all | solution.py:491
  10.5 1.0 %copy-done = bf16[1024,256]{1,0:T(8,128)(2,1)S(1)} copy-done((bf16[1024,256]{1,0:T(8,128)(2,1)S(1)}, bf16[1024,256]{1,0:T(8,128)(2,1)}, u32[]{:S(2)}) %copy-start) | copy-done | bytes 524312
  11.5 1.0 %copy-done.2 = bf16[1024,256]{1,0:T(8,128)(2,1)S(1)} copy-done((bf16[1024,256]{1,0:T(8,128)(2,1)S(1)}, bf16[1024,256]{1,0:T(8,128)(2,1)}, u32[]{:S(2)}) %copy-start.2) | copy-done | bytes 524312
  15.5 1.6 %all-to-all-done.arrived = f32[32,8,128]{2,1,0:T(8,128)S(1)} async-done(((f32[32,8,128]{2,1,0:T(8,128)}), f32[32,8,128]{2,1,0:T(8,128)S(1)}, u32[]{:S(2)}, u32[]{:S(2)}) %all-to-all-start) | async-done | bytes 131104 | tf_op jit(solution)/shard_map/all_to_all | solution.py:491
  17.1 2.0 %shard_map.121 = (bf16[32,80,128]{2,1,0:T(8,128)(2,1)}, f32[8,1024]{1,0:T(8,128)S(1)}, bf16[128,256]{1,0:T(8,128)(2,1)S(1)}) custom-call(s32[1]{0:T(128)} %bitcast.slab, f32[32,8,128]{2,1,0:T(8,128)S(1)} %all-to-all-done.arrived, bf16[1024,128]{1,0:T(8,128)(2,1)S(1)} %get-tuple-element.57.table, bf16[64,1024]{1,0:T(8,128)(2,1)S(1)} %get-tuple-element.58.table_t, ...), custom_call_target="tpu_custom_call" | custom-call | tf_op jit(solution)/shard_map/pallas_call | solution.py:533
  19.1 5.9 %all-to-all-start.1 = ((bf16[32,80,128]{2,1,0:T(8,128)(2,1)}), bf16[32,80,128]{2,1,0:T(8,128)(2,1)S(1)}, u32[]{:S(2)}, u32[]{:S(2)}) async-start(bf16[32,80,128]{2,1,0:T(8,128)(2,1)} %get-tuple-element.66), calls=%async_computation.1 | async-start | bytes 1310720 | tf_op jit(solution)/shard_map/all_to_all | solution.py:491
  25.0 7.3 %collective-permute-start = (bf16[128,256]{1,0:T(8,128)(2,1)S(1)}, bf16[128,256]{1,0:T(8,128)(2,1)S(1)}, u32[]{:S(2)}, u32[]{:S(2)}) collective-permute-start(bf16[128,256]{1,0:T(8,128)(2,1)S(1)} %get-tuple-element.81), channel_id=1, source_target_pairs={{0,4},{1,5},{2,6},{3,7},{4,0},{5,1},{6,2},{7,3},{8,12},{9,13},{10,... | collective-permute-start | bytes 196616 | tf_op jit(solution)/shard_map/ppermute | solution.py:495
  32.3 4.8 %shard_map.122.stats = f32[8,1024]{1,0:T(8,128)S(1)} custom-call(bf16[32,1024]{1,0:T(8,128)(2,1)S(1)} %get-tuple-element.64.query_t, bf16[32,1024]{1,0:T(8,128)(2,1)S(1)} %get-tuple-element.65.grad_t, s32[1024,1024]{1,0:T(8,128)} %mask_at.1, bf16[64,1024]{1,0:T(8,128)(2,1)S(1)} %get-tuple-element.58.table_t), custom_call_target="tpu_custom_call" | custom-call | tf_op jit(solution)/shard_map/pallas_call | solution.py:542
  37.1 2.3 %collective-permute-done.1.weights2 = bf16[128,256]{1,0:T(8,128)(2,1)S(1)} collective-permute-done((bf16[128,256]{1,0:T(8,128)(2,1)S(1)}, bf16[128,256]{1,0:T(8,128)(2,1)S(1)}, u32[]{:S(2)}, u32[]{:S(2)}) %collective-permute-start.1) | collective-permute-done | bytes 65568 | tf_op jit(solution)/shard_map/ppermute | solution.py:499
  39.4 3.0 %shard_map.123 = (bf16[32,80,128]{2,1,0:T(8,128)(2,1)}, f32[8,1024]{1,0:T(8,128)S(1)}, f32[32,1024]{1,0:T(8,128)S(1)}, f32[32,1024]{1,0:T(8,128)S(1)}) custom-call(bf16[32,1024]{1,0:T(8,128)(2,1)S(1)} %get-tuple-element.64.query_t, bf16[32,1024]{1,0:T(8,128)(2,1)S(1)} %get-tuple-element.65.grad_t, f32[8,1024]{1,0:T(8,128)S(1)} %shard_map.122.stats, ...), custom_call_target="tpu_custom_call" | custom-call | tf_op jit(solution)/shard_map/pallas_call | solution.py:552
  42.4 7.5 %all-to-all-start.2 = ((bf16[32,80,128]{2,1,0:T(8,128)(2,1)}), bf16[32,80,128]{2,1,0:T(8,128)(2,1)S(1)}, u32[]{:S(2)}, u32[]{:S(2)}) async-start(bf16[32,80,128]{2,1,0:T(8,128)(2,1)} %get-tuple-element.73), calls=%async_computation.2 | async-start | bytes 1310720 | tf_op jit(solution)/shard_map/all_to_all | solution.py:491
  49.9 3.1 %collective-permute-start.3 = (bf16[256,256]{1,0:T(8,128)(2,1)S(1)}, bf16[256,256]{1,0:T(8,128)(2,1)S(1)}, u32[]{:S(2)}, u32[]{:S(2)}) collective-permute-start(bf16[256,256]{1,0:T(8,128)(2,1)S(1)} %pad_maximum_fusion.weights0), channel_id=1, source_target_pairs={{1,0},{2,1},{3,2},{4,3},{5,4},{6,5},{7,6},{0,7},{9,8},{10,9},{11,1... | collective-permute-start | bytes 393224 | tf_op jit(solution)/shard_map/ppermute | solution.py:499
  52.9 1.0 collective-permute-start.2
  53.9 4.6 %shard_map.124 = (f32[64,1024]{1,0:T(8,128)S(1)}, bf16[64,1024]{1,0:T(8,128)(2,1)S(1)}, f32[32,256]{1,0:T(8,128)S(1)}) custom-call(f32[8,1024]{1,0:T(8,128)S(1)} %get-tuple-element.74.parts, f32[32,1024]{1,0:T(8,128)S(1)} %get-tuple-element.75.attended, f32[32,1024]{1,0:T(8,128)S(1)} %get-tuple-element.76.grad_query, ...), custom_call_target="tpu_custom_call" | custom-call | tf_op jit(solution)/shard_map/pallas_call | solution.py:563
  58.5 2.2 %all-to-all-done.2.arrived = bf16[32,80,128]{2,1,0:T(8,128)(2,1)S(1)} async-done(((bf16[32,80,128]{2,1,0:T(8,128)(2,1)}), bf16[32,80,128]{2,1,0:T(8,128)(2,1)S(1)}, u32[]{:S(2)}, u32[]{:S(2)}) %all-to-all-start.2) | async-done | bytes 655392 | tf_op jit(solution)/shard_map/all_to_all | solution.py:491
  60.7 1.6 %shard_map.125 = (bf16[8,144,128]{2,1,0:T(8,128)(2,1)}, bf16[128,1024]{1,0:T(8,128)(2,1)S(1)}, f32[16,128]{1,0:T(8,128)S(1)}) custom-call(bf16[32,80,128]{2,1,0:T(8,128)(2,1)S(1)} %all-to-all-done.2.arrived, f32[8,1024]{1,0:T(8,128)S(1)} %get-tuple-element.70.places, f32[64,1024]{1,0:T(8,128)S(1)} %get-tuple-element.77.local, ...), custom_call_target="tpu_custom_call" | custom-call | tf_op jit(solution)/shard_map/pallas_call | solution.py:577
  62.3 4.4 %all-to-all-start.3 = ((bf16[8,144,128]{2,1,0:T(8,128)(2,1)}), bf16[8,144,128]{2,1,0:T(8,128)(2,1)S(1)}, u32[]{:S(2)}, u32[]{:S(2)}) async-start(bf16[8,144,128]{2,1,0:T(8,128)(2,1)} %get-tuple-element.83), calls=%async_computation.3 | async-start | bytes 589824 | tf_op jit(solution)/shard_map/all_to_all | solution.py:491
  68.5 1.1 %collective-permute-start.6 = (f32[64,256]{1,0:T(8,128)S(1)}, f32[64,256]{1,0:T(8,128)S(1)}, u32[]{:S(2)}, u32[]{:S(2)}) collective-permute-start(f32[64,256]{1,0:T(8,128)S(1)} %add.21), channel_id=1, source_target_pairs={{0,16},{8,24},{16,0},{24,8},{32,48},{40,56},{48,32},{56,40},{64,80... | collective-permute-start | bytes 196616 | tf_op jit(solution)/shard_map/ppermute | solution.py:495
  69.6 2.4 %collective-permute-start.7 = (f32[64,256]{1,0:T(8,128)S(1)}, f32[64,256]{1,0:T(8,128)S(1)}, u32[]{:S(2)}, u32[]{:S(2)}) collective-permute-start(f32[64,256]{1,0:T(8,128)S(1)} %add.21), channel_id=1, source_target_pairs={{0,32},{8,40},{16,48},{24,56},{32,0},{40,8},{48,16},{56,24},{64,96... | collective-permute-start | bytes 196616 | tf_op jit(solution)/shard_map/ppermute | solution.py:495
  72.0 1.3 %collective-permute-start.8 = (f32[64,256]{1,0:T(8,128)S(1)}, f32[64,256]{1,0:T(8,128)S(1)}, u32[]{:S(2)}, u32[]{:S(2)}) collective-permute-start(f32[64,256]{1,0:T(8,128)S(1)} %add.21), channel_id=1, source_target_pairs={{0,48},{8,56},{16,32},{24,40},{32,16},{40,24},{48,0},{56,8},{64,11... | collective-permute-start | bytes 196616 | tf_op jit(solution)/shard_map/ppermute | solution.py:495
  73.3 2.4 %collective-permute-done.7 = f32[64,256]{1,0:T(8,128)S(1)} collective-permute-done((f32[64,256]{1,0:T(8,128)S(1)}, f32[64,256]{1,0:T(8,128)S(1)}, u32[]{:S(2)}, u32[]{:S(2)}) %collective-permute-start.7) | collective-permute-done | bytes 65568 | tf_op jit(solution)/shard_map/ppermute | solution.py:495
  75.6 1.8 %collective-permute-done.8 = f32[64,256]{1,0:T(8,128)S(1)} collective-permute-done((f32[64,256]{1,0:T(8,128)S(1)}, f32[64,256]{1,0:T(8,128)S(1)}, u32[]{:S(2)}, u32[]{:S(2)}) %collective-permute-start.8) | collective-permute-done | bytes 65568 | tf_op jit(solution)/shard_map/ppermute | solution.py:495
  77.5 2.7 %all-to-all-done.3.rows = bf16[8,144,128]{2,1,0:T(8,128)(2,1)S(1)} async-done(((bf16[8,144,128]{2,1,0:T(8,128)(2,1)}), bf16[8,144,128]{2,1,0:T(8,128)(2,1)S(1)}, u32[]{:S(2)}, u32[]{:S(2)}) %all-to-all-start.3) | async-done | bytes 294944 | tf_op jit(solution)/shard_map/all_to_all | solution.py:491
  80.2 1.4 %shard_map.127 = (bf16[8,96,128]{2,1,0:T(8,128)(2,1)}, f32[32,128]{1,0:T(8,128)S(1)}) custom-call(s32[1]{0:T(128)} %bitcast.1.head, s32[1]{0:T(128)S(6)} %and.10.group, bf16[8,144,128]{2,1,0:T(8,128)(2,1)S(1)} %all-to-all-done.3.rows, bf16[256,256]{1,0:T(8,128)(2,1)S(1)} %pad_maximum_fusion.weights0, bf16[128,256]{1,0:T(8,128)(2,1)S(1)} %collective-permute-done.1.weights2, ...), custom_call_target="tpu_custom_call" | custom-call | tf_op jit(solution)/shard_map/pallas_call | solution.py:596
  81.6 1.5 %collective-permute-start.10 = (f32[64,256]{1,0:T(8,128)S(1)}, f32[64,256]{1,0:T(8,128)S(1)}, u32[]{:S(2)}, u32[]{:S(2)}) collective-permute-start(f32[64,256]{1,0:T(8,128)S(1)} %add_add_fusion.1), channel_id=1, source_target_pairs={{0,128},{8,136},{16,144},{24,152},{32,160},{40,168},{48,176},{56,1... | collective-permute-start | bytes 196616 | tf_op jit(solution)/shard_map/ppermute | solution.py:495
  83.1 1.9 %collective-permute-start.11 = (f32[64,256]{1,0:T(8,128)S(1)}, f32[64,256]{1,0:T(8,128)S(1)}, u32[]{:S(2)}, u32[]{:S(2)}) collective-permute-start(f32[64,256]{1,0:T(8,128)S(1)} %add_add_fusion.1), channel_id=1, source_target_pairs={{0,192},{8,200},{16,208},{24,216},{32,224},{40,232},{48,240},{56,2... | collective-permute-start | bytes 196616 | tf_op jit(solution)/shard_map/ppermute | solution.py:495
  85.0 1.4 %collective-permute-start.9 = (f32[64,256]{1,0:T(8,128)S(1)}, f32[64,256]{1,0:T(8,128)S(1)}, u32[]{:S(2)}, u32[]{:S(2)}) collective-permute-start(f32[64,256]{1,0:T(8,128)S(1)} %add_add_fusion.1), channel_id=1, source_target_pairs={{0,64},{8,72},{16,80},{24,88},{32,96},{40,104},{48,112},{56,120},{... | collective-permute-start | bytes 196616 | tf_op jit(solution)/shard_map/ppermute | solution.py:495
  86.4 4.5 %all-to-all-start.4 = ((bf16[8,96,128]{2,1,0:T(8,128)(2,1)}), bf16[8,96,128]{2,1,0:T(8,128)(2,1)S(1)}, u32[]{:S(2)}, u32[]{:S(2)}) async-start(bf16[8,96,128]{2,1,0:T(8,128)(2,1)} %get-tuple-element.97), calls=%async_computation.4 | async-start | bytes 393216 | tf_op jit(solution)/shard_map/all_to_all | solution.py:491
  91.6 1.4 %collective-permute-start.15 = (f32[32,128]{1,0:T(8,128)S(1)}, f32[32,128]{1,0:T(8,128)S(1)}, u32[]{:S(2)}, u32[]{:S(2)}) collective-permute-start(f32[32,128]{1,0:T(8,128)S(1)} %get-tuple-element.99.virt0), channel_id=1, source_target_pairs={{0,24},{8,16},{16,8},{24,0},{32,56},{40,48},{48,40},{56,32},{64,88... | collective-permute-start | bytes 49160 | tf_op jit(solution)/shard_map/ppermute | solution.py:495
  93.1 2.3 %collective-permute-done.14.virt2 = f32[32,128]{1,0:T(8,128)S(1)} collective-permute-done((f32[32,128]{1,0:T(8,128)S(1)}, f32[32,128]{1,0:T(8,128)S(1)}, u32[]{:S(2)}, u32[]{:S(2)}) %collective-permute-start.14) | collective-permute-done | bytes 16416 | tf_op jit(solution)/shard_map/ppermute | solution.py:495
  95.4 5.4 %all-to-all-done.4.columns = bf16[8,96,128]{2,1,0:T(8,128)(2,1)S(1)} async-done(((bf16[8,96,128]{2,1,0:T(8,128)(2,1)}), bf16[8,96,128]{2,1,0:T(8,128)(2,1)S(1)}, u32[]{:S(2)}, u32[]{:S(2)}) %all-to-all-start.4) | async-done | bytes 196640 | tf_op jit(solution)/shard_map/all_to_all | solution.py:491
  (40 shorter events, 6.3 us)
Async XLA Ops:
  2.8 14.3 %all-to-all-start = ((f32[32,8,128]{2,1,0:T(8,128)}), f32[32,8,128]{2,1,0:T(8,128)S(1)}, u32[]{:S(2)}, u32[]{:S(2)}) async-start(f32[32,8,128]{2,1,0:T(8,128)} %shard_map.119), calls=%async_computation | async-start | bytes 262144 | tf_op jit(solution)/shard_map/all_to_all | solution.py:491
  10.5 1.0 %copy-start = (bf16[1024,256]{1,0:T(8,128)(2,1)S(1)}, bf16[1024,256]{1,0:T(8,128)(2,1)}, u32[]{:S(2)}) copy-start(bf16[1024,256]{1,0:T(8,128)(2,1)} %feats_at.3) | copy-start | bytes 1572868
  11.5 1.0 %copy-start.2 = (bf16[1024,256]{1,0:T(8,128)(2,1)S(1)}, bf16[1024,256]{1,0:T(8,128)(2,1)}, u32[]{:S(2)}) copy-start(bf16[1024,256]{1,0:T(8,128)(2,1)} %cotangent_at.3) | copy-start | bytes 1572868
  12.6 0.8 copy-start.4
  13.4 0.8 copy-start.5
  14.1 0.7 copy-start.6
  19.1 34.8 %copy-start.3 = (bf16[1024,256]{1,0:T(8,128)(2,1)S(1)}, bf16[1024,256]{1,0:T(8,128)(2,1)}, u32[]{:S(2)}) copy-start(bf16[1024,256]{1,0:T(8,128)(2,1)} %cotangent_at.3) | copy-start | bytes 1572868
  19.1 20.3 %all-to-all-start.1 = ((bf16[32,80,128]{2,1,0:T(8,128)(2,1)}), bf16[32,80,128]{2,1,0:T(8,128)(2,1)S(1)}, u32[]{:S(2)}, u32[]{:S(2)}) async-start(bf16[32,80,128]{2,1,0:T(8,128)(2,1)} %get-tuple-element.66), calls=%async_computation.1 | async-start | bytes 1310720 | tf_op jit(solution)/shard_map/all_to_all | solution.py:491
  25.0 12.0 %collective-permute-start = (bf16[128,256]{1,0:T(8,128)(2,1)S(1)}, bf16[128,256]{1,0:T(8,128)(2,1)S(1)}, u32[]{:S(2)}, u32[]{:S(2)}) collective-permute-start(bf16[128,256]{1,0:T(8,128)(2,1)S(1)} %get-tuple-element.81), channel_id=1, source_target_pairs={{0,4},{1,5},{2,6},{3,7},{4,0},{5,1},{6,2},{7,3},{8,12},{9,13},{10,... | collective-permute-start | bytes 196616 | tf_op jit(solution)/shard_map/ppermute | solution.py:495
  32.3 7.1 %collective-permute-start.1 = (bf16[128,256]{1,0:T(8,128)(2,1)S(1)}, bf16[128,256]{1,0:T(8,128)(2,1)S(1)}, u32[]{:S(2)}, u32[]{:S(2)}) collective-permute-start(bf16[128,256]{1,0:T(8,128)(2,1)S(1)} %get-tuple-element.81), channel_id=1, source_target_pairs={{2,0},{3,1},{4,2},{5,3},{6,4},{7,5},{0,6},{1,7},{10,8},{11,9},{12,... | collective-permute-start | bytes 196616 | tf_op jit(solution)/shard_map/ppermute | solution.py:499
  42.4 24.3 %copy-start.1 = (bf16[1024,256]{1,0:T(8,128)(2,1)S(1)}, bf16[1024,256]{1,0:T(8,128)(2,1)}, u32[]{:S(2)}) copy-start(bf16[1024,256]{1,0:T(8,128)(2,1)} %feats_at.3) | copy-start | bytes 1572868
  42.4 18.4 %all-to-all-start.2 = ((bf16[32,80,128]{2,1,0:T(8,128)(2,1)}), bf16[32,80,128]{2,1,0:T(8,128)(2,1)S(1)}, u32[]{:S(2)}, u32[]{:S(2)}) async-start(bf16[32,80,128]{2,1,0:T(8,128)(2,1)} %get-tuple-element.73), calls=%async_computation.2 | async-start | bytes 1310720 | tf_op jit(solution)/shard_map/all_to_all | solution.py:491
  49.9 12.4 %collective-permute-start.3 = (bf16[256,256]{1,0:T(8,128)(2,1)S(1)}, bf16[256,256]{1,0:T(8,128)(2,1)S(1)}, u32[]{:S(2)}, u32[]{:S(2)}) collective-permute-start(bf16[256,256]{1,0:T(8,128)(2,1)S(1)} %pad_maximum_fusion.weights0), channel_id=1, source_target_pairs={{1,0},{2,1},{3,2},{4,3},{5,4},{6,5},{7,6},{0,7},{9,8},{10,9},{11,1... | collective-permute-start | bytes 393224 | tf_op jit(solution)/shard_map/ppermute | solution.py:499
  52.9 9.4 %collective-permute-start.4 = (bf16[256,256]{1,0:T(8,128)(2,1)S(1)}, bf16[256,256]{1,0:T(8,128)(2,1)S(1)}, u32[]{:S(2)}, u32[]{:S(2)}) collective-permute-start(bf16[256,256]{1,0:T(8,128)(2,1)S(1)} %pad_maximum_fusion.weights0), channel_id=1, source_target_pairs={{7,0},{0,1},{1,2},{2,3},{3,4},{4,5},{5,6},{6,7},{15,8},{8,9},{9,10... | collective-permute-start | bytes 393224 | tf_op jit(solution)/shard_map/ppermute | solution.py:499
  52.9 9.3 %collective-permute-start.2 = (bf16[128,256]{1,0:T(8,128)(2,1)S(1)}, bf16[128,256]{1,0:T(8,128)(2,1)S(1)}, u32[]{:S(2)}, u32[]{:S(2)}) collective-permute-start(bf16[128,256]{1,0:T(8,128)(2,1)S(1)} %get-tuple-element.81), channel_id=1, source_target_pairs={{6,0},{7,1},{0,2},{1,3},{2,4},{3,5},{4,6},{5,7},{14,8},{15,9},{8,1... | collective-permute-start | bytes 196616 | tf_op jit(solution)/shard_map/ppermute | solution.py:499
  53.9 46.8 %copy-start.7 = (s32[1024]{0:T(1024)S(1)}, s32[1024]{0:T(1024)}, u32[]{:S(2)}) copy-start(s32[1024]{0:T(1024)} %param.12) | copy-start | bytes 12292
  62.3 17.9 %all-to-all-start.3 = ((bf16[8,144,128]{2,1,0:T(8,128)(2,1)}), bf16[8,144,128]{2,1,0:T(8,128)(2,1)S(1)}, u32[]{:S(2)}, u32[]{:S(2)}) async-start(bf16[8,144,128]{2,1,0:T(8,128)(2,1)} %get-tuple-element.83), calls=%async_computation.3 | async-start | bytes 589824 | tf_op jit(solution)/shard_map/all_to_all | solution.py:491
  67.0 1.5 %collective-permute-start.5 = (f32[64,256]{1,0:T(8,128)S(1)}, f32[64,256]{1,0:T(8,128)S(1)}, u32[]{:S(2)}, u32[]{:S(2)}) collective-permute-start(f32[64,256]{1,0:T(8,128)S(1)} %get-tuple-element.89), channel_id=1, source_target_pairs={{0,8},{8,0},{16,24},{24,16},{32,40},{40,32},{48,56},{56,48},{64,72... | collective-permute-start | bytes 196616 | tf_op jit(solution)/shard_map/ppermute | solution.py:495
  68.5 4.8 %collective-permute-start.6 = (f32[64,256]{1,0:T(8,128)S(1)}, f32[64,256]{1,0:T(8,128)S(1)}, u32[]{:S(2)}, u32[]{:S(2)}) collective-permute-start(f32[64,256]{1,0:T(8,128)S(1)} %add.21), channel_id=1, source_target_pairs={{0,16},{8,24},{16,0},{24,8},{32,48},{40,56},{48,32},{56,40},{64,80... | collective-permute-start | bytes 196616 | tf_op jit(solution)/shard_map/ppermute | solution.py:495
  69.6 6.1 %collective-permute-start.7 = (f32[64,256]{1,0:T(8,128)S(1)}, f32[64,256]{1,0:T(8,128)S(1)}, u32[]{:S(2)}, u32[]{:S(2)}) collective-permute-start(f32[64,256]{1,0:T(8,128)S(1)} %add.21), channel_id=1, source_target_pairs={{0,32},{8,40},{16,48},{24,56},{32,0},{40,8},{48,16},{56,24},{64,96... | collective-permute-start | bytes 196616 | tf_op jit(solution)/shard_map/ppermute | solution.py:495
  72.0 5.5 %collective-permute-start.8 = (f32[64,256]{1,0:T(8,128)S(1)}, f32[64,256]{1,0:T(8,128)S(1)}, u32[]{:S(2)}, u32[]{:S(2)}) collective-permute-start(f32[64,256]{1,0:T(8,128)S(1)} %add.21), channel_id=1, source_target_pairs={{0,48},{8,56},{16,32},{24,40},{32,16},{40,24},{48,0},{56,8},{64,11... | collective-permute-start | bytes 196616 | tf_op jit(solution)/shard_map/ppermute | solution.py:495
  81.6 9.3 %collective-permute-start.10 = (f32[64,256]{1,0:T(8,128)S(1)}, f32[64,256]{1,0:T(8,128)S(1)}, u32[]{:S(2)}, u32[]{:S(2)}) collective-permute-start(f32[64,256]{1,0:T(8,128)S(1)} %add_add_fusion.1), channel_id=1, source_target_pairs={{0,128},{8,136},{16,144},{24,152},{32,160},{40,168},{48,176},{56,1... | collective-permute-start | bytes 196616 | tf_op jit(solution)/shard_map/ppermute | solution.py:495
  83.1 7.8 %collective-permute-start.11 = (f32[64,256]{1,0:T(8,128)S(1)}, f32[64,256]{1,0:T(8,128)S(1)}, u32[]{:S(2)}, u32[]{:S(2)}) collective-permute-start(f32[64,256]{1,0:T(8,128)S(1)} %add_add_fusion.1), channel_id=1, source_target_pairs={{0,192},{8,200},{16,208},{24,216},{32,224},{40,232},{48,240},{56,2... | collective-permute-start | bytes 196616 | tf_op jit(solution)/shard_map/ppermute | solution.py:495
  85.0 6.0 %collective-permute-start.9 = (f32[64,256]{1,0:T(8,128)S(1)}, f32[64,256]{1,0:T(8,128)S(1)}, u32[]{:S(2)}, u32[]{:S(2)}) collective-permute-start(f32[64,256]{1,0:T(8,128)S(1)} %add_add_fusion.1), channel_id=1, source_target_pairs={{0,64},{8,72},{16,80},{24,88},{32,96},{40,104},{48,112},{56,120},{... | collective-permute-start | bytes 196616 | tf_op jit(solution)/shard_map/ppermute | solution.py:495
  86.4 14.3 %all-to-all-start.4 = ((bf16[8,96,128]{2,1,0:T(8,128)(2,1)}), bf16[8,96,128]{2,1,0:T(8,128)(2,1)S(1)}, u32[]{:S(2)}, u32[]{:S(2)}) async-start(bf16[8,96,128]{2,1,0:T(8,128)(2,1)} %get-tuple-element.97), calls=%async_computation.4 | async-start | bytes 393216 | tf_op jit(solution)/shard_map/all_to_all | solution.py:491
  91.0 4.3 %collective-permute-start.12 = (f32[64,256]{1,0:T(8,128)S(1)}, f32[64,256]{1,0:T(8,128)S(1)}, u32[]{:S(2)}, u32[]{:S(2)}) collective-permute-start(f32[64,256]{1,0:T(8,128)S(1)} %add_add_fusion.near), channel_id=1, source_target_pairs={{0,8},{8,0},{16,24},{24,16},{32,40},{40,32},{48,56},{56,48},{64,72... | collective-permute-start | bytes 196616 | tf_op jit(solution)/shard_map/ppermute | solution.py:495
  91.1 2.0 %collective-permute-start.13 = (f32[32,128]{1,0:T(8,128)S(1)}, f32[32,128]{1,0:T(8,128)S(1)}, u32[]{:S(2)}, u32[]{:S(2)}) collective-permute-start(f32[32,128]{1,0:T(8,128)S(1)} %get-tuple-element.99.virt0), channel_id=1, source_target_pairs={{0,8},{8,0},{16,24},{24,16},{32,40},{40,32},{48,56},{56,48},{64,72... | collective-permute-start | bytes 49160 | tf_op jit(solution)/shard_map/ppermute | solution.py:495
  91.6 3.7 %collective-permute-start.14 = (f32[32,128]{1,0:T(8,128)S(1)}, f32[32,128]{1,0:T(8,128)S(1)}, u32[]{:S(2)}, u32[]{:S(2)}) collective-permute-start(f32[32,128]{1,0:T(8,128)S(1)} %get-tuple-element.99.virt0), channel_id=1, source_target_pairs={{0,16},{8,24},{16,0},{24,8},{32,48},{40,56},{48,32},{56,40},{64,80... | collective-permute-start | bytes 49160 | tf_op jit(solution)/shard_map/ppermute | solution.py:495
  91.6 3.7 %collective-permute-start.15 = (f32[32,128]{1,0:T(8,128)S(1)}, f32[32,128]{1,0:T(8,128)S(1)}, u32[]{:S(2)}, u32[]{:S(2)}) collective-permute-start(f32[32,128]{1,0:T(8,128)S(1)} %get-tuple-element.99.virt0), channel_id=1, source_target_pairs={{0,24},{8,16},{16,8},{24,0},{32,56},{40,48},{48,40},{56,32},{64,88... | collective-permute-start | bytes 49160 | tf_op jit(solution)/shard_map/ppermute | solution.py:495

commit v5 on v3

--- a/solution.py
+++ b/solution.py
@@ -448,11 +448,11 @@
 
 
 def finish_kernel(
-    core, columns, near, far, virt0, virt1, virt2, virt3, member,
+    core, columns, both, virt0, virt1, virt2, virt3, member,
     mixed, grad_feats, grad_qkv, grad_out, grad_virtual, held,
 ):
-    held[core[0]] = near[...]
-    held[1 - core[0]] = far[...]
+    held[core[0]] = both[0:64, :]
+    held[1 - core[0]] = both[64:128, :]
     grad_qkv[0:64, :] = held[0]
     grad_qkv[64:96, :] = held[1, 0:32, :]
     grad_out[...] = held[1, 32:64, :]
@@ -603,13 +603,13 @@
             pltpu.SemaphoreType.DMA((2,)),
         ],
     )(head, slab & 3, rows, two, *others, feats, cotangent)
-    columns, keep = lax.optimization_barrier([columns, keep])
     columns = exchange(columns, "head")
-    keep = (keep + swap(keep, "dom", 8)) + (swap(keep, "dom", 16) + swap(keep, "dom", 24))
+    both = jnp.concatenate([keep, swap(keep, "dom", 1)], axis=0)
+    both = (both + swap(both, "dom", 8)) + (swap(both, "dom", 16) + swap(both, "dom", 24))
     virts = [virt] + [swap(virt, "dom", k) for k in (1, 2, 3)]
     mixed, grad_feats, grad_qkv, grad_out, grad_virtual = call(
         finish_kernel,
-        [SMEM] + [VMEM] * 8,
+        [SMEM] + [VMEM] * 7,
         (
             array((32, ROWS), bf16),
             array((32, ROWS), bf16),
@@ -618,7 +618,7 @@
             array((32, VIRT), f32),
         ),
         scratch=[pltpu.VMEM((2, 64, WIDTH), f32)],
-    )(slab & 1, columns, keep, swap(keep, "dom", 1), *virts, members)
+    )(slab & 1, columns, both, *virts, members)
     grad_qkv = jnp.transpose(grad_qkv.reshape(3, 32, WIDTH), (0, 2, 1))
     return (mixed.T, grad_feats.T, grad_qkv, grad_out, grad_virtual.T)
 

time: 102 us -> 103 us (level)
  the two profiles are of different devices: /device:TPU:2 before, /device:TPU:6 now
where the time goes in v5:
time: 103 us
  starting transfers between devices  57.3 us (56%)
  Pallas kernels  21.4 us (21%)
  waiting for transfers between devices  18.6 us (18%)
  local copies, waits for them, and re-layouts  4.37 us (4%)
    all_to_all x5, starting transfers between devices, exchange(): return lax.all_to_all(x, axis, split_axis=0, concat_axis=0, tiled=True)  32.5 us
    ppermute x12, starting transfers between devices, swap(): lax.ppermute(x, axis, [(i, i ^ k) for i in range(lax.axis_size(axis))])  18.7 us
    ppermute x12, waiting for transfers between devices, swap(): lax.ppermute(x, axis, [(i, i ^ k) for i in range(lax.axis_size(axis))])  9.35 us
    all_to_all x5, waiting for transfers between devices, exchange(): return lax.all_to_all(x, axis, split_axis=0, concat_axis=0, tiled=True)  8.49 us
    ppermute x4, starting transfers between devices, shift(): return lax.ppermute(x, 'head', [((h + k) % HEADS, h) for h in range(HEADS)])  6.04 us
    pallas_call x1, Pallas kernels, shards(): pl.pallas_call(local_kernel, grid=(ROWS // TI,), out_shape=array((8, ROWS...  4.78 us
    pallas_call x1, Pallas kernels, shards(): call(attend_kernel, [VMEM] * 6 + [HBM] * 2, (array((64, ROWS), f32), arra...  4.61 us
    unnamed x17, local copies, waits for them, and re-layouts  4.37 us
  transfers between devices with their start and end apart: 21, of which 9 were waited for; matrix products, arithmetic and copies ran while one was open for 0% of the time, Pallas kernels for 13%

profile of v5, /device:TPU:6, one launch (start us, length us, event | category | flops | bytes accessed | tf_op | source)
XLA Modules:
  0.0 102.6 jit_solution(12599900864417686590)
XLA Ops:
  0.6 2.2 %shard_map.119 = f32[32,8,128]{2,1,0:T(8,128)} custom-call(bf16[1024,256]{1,0:T(8,128)(2,1)} %feats_at.3, s32[1,1024]{1,0:T(1,128)} %bitcast.12, s32[2,1024]{1,0:T(2,128)} %bitcast.14), custom_call_target="tpu_custom_call" | custom-call | tf_op jit(solution)/shard_map/pallas_call | solution.py:506
  2.8 7.6 %all-to-all-start = ((f32[32,8,128]{2,1,0:T(8,128)}), f32[32,8,128]{2,1,0:T(8,128)S(1)}, u32[]{:S(2)}, u32[]{:S(2)}) async-start(f32[32,8,128]{2,1,0:T(8,128)} %shard_map.119), calls=%async_computation | async-start | bytes 262144 | tf_op jit(solution)/shard_map/all_to_all | solution.py:491
  10.5 1.0 %copy-done = bf16[1024,256]{1,0:T(8,128)(2,1)S(1)} copy-done((bf16[1024,256]{1,0:T(8,128)(2,1)S(1)}, bf16[1024,256]{1,0:T(8,128)(2,1)}, u32[]{:S(2)}) %copy-start) | copy-done | bytes 524312
  11.5 1.0 %copy-done.2 = bf16[1024,256]{1,0:T(8,128)(2,1)S(1)} copy-done((bf16[1024,256]{1,0:T(8,128)(2,1)S(1)}, bf16[1024,256]{1,0:T(8,128)(2,1)}, u32[]{:S(2)}) %copy-start.2) | copy-done | bytes 524312
  12.5 0.8 copy-done.4
  15.5 0.9 all-to-all-done.arrived
  16.4 2.0 %shard_map.121 = (bf16[32,80,128]{2,1,0:T(8,128)(2,1)}, f32[8,1024]{1,0:T(8,128)S(1)}, bf16[128,256]{1,0:T(8,128)(2,1)S(1)}) custom-call(s32[1]{0:T(128)} %bitcast.slab, f32[32,8,128]{2,1,0:T(8,128)S(1)} %all-to-all-done.arrived, bf16[1024,128]{1,0:T(8,128)(2,1)S(1)} %get-tuple-element.55.table, bf16[64,1024]{1,0:T(8,128)(2,1)S(1)} %get-tuple-element.56.table_t, ...), custom_call_target="tpu_custom_call" | custom-call | tf_op jit(solution)/shard_map/pallas_call | solution.py:533
  18.4 6.6 %all-to-all-start.1 = ((bf16[32,80,128]{2,1,0:T(8,128)(2,1)}), bf16[32,80,128]{2,1,0:T(8,128)(2,1)S(1)}, u32[]{:S(2)}, u32[]{:S(2)}) async-start(bf16[32,80,128]{2,1,0:T(8,128)(2,1)} %get-tuple-element.64), calls=%async_computation.1 | async-start | bytes 1310720 | tf_op jit(solution)/shard_map/all_to_all | solution.py:491
  25.0 7.3 %collective-permute-start = (bf16[128,256]{1,0:T(8,128)(2,1)S(1)}, bf16[128,256]{1,0:T(8,128)(2,1)S(1)}, u32[]{:S(2)}, u32[]{:S(2)}) collective-permute-start(bf16[128,256]{1,0:T(8,128)(2,1)S(1)} %get-tuple-element.79), channel_id=1, source_target_pairs={{0,4},{1,5},{2,6},{3,7},{4,0},{5,1},{6,2},{7,3},{8,12},{9,13},{10,... | collective-permute-start | bytes 196616 | tf_op jit(solution)/shard_map/ppermute | solution.py:495
  32.3 4.8 %shard_map.122.stats = f32[8,1024]{1,0:T(8,128)S(1)} custom-call(bf16[32,1024]{1,0:T(8,128)(2,1)S(1)} %get-tuple-element.62.query_t, bf16[32,1024]{1,0:T(8,128)(2,1)S(1)} %get-tuple-element.63.grad_t, s32[1024,1024]{1,0:T(8,128)} %mask_at.1, bf16[64,1024]{1,0:T(8,128)(2,1)S(1)} %get-tuple-element.56.table_t), custom_call_target="tpu_custom_call" | custom-call | tf_op jit(solution)/shard_map/pallas_call | solution.py:542
  37.1 3.0 %shard_map.123 = (bf16[32,80,128]{2,1,0:T(8,128)(2,1)}, f32[8,1024]{1,0:T(8,128)S(1)}, f32[32,1024]{1,0:T(8,128)S(1)}, f32[32,1024]{1,0:T(8,128)S(1)}) custom-call(bf16[32,1024]{1,0:T(8,128)(2,1)S(1)} %get-tuple-element.62.query_t, bf16[32,1024]{1,0:T(8,128)(2,1)S(1)} %get-tuple-element.63.grad_t, f32[8,1024]{1,0:T(8,128)S(1)} %shard_map.122.stats, ...), custom_call_target="tpu_custom_call" | custom-call | tf_op jit(solution)/shard_map/pallas_call | solution.py:551
  40.1 7.5 %all-to-all-start.2 = ((bf16[32,80,128]{2,1,0:T(8,128)(2,1)}), bf16[32,80,128]{2,1,0:T(8,128)(2,1)S(1)}, u32[]{:S(2)}, u32[]{:S(2)}) async-start(bf16[32,80,128]{2,1,0:T(8,128)(2,1)} %get-tuple-element.71), calls=%async_computation.2 | async-start | bytes 1310720 | tf_op jit(solution)/shard_map/all_to_all | solution.py:491
  47.6 3.1 %collective-permute-start.3 = (bf16[256,256]{1,0:T(8,128)(2,1)S(1)}, bf16[256,256]{1,0:T(8,128)(2,1)S(1)}, u32[]{:S(2)}, u32[]{:S(2)}) collective-permute-start(bf16[256,256]{1,0:T(8,128)(2,1)S(1)} %pad_maximum_fusion.weights0), channel_id=1, source_target_pairs={{1,0},{2,1},{3,2},{4,3},{5,4},{6,5},{7,6},{0,7},{9,8},{10,9},{11,1... | collective-permute-start | bytes 393224 | tf_op jit(solution)/shard_map/ppermute | solution.py:499
  50.7 2.7 %collective-permute-start.1 = (bf16[128,256]{1,0:T(8,128)(2,1)S(1)}, bf16[128,256]{1,0:T(8,128)(2,1)S(1)}, u32[]{:S(2)}, u32[]{:S(2)}) collective-permute-start(bf16[128,256]{1,0:T(8,128)(2,1)S(1)} %get-tuple-element.79), channel_id=1, source_target_pairs={{2,0},{3,1},{4,2},{5,3},{6,4},{7,5},{0,6},{1,7},{10,8},{11,9},{12,... | collective-permute-start | bytes 196616 | tf_op jit(solution)/shard_map/ppermute | solution.py:499
  53.6 4.6 %shard_map.124 = (f32[64,1024]{1,0:T(8,128)S(1)}, bf16[64,1024]{1,0:T(8,128)(2,1)S(1)}, f32[32,256]{1,0:T(8,128)S(1)}) custom-call(f32[8,1024]{1,0:T(8,128)S(1)} %get-tuple-element.72.parts, f32[32,1024]{1,0:T(8,128)S(1)} %get-tuple-element.73.attended, f32[32,1024]{1,0:T(8,128)S(1)} %get-tuple-element.74.grad_query, ...), custom_call_target="tpu_custom_call" | custom-call | tf_op jit(solution)/shard_map/pallas_call | solution.py:562
  58.3 1.6 %shard_map.125 = (bf16[8,144,128]{2,1,0:T(8,128)(2,1)}, bf16[128,1024]{1,0:T(8,128)(2,1)S(1)}, f32[16,128]{1,0:T(8,128)S(1)}) custom-call(bf16[32,80,128]{2,1,0:T(8,128)(2,1)S(1)} %all-to-all-done.2.arrived, f32[8,1024]{1,0:T(8,128)S(1)} %get-tuple-element.68.places, f32[64,1024]{1,0:T(8,128)S(1)} %get-tuple-element.75.local, ...), custom_call_target="tpu_custom_call" | custom-call | tf_op jit(solution)/shard_map/pallas_call | solution.py:576
  60.6 4.9 %all-to-all-start.3 = ((bf16[8,144,128]{2,1,0:T(8,128)(2,1)}), bf16[8,144,128]{2,1,0:T(8,128)(2,1)S(1)}, u32[]{:S(2)}, u32[]{:S(2)}) async-start(bf16[8,144,128]{2,1,0:T(8,128)(2,1)} %get-tuple-element.81), calls=%async_computation.3 | async-start | bytes 589824 | tf_op jit(solution)/shard_map/all_to_all | solution.py:491
  66.0 1.2 %collective-permute-done.5 = f32[64,256]{1,0:T(8,128)S(1)} collective-permute-done((f32[64,256]{1,0:T(8,128)S(1)}, f32[64,256]{1,0:T(8,128)S(1)}, u32[]{:S(2)}, u32[]{:S(2)}) %collective-permute-start.5) | collective-permute-done | bytes 65568 | tf_op jit(solution)/shard_map/ppermute | solution.py:495
  67.3 1.6 %collective-permute-start.6 = (f32[64,256]{1,0:T(8,128)S(1)}, f32[64,256]{1,0:T(8,128)S(1)}, u32[]{:S(2)}, u32[]{:S(2)}) collective-permute-start(f32[64,256]{1,0:T(8,128)S(1)} %add.21), channel_id=1, source_target_pairs={{0,16},{8,24},{16,0},{24,8},{32,48},{40,56},{48,32},{56,40},{64,80... | collective-permute-start | bytes 196616 | tf_op jit(solution)/shard_map/ppermute | solution.py:495
  68.8 2.7 %collective-permute-start.7 = (f32[64,256]{1,0:T(8,128)S(1)}, f32[64,256]{1,0:T(8,128)S(1)}, u32[]{:S(2)}, u32[]{:S(2)}) collective-permute-start(f32[64,256]{1,0:T(8,128)S(1)} %add.21), channel_id=1, source_target_pairs={{0,32},{8,40},{16,48},{24,56},{32,0},{40,8},{48,16},{56,24},{64,96... | collective-permute-start | bytes 196616 | tf_op jit(solution)/shard_map/ppermute | solution.py:495
  72.1 3.0 %collective-permute-done.7 = f32[64,256]{1,0:T(8,128)S(1)} collective-permute-done((f32[64,256]{1,0:T(8,128)S(1)}, f32[64,256]{1,0:T(8,128)S(1)}, u32[]{:S(2)}, u32[]{:S(2)}) %collective-permute-start.7) | collective-permute-done | bytes 65568 | tf_op jit(solution)/shard_map/ppermute | solution.py:495
  75.1 1.9 %collective-permute-done.8 = f32[64,256]{1,0:T(8,128)S(1)} collective-permute-done((f32[64,256]{1,0:T(8,128)S(1)}, f32[64,256]{1,0:T(8,128)S(1)}, u32[]{:S(2)}, u32[]{:S(2)}) %collective-permute-start.8) | collective-permute-done | bytes 65568 | tf_op jit(solution)/shard_map/ppermute | solution.py:495
  77.0 1.5 %all-to-all-done.3.rows = bf16[8,144,128]{2,1,0:T(8,128)(2,1)S(1)} async-done(((bf16[8,144,128]{2,1,0:T(8,128)(2,1)}), bf16[8,144,128]{2,1,0:T(8,128)(2,1)S(1)}, u32[]{:S(2)}, u32[]{:S(2)}) %all-to-all-start.3) | async-done | bytes 294944 | tf_op jit(solution)/shard_map/all_to_all | solution.py:491
  78.5 1.2 %collective-permute-done.9 = f32[64,256]{1,0:T(8,128)S(1)} collective-permute-done((f32[64,256]{1,0:T(8,128)S(1)}, f32[64,256]{1,0:T(8,128)S(1)}, u32[]{:S(2)}, u32[]{:S(2)}) %collective-permute-start.9) | collective-permute-done | bytes 65568 | tf_op jit(solution)/shard_map/ppermute | solution.py:495
  79.8 1.2 %collective-permute-start.10 = (f32[128,256]{1,0:T(8,128)S(1)}, f32[128,256]{1,0:T(8,128)S(1)}, u32[]{:S(2)}, u32[]{:S(2)}) collective-permute-start(f32[128,256]{1,0:T(8,128)S(1)} %constant_dynamic-update-slice_fusion), channel_id=1, source_target_pairs={{0,64},{8,72},{16,80},{24,88},{32,96},{40,104},{48,112},{56,120},{... | collective-permute-start | bytes 393224 | tf_op jit(solution)/shard_map/ppermute | solution.py:495
  81.0 2.7 %collective-permute-start.11 = (f32[128,256]{1,0:T(8,128)S(1)}, f32[128,256]{1,0:T(8,128)S(1)}, u32[]{:S(2)}, u32[]{:S(2)}) collective-permute-start(f32[128,256]{1,0:T(8,128)S(1)} %constant_dynamic-update-slice_fusion), channel_id=1, source_target_pairs={{0,128},{8,136},{16,144},{24,152},{32,160},{40,168},{48,176},{56,1... | collective-permute-start | bytes 393224 | tf_op jit(solution)/shard_map/ppermute | solution.py:495
  84.5 1.4 %shard_map.127 = (bf16[8,96,128]{2,1,0:T(8,128)(2,1)}, f32[32,128]{1,0:T(8,128)S(1)}) custom-call(s32[1]{0:T(128)} %bitcast.1.head, s32[1]{0:T(128)S(6)} %and.10.group, bf16[8,144,128]{2,1,0:T(8,128)(2,1)S(1)} %all-to-all-done.3.rows, bf16[256,256]{1,0:T(8,128)(2,1)S(1)} %pad_maximum_fusion.weights0, bf16[128,256]{1,0:T(8,128)(2,1)S(1)} %collective-permute-done.1.weights2, ...), custom_call_target="tpu_custom_call" | custom-call | tf_op jit(solution)/shard_map/pallas_call | solution.py:595
  85.9 5.8 %all-to-all-start.4 = ((bf16[8,96,128]{2,1,0:T(8,128)(2,1)}), bf16[8,96,128]{2,1,0:T(8,128)(2,1)S(1)}, u32[]{:S(2)}, u32[]{:S(2)}) async-start(bf16[8,96,128]{2,1,0:T(8,128)(2,1)} %get-tuple-element.93), calls=%async_computation.4 | async-start | bytes 393216 | tf_op jit(solution)/shard_map/all_to_all | solution.py:491
  91.9 1.8 %collective-permute-start.15 = (f32[32,128]{1,0:T(8,128)S(1)}, f32[32,128]{1,0:T(8,128)S(1)}, u32[]{:S(2)}, u32[]{:S(2)}) collective-permute-start(f32[32,128]{1,0:T(8,128)S(1)} %get-tuple-element.95.virt0), channel_id=1, source_target_pairs={{0,24},{8,16},{16,8},{24,0},{32,56},{40,48},{48,40},{56,32},{64,88... | collective-permute-start | bytes 49160 | tf_op jit(solution)/shard_map/ppermute | solution.py:495
  93.7 1.9 %collective-permute-done.14.virt2 = f32[32,128]{1,0:T(8,128)S(1)} collective-permute-done((f32[32,128]{1,0:T(8,128)S(1)}, f32[32,128]{1,0:T(8,128)S(1)}, u32[]{:S(2)}, u32[]{:S(2)}) %collective-permute-start.14) | collective-permute-done | bytes 16416 | tf_op jit(solution)/shard_map/ppermute | solution.py:495
  95.6 6.1 %all-to-all-done.4.columns = bf16[8,96,128]{2,1,0:T(8,128)(2,1)S(1)} async-done(((bf16[8,96,128]{2,1,0:T(8,128)(2,1)}), bf16[8,96,128]{2,1,0:T(8,128)(2,1)S(1)}, u32[]{:S(2)}, u32[]{:S(2)}) %all-to-all-start.4) | async-done | bytes 196640 | tf_op jit(solution)/shard_map/all_to_all | solution.py:491
  101.7 0.9 shard_map.128
  (42 shorter events, 5.1 us)
Async XLA Ops:
  2.8 13.6 %all-to-all-start = ((f32[32,8,128]{2,1,0:T(8,128)}), f32[32,8,128]{2,1,0:T(8,128)S(1)}, u32[]{:S(2)}, u32[]{:S(2)}) async-start(f32[32,8,128]{2,1,0:T(8,128)} %shard_map.119), calls=%async_computation | async-start | bytes 262144 | tf_op jit(solution)/shard_map/all_to_all | solution.py:491
  10.5 1.0 %copy-start = (bf16[1024,256]{1,0:T(8,128)(2,1)S(1)}, bf16[1024,256]{1,0:T(8,128)(2,1)}, u32[]{:S(2)}) copy-start(bf16[1024,256]{1,0:T(8,128)(2,1)} %feats_at.3) | copy-start | bytes 1572868
  11.5 1.0 %copy-start.2 = (bf16[1024,256]{1,0:T(8,128)(2,1)S(1)}, bf16[1024,256]{1,0:T(8,128)(2,1)}, u32[]{:S(2)}) copy-start(bf16[1024,256]{1,0:T(8,128)(2,1)} %cotangent_at.3) | copy-start | bytes 1572868
  12.5 0.8 copy-start.4
  13.3 0.8 copy-start.5
  14.1 0.7 copy-start.6
  18.4 35.3 %copy-start.3 = (bf16[1024,256]{1,0:T(8,128)(2,1)S(1)}, bf16[1024,256]{1,0:T(8,128)(2,1)}, u32[]{:S(2)}) copy-start(bf16[1024,256]{1,0:T(8,128)(2,1)} %cotangent_at.3) | copy-start | bytes 1572868
  18.4 18.7 %all-to-all-start.1 = ((bf16[32,80,128]{2,1,0:T(8,128)(2,1)}), bf16[32,80,128]{2,1,0:T(8,128)(2,1)S(1)}, u32[]{:S(2)}, u32[]{:S(2)}) async-start(bf16[32,80,128]{2,1,0:T(8,128)(2,1)} %get-tuple-element.64), calls=%async_computation.1 | async-start | bytes 1310720 | tf_op jit(solution)/shard_map/all_to_all | solution.py:491
  25.0 12.1 %collective-permute-start = (bf16[128,256]{1,0:T(8,128)(2,1)S(1)}, bf16[128,256]{1,0:T(8,128)(2,1)S(1)}, u32[]{:S(2)}, u32[]{:S(2)}) collective-permute-start(bf16[128,256]{1,0:T(8,128)(2,1)S(1)} %get-tuple-element.79), channel_id=1, source_target_pairs={{0,4},{1,5},{2,6},{3,7},{4,0},{5,1},{6,2},{7,3},{8,12},{9,13},{10,... | collective-permute-start | bytes 196616 | tf_op jit(solution)/shard_map/ppermute | solution.py:495
  40.1 25.5 %copy-start.1 = (bf16[1024,256]{1,0:T(8,128)(2,1)S(1)}, bf16[1024,256]{1,0:T(8,128)(2,1)}, u32[]{:S(2)}) copy-start(bf16[1024,256]{1,0:T(8,128)(2,1)} %feats_at.3) | copy-start | bytes 1572868
  40.1 18.2 %all-to-all-start.2 = ((bf16[32,80,128]{2,1,0:T(8,128)(2,1)}), bf16[32,80,128]{2,1,0:T(8,128)(2,1)S(1)}, u32[]{:S(2)}, u32[]{:S(2)}) async-start(bf16[32,80,128]{2,1,0:T(8,128)(2,1)} %get-tuple-element.71), calls=%async_computation.2 | async-start | bytes 1310720 | tf_op jit(solution)/shard_map/all_to_all | solution.py:491
  47.6 13.1 %collective-permute-start.3 = (bf16[256,256]{1,0:T(8,128)(2,1)S(1)}, bf16[256,256]{1,0:T(8,128)(2,1)S(1)}, u32[]{:S(2)}, u32[]{:S(2)}) collective-permute-start(bf16[256,256]{1,0:T(8,128)(2,1)S(1)} %pad_maximum_fusion.weights0), channel_id=1, source_target_pairs={{1,0},{2,1},{3,2},{4,3},{5,4},{6,5},{7,6},{0,7},{9,8},{10,9},{11,1... | collective-permute-start | bytes 393224 | tf_op jit(solution)/shard_map/ppermute | solution.py:499
  50.7 9.9 %collective-permute-start.4 = (bf16[256,256]{1,0:T(8,128)(2,1)S(1)}, bf16[256,256]{1,0:T(8,128)(2,1)S(1)}, u32[]{:S(2)}, u32[]{:S(2)}) collective-permute-start(bf16[256,256]{1,0:T(8,128)(2,1)S(1)} %pad_maximum_fusion.weights0), channel_id=1, source_target_pairs={{7,0},{0,1},{1,2},{2,3},{3,4},{4,5},{5,6},{6,7},{15,8},{8,9},{9,10... | collective-permute-start | bytes 393224 | tf_op jit(solution)/shard_map/ppermute | solution.py:499
  50.7 9.1 %collective-permute-start.1 = (bf16[128,256]{1,0:T(8,128)(2,1)S(1)}, bf16[128,256]{1,0:T(8,128)(2,1)S(1)}, u32[]{:S(2)}, u32[]{:S(2)}) collective-permute-start(bf16[128,256]{1,0:T(8,128)(2,1)S(1)} %get-tuple-element.79), channel_id=1, source_target_pairs={{2,0},{3,1},{4,2},{5,3},{6,4},{7,5},{0,6},{1,7},{10,8},{11,9},{12,... | collective-permute-start | bytes 196616 | tf_op jit(solution)/shard_map/ppermute | solution.py:499
  53.4 7.2 %collective-permute-start.2 = (bf16[128,256]{1,0:T(8,128)(2,1)S(1)}, bf16[128,256]{1,0:T(8,128)(2,1)S(1)}, u32[]{:S(2)}, u32[]{:S(2)}) collective-permute-start(bf16[128,256]{1,0:T(8,128)(2,1)S(1)} %get-tuple-element.79), channel_id=1, source_target_pairs={{6,0},{7,1},{0,2},{1,3},{2,4},{3,5},{4,6},{5,7},{14,8},{15,9},{8,1... | collective-permute-start | bytes 196616 | tf_op jit(solution)/shard_map/ppermute | solution.py:499
  58.2 43.5 %copy-start.7 = (s32[1024]{0:T(1024)S(1)}, s32[1024]{0:T(1024)}, u32[]{:S(2)}) copy-start(s32[1024]{0:T(1024)} %param.12) | copy-start | bytes 12292
  60.6 17.9 %all-to-all-start.3 = ((bf16[8,144,128]{2,1,0:T(8,128)(2,1)}), bf16[8,144,128]{2,1,0:T(8,128)(2,1)S(1)}, u32[]{:S(2)}, u32[]{:S(2)}) async-start(bf16[8,144,128]{2,1,0:T(8,128)(2,1)} %get-tuple-element.81), calls=%async_computation.3 | async-start | bytes 589824 | tf_op jit(solution)/shard_map/all_to_all | solution.py:491
  65.9 1.3 %collective-permute-start.5 = (f32[64,256]{1,0:T(8,128)S(1)}, f32[64,256]{1,0:T(8,128)S(1)}, u32[]{:S(2)}, u32[]{:S(2)}) collective-permute-start(f32[64,256]{1,0:T(8,128)S(1)} %get-tuple-element.87), channel_id=1, source_target_pairs={{0,8},{8,0},{16,24},{24,16},{32,40},{40,32},{48,56},{56,48},{64,72... | collective-permute-start | bytes 196616 | tf_op jit(solution)/shard_map/ppermute | solution.py:495
  67.3 4.8 %collective-permute-start.6 = (f32[64,256]{1,0:T(8,128)S(1)}, f32[64,256]{1,0:T(8,128)S(1)}, u32[]{:S(2)}, u32[]{:S(2)}) collective-permute-start(f32[64,256]{1,0:T(8,128)S(1)} %add.21), channel_id=1, source_target_pairs={{0,16},{8,24},{16,0},{24,8},{32,48},{40,56},{48,32},{56,40},{64,80... | collective-permute-start | bytes 196616 | tf_op jit(solution)/shard_map/ppermute | solution.py:495
  68.8 6.2 %collective-permute-start.7 = (f32[64,256]{1,0:T(8,128)S(1)}, f32[64,256]{1,0:T(8,128)S(1)}, u32[]{:S(2)}, u32[]{:S(2)}) collective-permute-start(f32[64,256]{1,0:T(8,128)S(1)} %add.21), channel_id=1, source_target_pairs={{0,32},{8,40},{16,48},{24,56},{32,0},{40,8},{48,16},{56,24},{64,96... | collective-permute-start | bytes 196616 | tf_op jit(solution)/shard_map/ppermute | solution.py:495
  71.5 5.5 %collective-permute-start.8 = (f32[64,256]{1,0:T(8,128)S(1)}, f32[64,256]{1,0:T(8,128)S(1)}, u32[]{:S(2)}, u32[]{:S(2)}) collective-permute-start(f32[64,256]{1,0:T(8,128)S(1)} %add.21), channel_id=1, source_target_pairs={{0,48},{8,56},{16,32},{24,40},{32,16},{40,24},{48,0},{56,8},{64,11... | collective-permute-start | bytes 196616 | tf_op jit(solution)/shard_map/ppermute | solution.py:495
  78.5 1.3 %collective-permute-start.9 = (f32[64,256]{1,0:T(8,128)S(1)}, f32[64,256]{1,0:T(8,128)S(1)}, u32[]{:S(2)}, u32[]{:S(2)}) collective-permute-start(f32[64,256]{1,0:T(8,128)S(1)} %add_add_fusion.1), channel_id=1, source_target_pairs={{0,8},{8,0},{16,24},{24,16},{32,40},{40,32},{48,56},{56,48},{64,72... | collective-permute-start | bytes 196616 | tf_op jit(solution)/shard_map/ppermute | solution.py:495
  79.8 12.1 %collective-permute-start.10 = (f32[128,256]{1,0:T(8,128)S(1)}, f32[128,256]{1,0:T(8,128)S(1)}, u32[]{:S(2)}, u32[]{:S(2)}) collective-permute-start(f32[128,256]{1,0:T(8,128)S(1)} %constant_dynamic-update-slice_fusion), channel_id=1, source_target_pairs={{0,64},{8,72},{16,80},{24,88},{32,96},{40,104},{48,112},{56,120},{... | collective-permute-start | bytes 393224 | tf_op jit(solution)/shard_map/ppermute | solution.py:495
  81.0 12.6 %collective-permute-start.11 = (f32[128,256]{1,0:T(8,128)S(1)}, f32[128,256]{1,0:T(8,128)S(1)}, u32[]{:S(2)}, u32[]{:S(2)}) collective-permute-start(f32[128,256]{1,0:T(8,128)S(1)} %constant_dynamic-update-slice_fusion), channel_id=1, source_target_pairs={{0,128},{8,136},{16,144},{24,152},{32,160},{40,168},{48,176},{56,1... | collective-permute-start | bytes 393224 | tf_op jit(solution)/shard_map/ppermute | solution.py:495
  83.7 9.9 %collective-permute-start.12 = (f32[128,256]{1,0:T(8,128)S(1)}, f32[128,256]{1,0:T(8,128)S(1)}, u32[]{:S(2)}, u32[]{:S(2)}) collective-permute-start(f32[128,256]{1,0:T(8,128)S(1)} %constant_dynamic-update-slice_fusion), channel_id=1, source_target_pairs={{0,192},{8,200},{16,208},{24,216},{32,224},{40,232},{48,240},{56,2... | collective-permute-start | bytes 393224 | tf_op jit(solution)/shard_map/ppermute | solution.py:495
  85.9 15.8 %all-to-all-start.4 = ((bf16[8,96,128]{2,1,0:T(8,128)(2,1)}), bf16[8,96,128]{2,1,0:T(8,128)(2,1)S(1)}, u32[]{:S(2)}, u32[]{:S(2)}) async-start(bf16[8,96,128]{2,1,0:T(8,128)(2,1)} %get-tuple-element.93), calls=%async_computation.4 | async-start | bytes 393216 | tf_op jit(solution)/shard_map/all_to_all | solution.py:491
  91.7 1.9 %collective-permute-start.13 = (f32[32,128]{1,0:T(8,128)S(1)}, f32[32,128]{1,0:T(8,128)S(1)}, u32[]{:S(2)}, u32[]{:S(2)}) collective-permute-start(f32[32,128]{1,0:T(8,128)S(1)} %get-tuple-element.95.virt0), channel_id=1, source_target_pairs={{0,8},{8,0},{16,24},{24,16},{32,40},{40,32},{48,56},{56,48},{64,72... | collective-permute-start | bytes 49160 | tf_op jit(solution)/shard_map/ppermute | solution.py:495
  91.8 3.8 %collective-permute-start.14 = (f32[32,128]{1,0:T(8,128)S(1)}, f32[32,128]{1,0:T(8,128)S(1)}, u32[]{:S(2)}, u32[]{:S(2)}) collective-permute-start(f32[32,128]{1,0:T(8,128)S(1)} %get-tuple-element.95.virt0), channel_id=1, source_target_pairs={{0,16},{8,24},{16,0},{24,8},{32,48},{40,56},{48,32},{56,40},{64,80... | collective-permute-start | bytes 49160 | tf_op jit(solution)/shard_map/ppermute | solution.py:495
  91.9 3.7 %collective-permute-start.15 = (f32[32,128]{1,0:T(8,128)S(1)}, f32[32,128]{1,0:T(8,128)S(1)}, u32[]{:S(2)}, u32[]{:S(2)}) collective-permute-start(f32[32,128]{1,0:T(8,128)S(1)} %get-tuple-element.95.virt0), channel_id=1, source_target_pairs={{0,24},{8,16},{16,8},{24,0},{32,56},{40,48},{48,40},{56,32},{64,88... | collective-permute-start | bytes 49160 | tf_op jit(solution)/shard_map/ppermute | solution.py:495

commit v6 on v3

--- a/solution.py
+++ b/solution.py
@@ -448,7 +448,7 @@
 
 
 def finish_kernel(
-    core, columns, near, far, virt0, virt1, virt2, virt3, member,
+    core, columns, near, far, virt0, virt1, member,
     mixed, grad_feats, grad_qkv, grad_out, grad_virtual, held,
 ):
     held[core[0]] = near[...]
@@ -456,7 +456,7 @@
     grad_qkv[0:64, :] = held[0]
     grad_qkv[64:96, :] = held[1, 0:32, :]
     grad_out[...] = held[1, 32:64, :]
-    virt = (virt0[...] + virt1[...]) + (virt2[...] + virt3[...])
+    virt = virt0[...] + virt1[...]
     grad_virtual[...] = virt[:, :VIRT]
     lookup = POOL_SCALE * dot3(virt, hot(member[...] == iota((128, ROWS), 0)))
     for h in range(HEADS):
@@ -606,10 +606,11 @@
     columns, keep = lax.optimization_barrier([columns, keep])
     columns = exchange(columns, "head")
     keep = (keep + swap(keep, "dom", 8)) + (swap(keep, "dom", 16) + swap(keep, "dom", 24))
-    virts = [virt] + [swap(virt, "dom", k) for k in (1, 2, 3)]
+    virt = virt + swap(virt, "dom", 1)
+    virts = [virt, swap(virt, "dom", 2)]
     mixed, grad_feats, grad_qkv, grad_out, grad_virtual = call(
         finish_kernel,
-        [SMEM] + [VMEM] * 8,
+        [SMEM] + [VMEM] * 6,
         (
             array((32, ROWS), bf16),
             array((32, ROWS), bf16),

time: 102 us -> 102 us (level)
  starting transfers between devices: 56.7 us -> 55.2 us
  waiting for transfers between devices: 17.9 us -> 19.3 us
    ppermute x12 -> x11, waiting for transfers between devices: 7.88 us -> 10.2 us  [swap(): lax.ppermute(x, axis, [(i, i ^ k) for i in range(lax.axis_size(axis))])]
    ppermute x12 -> x11, starting transfers between devices: 19.5 us -> 18 us  [swap(): lax.ppermute(x, axis, [(i, i ^ k) for i in range(lax.axis_size(axis))])]
  transfers between devices with their start and end apart: 21 -> 20, of which waited for: 9 -> 10; matrix products, arithmetic and copies ran while one was open for 0% -> 0% of each run, Pallas kernels for 12% -> 12%
where the time goes in v6:
time: 102 us; the launch traced here: 101 us
  starting transfers between devices  55.2 us (54%)
  Pallas kernels  21.4 us (21%)
  waiting for transfers between devices  19.3 us (19%)
  local copies, waits for them, and re-layouts  4.36 us (4%)
    all_to_all x5, starting transfers between devices, exchange(): return lax.all_to_all(x, axis, split_axis=0, concat_axis=0, tiled=True)  31.1 us
    ppermute x11, starting transfers between devices, swap(): lax.ppermute(x, axis, [(i, i ^ k) for i in range(lax.axis_size(axis))])  18 us
    ppermute x11, waiting for transfers between devices, swap(): lax.ppermute(x, axis, [(i, i ^ k) for i in range(lax.axis_size(axis))])  10.2 us
    all_to_all x5, waiting for transfers between devices, exchange(): return lax.all_to_all(x, axis, split_axis=0, concat_axis=0, tiled=True)  8.55 us
    ppermute x4, starting transfers between devices, shift(): return lax.ppermute(x, 'head', [((h + k) % HEADS, h) for h in range(HEADS)])  6.04 us
    pallas_call x1, Pallas kernels, shards(): pl.pallas_call(local_kernel, grid=(ROWS // TI,), out_shape=array((8, ROWS...  4.77 us
    pallas_call x1, Pallas kernels, shards(): call(attend_kernel, [VMEM] * 6 + [HBM] * 2, (array((64, ROWS), f32), arra...  4.6 us
    unnamed x16, local copies, waits for them, and re-layouts  4.36 us
  transfers between devices with their start and end apart: 20, of which 10 were waited for; matrix products, arithmetic and copies ran while one was open for 0% of the time, Pallas kernels for 12%

profile of v6, /device:TPU:2, one launch (start us, length us, event | category | flops | bytes accessed | tf_op | source)
XLA Modules:
  0.0 101.2 jit_solution(13138068581721902325)
XLA Ops:
  0.6 2.2 %shard_map.119 = f32[32,8,128]{2,1,0:T(8,128)} custom-call(bf16[1024,256]{1,0:T(8,128)(2,1)} %feats_at.3, s32[1,1024]{1,0:T(1,128)} %bitcast.12, s32[2,1024]{1,0:T(2,128)} %bitcast.14), custom_call_target="tpu_custom_call" | custom-call | tf_op jit(solution)/shard_map/pallas_call | solution.py:506
  2.8 7.6 %all-to-all-start = ((f32[32,8,128]{2,1,0:T(8,128)}), f32[32,8,128]{2,1,0:T(8,128)S(1)}, u32[]{:S(2)}, u32[]{:S(2)}) async-start(f32[32,8,128]{2,1,0:T(8,128)} %shard_map.119), calls=%async_computation | async-start | bytes 262144 | tf_op jit(solution)/shard_map/all_to_all | solution.py:491
  10.5 1.0 %copy-done = bf16[1024,256]{1,0:T(8,128)(2,1)S(1)} copy-done((bf16[1024,256]{1,0:T(8,128)(2,1)S(1)}, bf16[1024,256]{1,0:T(8,128)(2,1)}, u32[]{:S(2)}) %copy-start) | copy-done | bytes 524312
  11.5 1.0 %copy-done.2 = bf16[1024,256]{1,0:T(8,128)(2,1)S(1)} copy-done((bf16[1024,256]{1,0:T(8,128)(2,1)S(1)}, bf16[1024,256]{1,0:T(8,128)(2,1)}, u32[]{:S(2)}) %copy-start.2) | copy-done | bytes 524312
  15.5 1.6 %all-to-all-done.arrived = f32[32,8,128]{2,1,0:T(8,128)S(1)} async-done(((f32[32,8,128]{2,1,0:T(8,128)}), f32[32,8,128]{2,1,0:T(8,128)S(1)}, u32[]{:S(2)}, u32[]{:S(2)}) %all-to-all-start) | async-done | bytes 131104 | tf_op jit(solution)/shard_map/all_to_all | solution.py:491
  17.1 2.0 %shard_map.121 = (bf16[32,80,128]{2,1,0:T(8,128)(2,1)}, f32[8,1024]{1,0:T(8,128)S(1)}, bf16[128,256]{1,0:T(8,128)(2,1)S(1)}) custom-call(s32[1]{0:T(128)} %bitcast.slab, f32[32,8,128]{2,1,0:T(8,128)S(1)} %all-to-all-done.arrived, bf16[1024,128]{1,0:T(8,128)(2,1)S(1)} %get-tuple-element.57.table, bf16[64,1024]{1,0:T(8,128)(2,1)S(1)} %get-tuple-element.58.table_t, ...), custom_call_target="tpu_custom_call" | custom-call | tf_op jit(solution)/shard_map/pallas_call | solution.py:533
  19.1 5.9 %all-to-all-start.1 = ((bf16[32,80,128]{2,1,0:T(8,128)(2,1)}), bf16[32,80,128]{2,1,0:T(8,128)(2,1)S(1)}, u32[]{:S(2)}, u32[]{:S(2)}) async-start(bf16[32,80,128]{2,1,0:T(8,128)(2,1)} %get-tuple-element.66), calls=%async_computation.1 | async-start | bytes 1310720 | tf_op jit(solution)/shard_map/all_to_all | solution.py:491
  25.0 7.3 %collective-permute-start = (bf16[128,256]{1,0:T(8,128)(2,1)S(1)}, bf16[128,256]{1,0:T(8,128)(2,1)S(1)}, u32[]{:S(2)}, u32[]{:S(2)}) collective-permute-start(bf16[128,256]{1,0:T(8,128)(2,1)S(1)} %get-tuple-element.81), channel_id=1, source_target_pairs={{0,4},{1,5},{2,6},{3,7},{4,0},{5,1},{6,2},{7,3},{8,12},{9,13},{10,... | collective-permute-start | bytes 196616 | tf_op jit(solution)/shard_map/ppermute | solution.py:495
  32.3 4.8 %shard_map.122.stats = f32[8,1024]{1,0:T(8,128)S(1)} custom-call(bf16[32,1024]{1,0:T(8,128)(2,1)S(1)} %get-tuple-element.64.query_t, bf16[32,1024]{1,0:T(8,128)(2,1)S(1)} %get-tuple-element.65.grad_t, s32[1024,1024]{1,0:T(8,128)} %mask_at.1, bf16[64,1024]{1,0:T(8,128)(2,1)S(1)} %get-tuple-element.58.table_t), custom_call_target="tpu_custom_call" | custom-call | tf_op jit(solution)/shard_map/pallas_call | solution.py:542
  37.1 3.0 %shard_map.123 = (bf16[32,80,128]{2,1,0:T(8,128)(2,1)}, f32[8,1024]{1,0:T(8,128)S(1)}, f32[32,1024]{1,0:T(8,128)S(1)}, f32[32,1024]{1,0:T(8,128)S(1)}) custom-call(bf16[32,1024]{1,0:T(8,128)(2,1)S(1)} %get-tuple-element.64.query_t, bf16[32,1024]{1,0:T(8,128)(2,1)S(1)} %get-tuple-element.65.grad_t, f32[8,1024]{1,0:T(8,128)S(1)} %shard_map.122.stats, ...), custom_call_target="tpu_custom_call" | custom-call | tf_op jit(solution)/shard_map/pallas_call | solution.py:551
  40.1 7.5 %all-to-all-start.2 = ((bf16[32,80,128]{2,1,0:T(8,128)(2,1)}), bf16[32,80,128]{2,1,0:T(8,128)(2,1)S(1)}, u32[]{:S(2)}, u32[]{:S(2)}) async-start(bf16[32,80,128]{2,1,0:T(8,128)(2,1)} %get-tuple-element.73), calls=%async_computation.2 | async-start | bytes 1310720 | tf_op jit(solution)/shard_map/all_to_all | solution.py:491
  47.6 3.1 %collective-permute-start.3 = (bf16[256,256]{1,0:T(8,128)(2,1)S(1)}, bf16[256,256]{1,0:T(8,128)(2,1)S(1)}, u32[]{:S(2)}, u32[]{:S(2)}) collective-permute-start(bf16[256,256]{1,0:T(8,128)(2,1)S(1)} %pad_maximum_fusion.weights0), channel_id=1, source_target_pairs={{1,0},{2,1},{3,2},{4,3},{5,4},{6,5},{7,6},{0,7},{9,8},{10,9},{11,1... | collective-permute-start | bytes 393224 | tf_op jit(solution)/shard_map/ppermute | solution.py:499
  50.7 2.7 %collective-permute-start.1 = (bf16[128,256]{1,0:T(8,128)(2,1)S(1)}, bf16[128,256]{1,0:T(8,128)(2,1)S(1)}, u32[]{:S(2)}, u32[]{:S(2)}) collective-permute-start(bf16[128,256]{1,0:T(8,128)(2,1)S(1)} %get-tuple-element.81), channel_id=1, source_target_pairs={{2,0},{3,1},{4,2},{5,3},{6,4},{7,5},{0,6},{1,7},{10,8},{11,9},{12,... | collective-permute-start | bytes 196616 | tf_op jit(solution)/shard_map/ppermute | solution.py:499
  53.7 4.6 %shard_map.124 = (f32[64,1024]{1,0:T(8,128)S(1)}, bf16[64,1024]{1,0:T(8,128)(2,1)S(1)}, f32[32,256]{1,0:T(8,128)S(1)}) custom-call(f32[8,1024]{1,0:T(8,128)S(1)} %get-tuple-element.74.parts, f32[32,1024]{1,0:T(8,128)S(1)} %get-tuple-element.75.attended, f32[32,1024]{1,0:T(8,128)S(1)} %get-tuple-element.76.grad_query, ...), custom_call_target="tpu_custom_call" | custom-call | tf_op jit(solution)/shard_map/pallas_call | solution.py:562
  58.5 1.6 %shard_map.125 = (bf16[8,144,128]{2,1,0:T(8,128)(2,1)}, bf16[128,1024]{1,0:T(8,128)(2,1)S(1)}, f32[16,128]{1,0:T(8,128)S(1)}) custom-call(bf16[32,80,128]{2,1,0:T(8,128)(2,1)S(1)} %all-to-all-done.2.arrived, f32[8,1024]{1,0:T(8,128)S(1)} %get-tuple-element.70.places, f32[64,1024]{1,0:T(8,128)S(1)} %get-tuple-element.77.local, ...), custom_call_target="tpu_custom_call" | custom-call | tf_op jit(solution)/shard_map/pallas_call | solution.py:576
  60.7 5.0 %all-to-all-start.3 = ((bf16[8,144,128]{2,1,0:T(8,128)(2,1)}), bf16[8,144,128]{2,1,0:T(8,128)(2,1)S(1)}, u32[]{:S(2)}, u32[]{:S(2)}) async-start(bf16[8,144,128]{2,1,0:T(8,128)(2,1)} %get-tuple-element.83), calls=%async_computation.3 | async-start | bytes 589824 | tf_op jit(solution)/shard_map/all_to_all | solution.py:491
  66.6 0.9 collective-permute-done.5
  67.5 1.3 %collective-permute-start.6 = (f32[64,256]{1,0:T(8,128)S(1)}, f32[64,256]{1,0:T(8,128)S(1)}, u32[]{:S(2)}, u32[]{:S(2)}) collective-permute-start(f32[64,256]{1,0:T(8,128)S(1)} %add.24), channel_id=1, source_target_pairs={{0,16},{8,24},{16,0},{24,8},{32,48},{40,56},{48,32},{56,40},{64,80... | collective-permute-start | bytes 196616 | tf_op jit(solution)/shard_map/ppermute | solution.py:495
  68.8 2.7 %collective-permute-start.7 = (f32[64,256]{1,0:T(8,128)S(1)}, f32[64,256]{1,0:T(8,128)S(1)}, u32[]{:S(2)}, u32[]{:S(2)}) collective-permute-start(f32[64,256]{1,0:T(8,128)S(1)} %add.24), channel_id=1, source_target_pairs={{0,32},{8,40},{16,48},{24,56},{32,0},{40,8},{48,16},{56,24},{64,96... | collective-permute-start | bytes 196616 | tf_op jit(solution)/shard_map/ppermute | solution.py:495
  71.5 0.8 collective-permute-start.8
  72.3 2.7 %collective-permute-done.7 = f32[64,256]{1,0:T(8,128)S(1)} collective-permute-done((f32[64,256]{1,0:T(8,128)S(1)}, f32[64,256]{1,0:T(8,128)S(1)}, u32[]{:S(2)}, u32[]{:S(2)}) %collective-permute-start.7) | collective-permute-done | bytes 65568 | tf_op jit(solution)/shard_map/ppermute | solution.py:495
  75.1 1.9 %collective-permute-done.8 = f32[64,256]{1,0:T(8,128)S(1)} collective-permute-done((f32[64,256]{1,0:T(8,128)S(1)}, f32[64,256]{1,0:T(8,128)S(1)}, u32[]{:S(2)}, u32[]{:S(2)}) %collective-permute-start.8) | collective-permute-done | bytes 65568 | tf_op jit(solution)/shard_map/ppermute | solution.py:495
  77.0 2.2 %all-to-all-done.3.rows = bf16[8,144,128]{2,1,0:T(8,128)(2,1)S(1)} async-done(((bf16[8,144,128]{2,1,0:T(8,128)(2,1)}), bf16[8,144,128]{2,1,0:T(8,128)(2,1)S(1)}, u32[]{:S(2)}, u32[]{:S(2)}) %all-to-all-start.3) | async-done | bytes 294944 | tf_op jit(solution)/shard_map/all_to_all | solution.py:491
  79.3 1.5 %shard_map.127 = (bf16[8,96,128]{2,1,0:T(8,128)(2,1)}, f32[32,128]{1,0:T(8,128)S(1)}) custom-call(s32[1]{0:T(128)} %bitcast.1.head, s32[1]{0:T(128)S(6)} %and.10.group, bf16[8,144,128]{2,1,0:T(8,128)(2,1)S(1)} %all-to-all-done.3.rows, bf16[256,256]{1,0:T(8,128)(2,1)S(1)} %pad_maximum_fusion.weights0, bf16[128,256]{1,0:T(8,128)(2,1)S(1)} %collective-permute-done.1.weights2, ...), custom_call_target="tpu_custom_call" | custom-call | tf_op jit(solution)/shard_map/pallas_call | solution.py:595
  80.7 1.5 %collective-permute-start.10 = (f32[64,256]{1,0:T(8,128)S(1)}, f32[64,256]{1,0:T(8,128)S(1)}, u32[]{:S(2)}, u32[]{:S(2)}) collective-permute-start(f32[64,256]{1,0:T(8,128)S(1)} %add_add_fusion.1), channel_id=1, source_target_pairs={{0,128},{8,136},{16,144},{24,152},{32,160},{40,168},{48,176},{56,1... | collective-permute-start | bytes 196616 | tf_op jit(solution)/shard_map/ppermute | solution.py:495
  82.2 1.9 %collective-permute-start.11 = (f32[64,256]{1,0:T(8,128)S(1)}, f32[64,256]{1,0:T(8,128)S(1)}, u32[]{:S(2)}, u32[]{:S(2)}) collective-permute-start(f32[64,256]{1,0:T(8,128)S(1)} %add_add_fusion.1), channel_id=1, source_target_pairs={{0,192},{8,200},{16,208},{24,216},{32,224},{40,232},{48,240},{56,2... | collective-permute-start | bytes 196616 | tf_op jit(solution)/shard_map/ppermute | solution.py:495
  84.1 1.4 %collective-permute-start.9 = (f32[64,256]{1,0:T(8,128)S(1)}, f32[64,256]{1,0:T(8,128)S(1)}, u32[]{:S(2)}, u32[]{:S(2)}) collective-permute-start(f32[64,256]{1,0:T(8,128)S(1)} %add_add_fusion.1), channel_id=1, source_target_pairs={{0,64},{8,72},{16,80},{24,88},{32,96},{40,104},{48,112},{56,120},{... | collective-permute-start | bytes 196616 | tf_op jit(solution)/shard_map/ppermute | solution.py:495
  85.5 5.0 %all-to-all-start.4 = ((bf16[8,96,128]{2,1,0:T(8,128)(2,1)}), bf16[8,96,128]{2,1,0:T(8,128)(2,1)S(1)}, u32[]{:S(2)}, u32[]{:S(2)}) async-start(bf16[8,96,128]{2,1,0:T(8,128)(2,1)} %get-tuple-element.97), calls=%async_computation.4 | async-start | bytes 393216 | tf_op jit(solution)/shard_map/all_to_all | solution.py:491
  91.2 0.8 collective-permute-done.13
  92.0 3.7 %collective-permute-done.14.virt1 = f32[32,128]{1,0:T(8,128)S(1)} collective-permute-done((f32[32,128]{1,0:T(8,128)S(1)}, f32[32,128]{1,0:T(8,128)S(1)}, u32[]{:S(2)}, u32[]{:S(2)}) %collective-permute-start.14) | collective-permute-done | bytes 16416 | tf_op jit(solution)/shard_map/ppermute | solution.py:495
  95.8 4.5 %all-to-all-done.4.columns = bf16[8,96,128]{2,1,0:T(8,128)(2,1)S(1)} async-done(((bf16[8,96,128]{2,1,0:T(8,128)(2,1)}), bf16[8,96,128]{2,1,0:T(8,128)(2,1)S(1)}, u32[]{:S(2)}, u32[]{:S(2)}) %all-to-all-start.4) | async-done | bytes 196640 | tf_op jit(solution)/shard_map/all_to_all | solution.py:491
  100.3 0.9 shard_map.128
  (39 shorter events, 5.6 us)
Async XLA Ops:
  2.8 14.3 %all-to-all-start = ((f32[32,8,128]{2,1,0:T(8,128)}), f32[32,8,128]{2,1,0:T(8,128)S(1)}, u32[]{:S(2)}, u32[]{:S(2)}) async-start(f32[32,8,128]{2,1,0:T(8,128)} %shard_map.119), calls=%async_computation | async-start | bytes 262144 | tf_op jit(solution)/shard_map/all_to_all | solution.py:491
  10.5 1.0 %copy-start = (bf16[1024,256]{1,0:T(8,128)(2,1)S(1)}, bf16[1024,256]{1,0:T(8,128)(2,1)}, u32[]{:S(2)}) copy-start(bf16[1024,256]{1,0:T(8,128)(2,1)} %feats_at.3) | copy-start | bytes 1572868
  11.5 1.0 %copy-start.2 = (bf16[1024,256]{1,0:T(8,128)(2,1)S(1)}, bf16[1024,256]{1,0:T(8,128)(2,1)}, u32[]{:S(2)}) copy-start(bf16[1024,256]{1,0:T(8,128)(2,1)} %cotangent_at.3) | copy-start | bytes 1572868
  12.6 0.8 copy-start.4
  13.4 0.8 copy-start.5
  14.1 0.7 copy-start.6
  19.1 34.6 %copy-start.3 = (bf16[1024,256]{1,0:T(8,128)(2,1)S(1)}, bf16[1024,256]{1,0:T(8,128)(2,1)}, u32[]{:S(2)}) copy-start(bf16[1024,256]{1,0:T(8,128)(2,1)} %cotangent_at.3) | copy-start | bytes 1572868
  19.1 18.0 %all-to-all-start.1 = ((bf16[32,80,128]{2,1,0:T(8,128)(2,1)}), bf16[32,80,128]{2,1,0:T(8,128)(2,1)S(1)}, u32[]{:S(2)}, u32[]{:S(2)}) async-start(bf16[32,80,128]{2,1,0:T(8,128)(2,1)} %get-tuple-element.66), calls=%async_computation.1 | async-start | bytes 1310720 | tf_op jit(solution)/shard_map/all_to_all | solution.py:491
  25.0 12.0 %collective-permute-start = (bf16[128,256]{1,0:T(8,128)(2,1)S(1)}, bf16[128,256]{1,0:T(8,128)(2,1)S(1)}, u32[]{:S(2)}, u32[]{:S(2)}) collective-permute-start(bf16[128,256]{1,0:T(8,128)(2,1)S(1)} %get-tuple-element.81), channel_id=1, source_target_pairs={{0,4},{1,5},{2,6},{3,7},{4,0},{5,1},{6,2},{7,3},{8,12},{9,13},{10,... | collective-permute-start | bytes 196616 | tf_op jit(solution)/shard_map/ppermute | solution.py:495
  40.1 25.6 %copy-start.1 = (bf16[1024,256]{1,0:T(8,128)(2,1)S(1)}, bf16[1024,256]{1,0:T(8,128)(2,1)}, u32[]{:S(2)}) copy-start(bf16[1024,256]{1,0:T(8,128)(2,1)} %feats_at.3) | copy-start | bytes 1572868
  40.1 18.4 %all-to-all-start.2 = ((bf16[32,80,128]{2,1,0:T(8,128)(2,1)}), bf16[32,80,128]{2,1,0:T(8,128)(2,1)S(1)}, u32[]{:S(2)}, u32[]{:S(2)}) async-start(bf16[32,80,128]{2,1,0:T(8,128)(2,1)} %get-tuple-element.73), calls=%async_computation.2 | async-start | bytes 1310720 | tf_op jit(solution)/shard_map/all_to_all | solution.py:491
  47.6 13.1 %collective-permute-start.3 = (bf16[256,256]{1,0:T(8,128)(2,1)S(1)}, bf16[256,256]{1,0:T(8,128)(2,1)S(1)}, u32[]{:S(2)}, u32[]{:S(2)}) collective-permute-start(bf16[256,256]{1,0:T(8,128)(2,1)S(1)} %pad_maximum_fusion.weights0), channel_id=1, source_target_pairs={{1,0},{2,1},{3,2},{4,3},{5,4},{6,5},{7,6},{0,7},{9,8},{10,9},{11,1... | collective-permute-start | bytes 393224 | tf_op jit(solution)/shard_map/ppermute | solution.py:499
  50.7 9.9 %collective-permute-start.4 = (bf16[256,256]{1,0:T(8,128)(2,1)S(1)}, bf16[256,256]{1,0:T(8,128)(2,1)S(1)}, u32[]{:S(2)}, u32[]{:S(2)}) collective-permute-start(bf16[256,256]{1,0:T(8,128)(2,1)S(1)} %pad_maximum_fusion.weights0), channel_id=1, source_target_pairs={{7,0},{0,1},{1,2},{2,3},{3,4},{4,5},{5,6},{6,7},{15,8},{8,9},{9,10... | collective-permute-start | bytes 393224 | tf_op jit(solution)/shard_map/ppermute | solution.py:499
  50.7 9.3 %collective-permute-start.1 = (bf16[128,256]{1,0:T(8,128)(2,1)S(1)}, bf16[128,256]{1,0:T(8,128)(2,1)S(1)}, u32[]{:S(2)}, u32[]{:S(2)}) collective-permute-start(bf16[128,256]{1,0:T(8,128)(2,1)S(1)} %get-tuple-element.81), channel_id=1, source_target_pairs={{2,0},{3,1},{4,2},{5,3},{6,4},{7,5},{0,6},{1,7},{10,8},{11,9},{12,... | collective-permute-start | bytes 196616 | tf_op jit(solution)/shard_map/ppermute | solution.py:499
  53.4 7.2 %collective-permute-start.2 = (bf16[128,256]{1,0:T(8,128)(2,1)S(1)}, bf16[128,256]{1,0:T(8,128)(2,1)S(1)}, u32[]{:S(2)}, u32[]{:S(2)}) collective-permute-start(bf16[128,256]{1,0:T(8,128)(2,1)S(1)} %get-tuple-element.81), channel_id=1, source_target_pairs={{6,0},{7,1},{0,2},{1,3},{2,4},{3,5},{4,6},{5,7},{14,8},{15,9},{8,1... | collective-permute-start | bytes 196616 | tf_op jit(solution)/shard_map/ppermute | solution.py:499
  58.3 42.0 %copy-start.7 = (s32[1024]{0:T(1024)S(1)}, s32[1024]{0:T(1024)}, u32[]{:S(2)}) copy-start(s32[1024]{0:T(1024)} %param.12) | copy-start | bytes 12292
  60.7 18.6 %all-to-all-start.3 = ((bf16[8,144,128]{2,1,0:T(8,128)(2,1)}), bf16[8,144,128]{2,1,0:T(8,128)(2,1)S(1)}, u32[]{:S(2)}, u32[]{:S(2)}) async-start(bf16[8,144,128]{2,1,0:T(8,128)(2,1)} %get-tuple-element.83), calls=%async_computation.3 | async-start | bytes 589824 | tf_op jit(solution)/shard_map/all_to_all | solution.py:491
  66.0 1.5 %collective-permute-start.5 = (f32[64,256]{1,0:T(8,128)S(1)}, f32[64,256]{1,0:T(8,128)S(1)}, u32[]{:S(2)}, u32[]{:S(2)}) collective-permute-start(f32[64,256]{1,0:T(8,128)S(1)} %get-tuple-element.89), channel_id=1, source_target_pairs={{0,8},{8,0},{16,24},{24,16},{32,40},{40,32},{48,56},{56,48},{64,72... | collective-permute-start | bytes 196616 | tf_op jit(solution)/shard_map/ppermute | solution.py:495
  67.5 4.8 %collective-permute-start.6 = (f32[64,256]{1,0:T(8,128)S(1)}, f32[64,256]{1,0:T(8,128)S(1)}, u32[]{:S(2)}, u32[]{:S(2)}) collective-permute-start(f32[64,256]{1,0:T(8,128)S(1)} %add.24), channel_id=1, source_target_pairs={{0,16},{8,24},{16,0},{24,8},{32,48},{40,56},{48,32},{56,40},{64,80... | collective-permute-start | bytes 196616 | tf_op jit(solution)/shard_map/ppermute | solution.py:495
  68.8 6.2 %collective-permute-start.7 = (f32[64,256]{1,0:T(8,128)S(1)}, f32[64,256]{1,0:T(8,128)S(1)}, u32[]{:S(2)}, u32[]{:S(2)}) collective-permute-start(f32[64,256]{1,0:T(8,128)S(1)} %add.24), channel_id=1, source_target_pairs={{0,32},{8,40},{16,48},{24,56},{32,0},{40,8},{48,16},{56,24},{64,96... | collective-permute-start | bytes 196616 | tf_op jit(solution)/shard_map/ppermute | solution.py:495
  71.5 5.5 %collective-permute-start.8 = (f32[64,256]{1,0:T(8,128)S(1)}, f32[64,256]{1,0:T(8,128)S(1)}, u32[]{:S(2)}, u32[]{:S(2)}) collective-permute-start(f32[64,256]{1,0:T(8,128)S(1)} %add.24), channel_id=1, source_target_pairs={{0,48},{8,56},{16,32},{24,40},{32,16},{40,24},{48,0},{56,8},{64,11... | collective-permute-start | bytes 196616 | tf_op jit(solution)/shard_map/ppermute | solution.py:495
  80.7 9.8 %collective-permute-start.10 = (f32[64,256]{1,0:T(8,128)S(1)}, f32[64,256]{1,0:T(8,128)S(1)}, u32[]{:S(2)}, u32[]{:S(2)}) collective-permute-start(f32[64,256]{1,0:T(8,128)S(1)} %add_add_fusion.1), channel_id=1, source_target_pairs={{0,128},{8,136},{16,144},{24,152},{32,160},{40,168},{48,176},{56,1... | collective-permute-start | bytes 196616 | tf_op jit(solution)/shard_map/ppermute | solution.py:495
  82.2 8.3 %collective-permute-start.11 = (f32[64,256]{1,0:T(8,128)S(1)}, f32[64,256]{1,0:T(8,128)S(1)}, u32[]{:S(2)}, u32[]{:S(2)}) collective-permute-start(f32[64,256]{1,0:T(8,128)S(1)} %add_add_fusion.1), channel_id=1, source_target_pairs={{0,192},{8,200},{16,208},{24,216},{32,224},{40,232},{48,240},{56,2... | collective-permute-start | bytes 196616 | tf_op jit(solution)/shard_map/ppermute | solution.py:495
  84.1 6.4 %collective-permute-start.9 = (f32[64,256]{1,0:T(8,128)S(1)}, f32[64,256]{1,0:T(8,128)S(1)}, u32[]{:S(2)}, u32[]{:S(2)}) collective-permute-start(f32[64,256]{1,0:T(8,128)S(1)} %add_add_fusion.1), channel_id=1, source_target_pairs={{0,64},{8,72},{16,80},{24,88},{32,96},{40,104},{48,112},{56,120},{... | collective-permute-start | bytes 196616 | tf_op jit(solution)/shard_map/ppermute | solution.py:495
  85.5 14.8 %all-to-all-start.4 = ((bf16[8,96,128]{2,1,0:T(8,128)(2,1)}), bf16[8,96,128]{2,1,0:T(8,128)(2,1)S(1)}, u32[]{:S(2)}, u32[]{:S(2)}) async-start(bf16[8,96,128]{2,1,0:T(8,128)(2,1)} %get-tuple-element.97), calls=%async_computation.4 | async-start | bytes 393216 | tf_op jit(solution)/shard_map/all_to_all | solution.py:491
  90.6 5.2 %collective-permute-start.12 = (f32[64,256]{1,0:T(8,128)S(1)}, f32[64,256]{1,0:T(8,128)S(1)}, u32[]{:S(2)}, u32[]{:S(2)}) collective-permute-start(f32[64,256]{1,0:T(8,128)S(1)} %add_add_fusion.near), channel_id=1, source_target_pairs={{0,8},{8,0},{16,24},{24,16},{32,40},{40,32},{48,56},{56,48},{64,72... | collective-permute-start | bytes 196616 | tf_op jit(solution)/shard_map/ppermute | solution.py:495
  90.7 1.3 %collective-permute-start.13 = (f32[32,128]{1,0:T(8,128)S(1)}, f32[32,128]{1,0:T(8,128)S(1)}, u32[]{:S(2)}, u32[]{:S(2)}) collective-permute-start(f32[32,128]{1,0:T(8,128)S(1)} %get-tuple-element.99), channel_id=1, source_target_pairs={{0,8},{8,0},{16,24},{24,16},{32,40},{40,32},{48,56},{56,48},{64,72... | collective-permute-start | bytes 49160 | tf_op jit(solution)/shard_map/ppermute | solution.py:495
  92.0 3.7 %collective-permute-start.14 = (f32[32,128]{1,0:T(8,128)S(1)}, f32[32,128]{1,0:T(8,128)S(1)}, u32[]{:S(2)}, u32[]{:S(2)}) collective-permute-start(f32[32,128]{1,0:T(8,128)S(1)} %add.31.virt0), channel_id=1, source_target_pairs={{0,16},{8,24},{16,0},{24,8},{32,48},{40,56},{48,32},{56,40},{64,80... | collective-permute-start | bytes 49160 | tf_op jit(solution)/shard_map/ppermute | solution.py:495
